TPU v7x, 32 devices: a whole 2x2x4 slice. The times are simulated.
32 devices in a mesh: dp: 32 (over z, y, x, core).
Axes of the slice: x: 2, y: 2, z: 4, core: 2. Of those that a mesh axis runs over, the one named last changes fastest.
Arguments:
- tokens: bfloat16 [4096, 1024], P('dp'), may hold values from -6 to 6
- segment_ids: int32 [4096], P('dp'), may hold values from 0 to 2, as said below
- pad_mask: int32 [4096], P('dp'), may hold values from 0 to 1, as said below
- ln1_gain: bfloat16 [1024], P('dp'), may hold values from 0.5 to 1.5
- ln1_bias: bfloat16 [1024], P('dp'), may hold values from -1.796875 to 1.796875
- qkv_weight: bfloat16 [1024, 3072], P('dp'), may hold values from -0.1875 to 0.1875
- qkv_bias: bfloat16 [2048], P('dp'), may hold values from -1.796875 to 1.796875
- out_weight: bfloat16 [1024, 1024], P('dp'), may hold values from -1 to 1
- out_bias: bfloat16 [1024], P('dp'), may hold values from -1.796875 to 1.796875
- ln2_gain: bfloat16 [1024], P('dp'), may hold values from 0.5 to 1.5
- ln2_bias: bfloat16 [1024], P('dp'), may hold values from -1.796875 to 1.796875
- up_weight: bfloat16 [1024, 4096], P('dp'), may hold values from -0.1875 to 0.1875
- up_bias: bfloat16 [4096], P('dp'), may hold values from -1.796875 to 1.796875
- down_weight: bfloat16 [4096, 1024], P('dp'), may hold values from -0.09375 to 0.09375
- down_bias: bfloat16 [1024], P('dp'), may hold values from -1.796875 to 1.796875
- cotangent: bfloat16 [4096, 1024], P('dp'), may hold values from -6 to 6
Outputs:
- block_out: bfloat16 [4096, 1024], P('dp')
- grad_tokens: float32 [4096, 1024], P('dp')
- grad_ln1_gain: float32 [1024], P('dp')
- grad_ln1_bias: float32 [1024], P('dp')
- grad_qkv_weight: float32 [1024, 3072], P('dp')
- grad_qkv_bias: float32 [2048], P('dp')
- grad_out_weight: float32 [1024, 1024], P('dp')
- grad_out_bias: float32 [1024], P('dp')
- grad_ln2_gain: float32 [1024], P('dp')
- grad_ln2_bias: float32 [1024], P('dp')
- grad_up_weight: float32 [1024, 4096], P('dp')
- grad_up_bias: float32 [4096], P('dp')
- grad_down_weight: float32 [4096, 1024], P('dp')
- grad_down_bias: float32 [1024], P('dp')
Inputs may be any that keep to these rules, and one draw needn't show every extreme that they name: `segment_ids`: along one device's 128 slots the numbers never fall; padding slots carry the number of the device's last sequence. `pad_mask`: on each device the live slots come first, 64 or more of them; some device has all 128 slots live.
All inputs are finite; a program needn't handle non-finite values.
Results may differ from a plain program's by a relative error of at most 0.0092.
Values may be sent and summed in bfloat16 or wider, within the bound.
No kernel may reach another device: no remote copies, remote signals or barrier semaphores. Data moves between devices by JAX's collectives and lax.ppermute only.
A program may use at most 256 MiB of HBM per device.

v0:
```python
import functools
import math

import jax
import jax.numpy as jnp
from jax import lax
from jax.experimental import pallas as pl
from jax.experimental.pallas import tpu as pltpu
from jax.sharding import PartitionSpec as P

HEAD_DIM = 64
EPS = 1e-05
NEG = -1e30
GROUP = 8
DIRECT_PLANES = 8
LOW = jnp.bfloat16
WIDE = jnp.float32


def norm_rows(inputs):
    average = jnp.mean(inputs, axis=-1, keepdims=True)
    centered = inputs - average
    variance = jnp.mean(centered * centered, axis=-1, keepdims=True)
    inverse = lax.rsqrt(variance + EPS)
    return (centered * inverse, inverse)


def norm_back(grad_in, normed, inverse, gain):
    scaled = grad_in * gain
    return inverse * (
        scaled
        - jnp.mean(scaled, axis=1, keepdims=True)
        - normed * jnp.mean(scaled * normed, axis=1, keepdims=True)
    )


def gelu_tanh(inputs):
    return (
        0.5
        * inputs
        * (1.0 + jnp.tanh(0.7978845608028654 * (inputs + 0.044715 * inputs * inputs * inputs)))
    )


def dot(first, second, dims):
    return lax.dot_general(first, second, (dims, ((), ())), preferred_element_type=jnp.float32)


def plain_dot(first, second):
    return dot(first, second, ((1,), (0,)))


def left_dot(first, second):
    return dot(first, second, ((0,), (0,)))


def right_dot(first, second):
    return dot(first, second, ((1,), (1,)))


def head_masks():
    lane = lax.broadcasted_iota(jnp.int32, (1, 2 * HEAD_DIM), 1)
    return [((lane // HEAD_DIM) == h).astype(LOW) for h in range(2)]


def softmax_rows(query, key, allowed):
    scores = right_dot(query, key) * (1.0 / math.sqrt(HEAD_DIM))
    scores = jnp.where(allowed, scores, NEG)
    top = jnp.max(scores, axis=1, keepdims=True)
    raw = jnp.exp(scores - top)
    return raw / jnp.sum(raw, axis=1, keepdims=True)


def attention_kernel(packed_ref, allowed_ref, out_ref):
    masks = head_masks()
    rows = allowed_ref.shape[1]
    width = 2 * HEAD_DIM
    for block in range(allowed_ref.shape[0]):
        part = pl.ds(block * rows, rows)
        query = packed_ref[part, :width]
        key = packed_ref[part, width : 2 * width]
        value = packed_ref[part, 2 * width :]
        allowed = allowed_ref[block] > 0
        total = None
        for mask in masks:
            weights = softmax_rows(query * mask, key, allowed).astype(LOW)
            term = plain_dot(weights, value * mask)
            total = term if total is None else total + term
        out_ref[part, :] = total.astype(LOW)


def attention_back_kernel(packed_ref, grad_ref, allowed_ref, out_ref):
    masks = head_masks()
    rows = allowed_ref.shape[1]
    width = 2 * HEAD_DIM
    scale = 1.0 / math.sqrt(HEAD_DIM)
    for block in range(allowed_ref.shape[0]):
        part = pl.ds(block * rows, rows)
        query = packed_ref[part, :width]
        key = packed_ref[part, width : 2 * width]
        value = packed_ref[part, 2 * width :]
        grad = grad_ref[part, :]
        allowed = allowed_ref[block] > 0
        sums = [None, None, None]
        for mask in masks:
            query_head = query * mask
            grad_head = grad * mask
            weights = softmax_rows(query_head, key, allowed)
            grad_weights = right_dot(grad_head, value)
            grad_scores = weights * (
                grad_weights - jnp.sum(grad_weights * weights, axis=1, keepdims=True)
            )
            grad_scores = grad_scores.astype(LOW)
            terms = (
                plain_dot(grad_scores, key * mask),
                left_dot(grad_scores, query_head),
                left_dot(weights.astype(LOW), grad_head),
            )
            sums = [t if s is None else s + t for s, t in zip(sums, terms)]
        out_ref[part, :width] = (sums[0] * scale).astype(LOW)
        out_ref[part, width : 2 * width] = (sums[1] * scale).astype(LOW)
        out_ref[part, 2 * width :] = sums[2].astype(LOW)


def block_place(i, place_ref):
    return place_ref[0] ^ (((i & 3) << 1) | (i >> 2))


def attention(packed, allowed, place):
    blocks, rows, _ = allowed.shape
    width = 2 * HEAD_DIM
    return pl.pallas_call(
        lambda place_ref, *refs: attention_kernel(*refs),
        grid_spec=pltpu.PrefetchScalarGridSpec(
            num_scalar_prefetch=1,
            grid=(blocks,),
            in_specs=[
                pl.BlockSpec((rows, 3 * width), lambda i, p: (i, 0)),
                pl.BlockSpec((1, rows, rows), lambda i, p: (block_place(i, p), 0, 0)),
            ],
            out_specs=pl.BlockSpec((rows, width), lambda i, p: (block_place(i, p), 0)),
        ),
        out_shape=jax.ShapeDtypeStruct((blocks * rows, width), LOW),
        cost_estimate=pl.CostEstimate(
            flops=8 * blocks * rows * rows * width,
            bytes_accessed=2 * packed.size + 4 * allowed.size,
            transcendentals=2 * allowed.size,
        ),
    )(place[None], packed, allowed)


def attention_back(packed, grad, allowed, place):
    blocks, rows, _ = allowed.shape
    width = 2 * HEAD_DIM
    return pl.pallas_call(
        lambda place_ref, *refs: attention_back_kernel(*refs),
        grid_spec=pltpu.PrefetchScalarGridSpec(
            num_scalar_prefetch=1,
            grid=(blocks,),
            in_specs=[
                pl.BlockSpec((rows, 3 * width), lambda i, p: (i, 0)),
                pl.BlockSpec((rows, width), lambda i, p: (block_place(i, p), 0)),
                pl.BlockSpec((1, rows, rows), lambda i, p: (block_place(i, p), 0, 0)),
            ],
            out_specs=pl.BlockSpec((rows, 3 * width), lambda i, p: (i, 0)),
        ),
        out_shape=jax.ShapeDtypeStruct((blocks * rows, 3 * width), LOW),
        cost_estimate=pl.CostEstimate(
            flops=20 * blocks * rows * rows * width,
            bytes_accessed=4 * packed.size + 4 * allowed.size,
            transcendentals=2 * allowed.size,
        ),
    )(place[None], packed, grad, allowed)


class Links:
    def __init__(self, count):
        self.count = count
        self.planes = count // GROUP
        index = lax.axis_index("dp")
        self.place = index & (GROUP - 1)
        self.plane = index // GROUP

    def swap(self, array, flip):
        return lax.ppermute(array, "dp", [(i, i ^ flip) for i in range(self.count)])

    def shift(self, array, steps):
        hop = steps * GROUP
        return lax.ppermute(array, "dp", [(i, (i + hop) % self.count) for i in range(self.count)])

    def chip_gather(self, block):
        others = {flip: self.swap(block, flip) for flip in (6, 2, 4)}
        return jnp.concatenate([block, others[2], others[4], others[6]], axis=0)

    def core_gather(self, near):
        return jnp.concatenate([near, self.swap(near, 1)], axis=0)

    def core_sum(self, near, far):
        return (near.astype(WIDE) + self.swap(far, 1).astype(WIDE)).astype(LOW)

    def chip_sum(self, halves):
        total = halves[0].astype(WIDE)
        for k in (3, 1, 2):
            total = total + self.swap(halves[k], 2 * k).astype(WIDE)
        return total

    def group_lists(self):
        return [[p * GROUP + j for j in range(GROUP)] for p in range(self.planes)]

    def plane_exchange(self, parts):
        return lax.all_to_all(
            parts, "dp", 0, 0, axis_index_groups=self.plane_groups(), tiled=True
        )

    def exchange(self, parts):
        return lax.all_to_all(
            parts, "dp", 0, 0, axis_index_groups=self.group_lists(), tiled=True
        )

    def plane_groups(self):
        return [[p * GROUP + j for p in range(self.planes)] for j in range(GROUP)]

    def plane_gather(self, block):
        if self.planes > DIRECT_PLANES:
            return lax.all_gather(block, "dp", axis_index_groups=self.plane_groups())
        found = jnp.zeros((self.planes,) + block.shape, block.dtype)
        found = lax.dynamic_update_index_in_dim(found, block, self.plane, 0)
        for k in range(1, self.planes):
            source = (self.plane + self.planes - k) % self.planes
            found = lax.dynamic_update_index_in_dim(found, self.shift(block, k), source, 0)
        return found

    def plane_sum(self, chunks):
        if self.planes > DIRECT_PLANES:
            return lax.psum_scatter(
                chunks.astype(WIDE), "dp", axis_index_groups=self.plane_groups()
            )
        total = lax.dynamic_index_in_dim(chunks, self.plane, 0, False).astype(WIDE)
        for k in range(1, self.planes):
            target = (self.plane + k) % self.planes
            term = lax.dynamic_index_in_dim(chunks, target, 0, False)
            total = total + self.shift(term, k).astype(WIDE)
        return total


def after(array, *others):
    return lax.optimization_barrier((array,) + others)[0]


def local(
    tokens,
    segment_ids,
    pad_mask,
    ln1_gain,
    ln1_bias,
    qkv_weight,
    qkv_bias,
    out_weight,
    out_bias,
    ln2_gain,
    ln2_bias,
    up_weight,
    up_bias,
    down_weight,
    down_bias,
    cotangent,
):
    count = lax.axis_size("dp")
    links = Links(count)
    place, planes = links.place, links.planes
    rows, width = tokens.shape
    own_rows = qkv_weight.shape[0]
    hidden = up_weight.shape[1]
    shard = width // GROUP
    hidden_shard = hidden // GROUP
    own_hidden = hidden // count
    heads_width = 3 * shard

    code = (segment_ids * 2 + pad_mask).astype(LOW)
    fill = jnp.zeros((shard - 4 * own_rows,), LOW)
    wide_fill = jnp.zeros((shard - own_hidden,), LOW)
    empty = jnp.zeros((shard,), LOW)
    small = [
        jnp.concatenate([ln1_gain, ln1_bias, out_bias, ln2_gain, fill]),
        jnp.concatenate([ln2_bias, down_bias, qkv_bias, fill]),
        jnp.concatenate([up_bias, wide_fill]),
        code,
    ]
    small = jnp.stack(small + [empty] * 4)
    qkv_parts = qkv_weight.reshape(own_rows, 3, GROUP, shard).transpose(2, 1, 0, 3)
    qkv_parts = qkv_parts.reshape(GROUP, 3 * own_rows, shard)
    small_parts = jnp.broadcast_to(small[None], (GROUP,) + small.shape)
    sent = jnp.concatenate([qkv_parts, small_parts], axis=1)
    sent = jnp.broadcast_to(sent[None], (planes,) + sent.shape).reshape((count,) + sent.shape[1:])
    up_parts = up_weight.reshape(own_rows, planes, GROUP, own_hidden)
    up_parts = up_parts.transpose(2, 0, 1, 3).reshape(GROUP, own_rows, hidden_shard)
    up_plane = links.exchange(up_parts)
    sent = after(sent, up_plane)
    token_near = links.chip_gather(tokens)
    up_full = links.plane_gather(up_plane).reshape(width, hidden_shard)
    buffer = lax.all_to_all(sent, "dp", 0, 0, tiled=True)
    buffer, token_near = lax.optimization_barrier((buffer, token_near))
    out_full = lax.all_gather(out_weight, "dp", axis=0, tiled=True)
    down_full = lax.all_gather(
        down_weight, "dp", axis_index_groups=links.plane_groups(), tiled=True
    )
    qkv_full = jnp.concatenate(
        [
            buffer[:, i * own_rows : (i + 1) * own_rows].reshape(width, shard)
            for i in range(3)
        ],
        axis=1,
    )

    def small_vector(row, start, length):
        start = start * own_rows
        return buffer[:, 3 * own_rows + row, start : start + length].astype(WIDE)

    gain_one, bias_one, bias_out, gain_two, bias_two, bias_down = (
        small_vector(i // 4, i % 4, own_rows).reshape(width) for i in range(6)
    )
    qkv_bias_all = small_vector(1, 2, 2 * own_rows).reshape(2, width)
    bias_qv = lax.dynamic_slice_in_dim(qkv_bias_all, place * shard, shard, 1)
    bias_heads = jnp.concatenate([bias_qv[0], jnp.zeros((shard,), WIDE), bias_qv[1]])
    up_bias_all = small_vector(2, 0, own_hidden).reshape(planes, GROUP, own_hidden)
    bias_up = lax.dynamic_index_in_dim(up_bias_all, place, 1, False).reshape(hidden_shard)

    token_all = links.core_gather(token_near)
    codes = lax.dynamic_slice_in_dim(small_vector(3, 0, rows), links.plane * GROUP, GROUP, 0)
    codes = codes.astype(jnp.int32)
    segments, live = codes >> 1, codes & 1
    positions = jnp.arange(rows, dtype=jnp.int32)
    allowed = (
        (segments[:, :, None] == segments[:, None, :])
        & (positions[None, :] <= positions[:, None])[None]
        & (live[:, None, :] == 1)
    ).astype(WIDE)

    grad_out = cotangent.astype(WIDE) * pad_mask.astype(WIDE)[:, None]
    grad_feed_own = grad_out.astype(LOW)

    normed_all, _ = norm_rows(token_all.astype(WIDE))
    hidden_one = (normed_all * gain_one + bias_one).astype(LOW)
    packed = (plain_dot(hidden_one, qkv_full) + bias_heads).astype(LOW)
    grad_feed_near = links.chip_gather(after(grad_feed_own, packed))
    mixed_heads = attention(packed, allowed, place).reshape(GROUP, rows, shard)
    mixed = links.exchange(after(mixed_heads, grad_feed_near))
    grad_feed = links.core_gather(after(grad_feed_near, mixed_heads))
    mixed = mixed.transpose(1, 0, 2).reshape(rows, width)
    token_rows = tokens.astype(WIDE)
    middle = token_rows + (plain_dot(mixed, out_full) + bias_out)
    normed_two, inverse_two = norm_rows(middle)
    hidden_two_own = (normed_two * gain_two + bias_two).astype(LOW)
    hidden_two_near = links.chip_gather(hidden_two_own)
    hidden_two = links.core_gather(after(hidden_two_near, up_full, grad_feed))
    pre_act = plain_dot(hidden_two, up_full) + bias_up
    activated, gelu_pull = jax.vjp(gelu_tanh, pre_act)
    activated_low = activated.astype(LOW)

    (grad_pre,) = gelu_pull(right_dot(grad_feed, down_full))
    grad_pre_low = grad_pre.astype(LOW)
    half_rows = GROUP * rows // 2
    far = right_dot(grad_pre_low[half_rows:], up_full).astype(LOW)
    near = right_dot(grad_pre_low[:half_rows], up_full).astype(LOW)
    grad_hidden_half = links.core_sum(near, far).reshape(4, rows, width)
    grad_hidden_two = links.chip_sum(grad_hidden_half)
    activated_low, _ = lax.optimization_barrier((activated_low, grad_hidden_half))
    far = plain_dot(activated_low[half_rows:], down_full).astype(LOW)
    near = plain_dot(activated_low[:half_rows], down_full).astype(LOW)
    feed_half = links.core_sum(near, far).reshape(4, rows, width)
    grad_middle = grad_out + norm_back(grad_hidden_two, normed_two, inverse_two, gain_two)
    grad_branch = grad_middle.astype(LOW)
    grad_mixed_own = right_dot(grad_branch, out_full).astype(LOW)
    grad_mixed = links.exchange(grad_mixed_own.reshape(rows, GROUP, shard).transpose(1, 0, 2))
    grad_mixed = grad_mixed.reshape(GROUP * rows, shard)

    out_parts = left_dot(mixed, grad_branch).astype(LOW)
    out_parts = out_parts.reshape(planes, GROUP, own_rows, width)
    near, far = (
        jnp.stack(
            [lax.dynamic_index_in_dim(out_parts, place ^ r, 1, False) for r in order]
        ).reshape(4, planes * own_rows, width)
        for order in ((0, 2, 4, 6), (1, 3, 5, 7))
    )
    out_half = links.core_sum(near, far)
    both_half = jnp.concatenate([feed_half, out_half], axis=1)
    both_sum = links.chip_sum(both_half)
    feed, out_sum = both_sum[:rows], both_sum[rows:].astype(LOW)
    block_out = (middle + feed + bias_down).astype(LOW)

    hidden_two, activated_low, _ = lax.optimization_barrier(
        (hidden_two, activated_low, grad_mixed_own)
    )
    pieces = [left_dot(hidden_two, grad_pre_low).astype(LOW).reshape(planes, -1, hidden_shard)]
    for start in range(0, width, hidden_shard):
        piece = left_dot(activated_low, grad_feed[:, start : start + hidden_shard]).astype(LOW)
        pieces.append(piece.reshape(planes, own_hidden, hidden_shard))
    both_rows = lax.psum_scatter(
        jnp.concatenate(pieces, axis=1), "dp", axis_index_groups=links.plane_groups()
    )
    up_rows = both_rows[: GROUP * own_rows].reshape(GROUP, own_rows, hidden_shard)
    grad_down_w = both_rows[GROUP * own_rows :].reshape(-1, own_hidden, hidden_shard)
    grad_down_w = grad_down_w.transpose(1, 0, 2).reshape(own_hidden, width).astype(WIDE)

    grad_packed = attention_back(packed, after(grad_mixed, both_half), allowed, place)
    far = right_dot(grad_packed[half_rows:], qkv_full).astype(LOW)
    near = right_dot(grad_packed[:half_rows], qkv_full).astype(LOW)
    grad_hidden_half = links.core_sum(near, far).reshape(4, rows, width)
    grad_hidden_one = links.chip_sum(after(grad_hidden_half, both_sum))
    normed_one, inverse_one = norm_rows(token_rows)
    grad_inputs = grad_middle + norm_back(grad_hidden_one, normed_one, inverse_one, gain_one)

    proj_rows = left_dot(hidden_one, grad_packed).astype(LOW)
    proj_rows = proj_rows.reshape(planes, GROUP, own_rows, heads_width)
    proj_rows = links.plane_sum(proj_rows).astype(LOW)
    grad_out_w = links.plane_exchange(out_sum.reshape(planes, own_rows, width))
    grad_out_w = jnp.sum(grad_out_w.astype(WIDE), axis=0)
    row_blocks = links.exchange(jnp.concatenate([proj_rows, up_rows], axis=2)).astype(WIDE)
    grad_proj_w = row_blocks[:, :, :heads_width]
    grad_proj_w = grad_proj_w.reshape(GROUP, own_rows, 3, shard).transpose(1, 2, 0, 3)
    grad_proj_w = grad_proj_w.reshape(own_rows, 3 * width)
    grad_up_w = row_blocks[:, :, heads_width:]
    grad_up_w = grad_up_w.reshape(GROUP, own_rows, planes, own_hidden).transpose(1, 2, 0, 3)
    grad_up_w = grad_up_w.reshape(own_rows, hidden)

    packed_sums = jnp.sum(grad_packed.astype(WIDE), axis=0)
    proj_sums = jnp.zeros((2, width), WIDE)
    proj_sums = lax.dynamic_update_slice_in_dim(
        proj_sums,
        jnp.stack([packed_sums[:shard], packed_sums[2 * shard :]]),
        place * shard,
        1,
    )
    up_sums = jnp.zeros((planes, GROUP, own_hidden), WIDE)
    up_sums = lax.dynamic_update_index_in_dim(
        up_sums,
        jnp.sum(grad_pre_low.astype(WIDE), axis=0).reshape(planes, own_hidden),
        place,
        1,
    )
    def over_tokens(scale):
        terms = ((near, normed_all[:half_rows]), (far, normed_all[half_rows:]))
        return sum(
            jnp.sum(part.astype(WIDE) * (normed if scale else 1.0), axis=0)
            for part, normed in terms
        )

    vectors = [
        over_tokens(True),
        over_tokens(False),
        jnp.sum(grad_branch.astype(WIDE), axis=0),
        jnp.sum(grad_hidden_two * normed_two, axis=0),
        jnp.sum(grad_hidden_two, axis=0),
        jnp.sum(grad_feed_own.astype(WIDE), axis=0),
        proj_sums,
        up_sums,
    ]
    vectors = jnp.concatenate([v.reshape(planes, GROUP, -1) for v in vectors], axis=2)
    vectors = vectors.reshape(count, -1)
    sums = jnp.sum(lax.all_to_all(vectors, "dp", 0, 0, tiled=True), axis=0)
    grads = [sums[i * own_rows : (i + 1) * own_rows] for i in range(6)]
    grad_proj_b = sums[6 * own_rows : 8 * own_rows]
    grad_up_b = sums[8 * own_rows :]
    return (
        block_out,
        grad_inputs,
        grads[0],
        grads[1],
        grad_proj_w,
        grad_proj_b,
        grad_out_w,
        grads[2],
        grads[3],
        grads[4],
        grad_up_w,
        grad_up_b,
        grad_down_w,
        grads[5],
    )


def solution(mesh):
    flat, wide = P("dp"), P("dp", None)
    in_specs = (
        (wide, flat, flat, flat, flat, wide, flat, wide, flat, flat, flat, wide, flat, wide)
        + (flat, wide)
    )
    out_specs = (
        (wide, wide, flat, flat, wide, flat, wide, flat, flat, flat, wide, flat, wide, flat)
    )
    return jax.shard_map(local, mesh=mesh, in_specs=in_specs, out_specs=out_specs, check_vma=False)
```

profile of v0, /device:TPU:0, one launch (start us, length us, event | category | flops | bytes accessed | tf_op | source)
XLA Modules:
  0.0 300.1 jit_solution(16017935430561951993)
XLA Ops:
  9.9 5.2 %all-to-all-start = ((bf16[8,32,512]{2,1,0:T(8,128)(2,1)}), bf16[8,32,512]{2,1,0:T(8,128)(2,1)S(1)}, u32[]{:S(2)}, u32[]{:S(2)}) async-start(bf16[8,32,512]{2,1,0:T(8,128)(2,1)} %reshape.329), calls=%async_computation | async-start | bytes 524288 | tf_op jit(solution)/shard_map/all_to_all | solution.py:216
  15.5 6.6 %all-to-all-done = bf16[8,32,512]{2,1,0:T(8,128)(2,1)S(1)} async-done(((bf16[8,32,512]{2,1,0:T(8,128)(2,1)}), bf16[8,32,512]{2,1,0:T(8,128)(2,1)S(1)}, u32[]{:S(2)}, u32[]{:S(2)}) %all-to-all-start) | async-done | bytes 262176 | tf_op jit(solution)/shard_map/all_to_all | solution.py:216
  23.1 4.0 %all-to-all-start.1 = ((bf16[32,104,128]{2,1,0:T(8,128)(2,1)}), bf16[32,104,128]{2,1,0:T(8,128)(2,1)S(1)}, u32[]{:S(2)}, u32[]{:S(2)}) async-start(bf16[32,104,128]{2,1,0:T(8,128)(2,1)} %bitcast.7), calls=%async_computation.1 | async-start | bytes 1703936 | tf_op jit(solution)/shard_map/all_to_all | solution.py:301
  27.1 1.8 collective-permute-start
  30.9 1.8 collective-permute-start.10
  32.8 2.4 collective-permute-start.11
  37.0 8.4 %collective-permute-done = bf16[128,1024]{1,0:T(8,128)(2,1)S(1)} collective-permute-done((bf16[128,1024]{1,0:T(8,128)(2,1)S(1)}, bf16[128,1024]{1,0:T(8,128)(2,1)S(1)}, u32[]{:S(2)}, u32[]{:S(2)}) %collective-permute-start) | collective-permute-done | bytes 262176 | tf_op jit(solution)/shard_map/ppermute | solution.py:185
  45.3 3.0 collective-permute-start.12
  49.0 3.4 %collective-permute-done.2 = bf16[128,1024]{1,0:T(8,128)(2,1)} collective-permute-done((bf16[128,1024]{1,0:T(8,128)(2,1)S(1)}, bf16[128,1024]{1,0:T(8,128)(2,1)}, u32[]{:S(2)}, u32[]{:S(2)}) %collective-permute-start.2) | collective-permute-done | bytes 262176 | tf_op jit(solution)/shard_map/ppermute | solution.py:185
  55.2 14.4 %collective-permute-done.11 = bf16[8,32,512]{2,1,0:T(8,128)(2,1)S(1)} collective-permute-done((bf16[8,32,512]{2,1,0:T(8,128)(2,1)S(1)}, bf16[8,32,512]{2,1,0:T(8,128)(2,1)S(1)}, u32[]{:S(2)}, u32[]{:S(2)}) %collective-permute-start.11) | collective-permute-done | bytes 262176 | tf_op jit(solution)/shard_map/ppermute | solution.py:189
  75.1 2.2 add_convert_fusion.4.refs_0_
  82.5 6.8 %shard_map.263 = bf16[1024,128]{1,0:T(8,128)(2,1)} custom-call(s32[1]{0:T(128)} %bitcast.place_ref, bf16[1024,384]{1,0:T(8,128)(2,1)} %add_convert_fusion.4.refs_0_, f32[8,128,128]{2,1,0:T(8,128)} %and_convert_fusion.refs_1_.refs_2_), custom_call_target="tpu_custom_call" | custom-call | flops 134217728 | bytes 1310720 | tf_op jit(solution)/shard_map/pallas_call | solution.py:132
  96.8 3.6 %all-to-all-start.2 = ((bf16[8,128,128]{1,2,0:T(8,128)(2,1)}), bf16[8,128,128]{1,2,0:T(8,128)(2,1)S(1)}, u32[]{:S(2)}, u32[]{:S(2)}) async-start(bf16[8,128,128]{1,2,0:T(8,128)(2,1)} %copy.69), calls=%async_computation.2 | async-start | bytes 524288 | tf_op jit(solution)/shard_map/all_to_all | solution.py:216
  101.5 5.5 %all-to-all-done.2 = bf16[8,128,128]{1,2,0:T(8,128)(2,1)S(1)} async-done(((bf16[8,128,128]{1,2,0:T(8,128)(2,1)}), bf16[8,128,128]{1,2,0:T(8,128)(2,1)S(1)}, u32[]{:S(2)}, u32[]{:S(2)}) %all-to-all-start.2) | async-done | bytes 262176 | tf_op jit(solution)/shard_map/all_to_all | solution.py:216
  107.1 2.3 fusion.64
  110.9 2.4 collective-permute-start.9
  114.7 4.4 %collective-permute-done.7 = bf16[128,1024]{1,0:T(8,128)(2,1)S(1)} collective-permute-done((bf16[128,1024]{1,0:T(8,128)(2,1)S(1)}, bf16[128,1024]{1,0:T(8,128)(2,1)S(1)}, u32[]{:S(2)}, u32[]{:S(2)}) %collective-permute-start.7) | collective-permute-done | bytes 262176 | tf_op jit(solution)/shard_map/ppermute | solution.py:185
  119.1 4.9 %collective-permute-done.8 = bf16[128,1024]{1,0:T(8,128)(2,1)S(1)} collective-permute-done((bf16[128,1024]{1,0:T(8,128)(2,1)S(1)}, bf16[128,1024]{1,0:T(8,128)(2,1)S(1)}, u32[]{:S(2)}, u32[]{:S(2)}) %collective-permute-start.8) | collective-permute-done | bytes 262176 | tf_op jit(solution)/shard_map/ppermute | solution.py:185
  130.7 3.8 %fusion.65 = f32[1024,512]{1,0:T(8,128)} fusion(bf16[1024,1024]{1,0:T(8,128)(2,1)S(1)} %constant_dynamic-update-slice_fusion.6, bf16[1024,512]{1,0:T(8,128)(2,1)} %bitcast.22), kind=kOutput, calls=%fused_computation.193 | convolution fusion | flops 1073741824 | bytes 5242880 | tf_op jit(solution)/shard_map/dot_general | solution.py:46
  134.6 6.5 %convert_reduce_fusion.3 = (f32[512]{0:T(512)S(1)}, bf16[1024,512]{1,0:T(8,128)(2,1)S(1)}, bf16[1024,512]{1,0:T(8,128)(2,1)}) fusion(f32[1024,512]{1,0:T(8,128)} %fusion.65, f32[512]{0:T(512)S(1)} %bitcast.208, bf16[1024,1024]{1,0:T(8,128)(2,1)} %copy-done.16, bf16[512,1024]{1,0:T(8,128)(2,1)} %all-gather.5.cloned.1.call-done), kind=kOutput, calls=%fused_computation.35 | convolution fusion | flops 1088945664 | bytes 7344128 | tf_op jit(solution)/shard_map/dot_general | solution.py:46
  141.1 3.3 %convolution_convert_fusion.4 = bf16[512,1024]{1,0:T(8,128)(2,1)} fusion(bf16[1024,512]{1,0:T(8,128)(2,1)} %bitcast.22, bf16[1024,512]{1,0:T(8,128)(2,1)S(1)} %get-tuple-element.53), kind=kOutput, calls=%fused_computation.46 | convolution fusion | flops 537395200 | bytes 2621440 | tf_op jit(solution)/shard_map/dot_general | solution.py:46
  145.8 3.1 %convolution_convert_fusion.6 = bf16[512,1024]{1,0:T(8,128)(2,1)} fusion(bf16[512,1024]{1,0:T(8,128)(2,1)} %all-gather.5.cloned.1.call-done, bf16[1024,512]{1,0:T(8,128)(2,1)} %get-tuple-element.35), kind=kOutput, calls=%fused_computation.48 | convolution fusion | flops 537395200 | bytes 2621440 | tf_op jit(solution)/shard_map/dot_general | solution.py:46
  149.3 2.5 fusion
  152.0 2.1 convolution_convert_fusion.5
  159.6 2.9 add_convert_fusion.3
  162.5 3.7 %collective-permute-done.17 = bf16[128,1024]{1,0:T(8,128)(2,1)S(1)} collective-permute-done((bf16[128,1024]{1,0:T(8,128)(2,1)S(1)}, bf16[128,1024]{1,0:T(8,128)(2,1)S(1)}, u32[]{:S(2)}, u32[]{:S(2)}) %collective-permute-start.17) | collective-permute-done | bytes 262176 | tf_op jit(solution)/shard_map/ppermute | solution.py:185
  166.1 3.8 %collective-permute-done.18 = bf16[128,1024]{1,0:T(8,128)(2,1)S(1)} collective-permute-done((bf16[128,1024]{1,0:T(8,128)(2,1)S(1)}, bf16[128,1024]{1,0:T(8,128)(2,1)S(1)}, u32[]{:S(2)}, u32[]{:S(2)}) %collective-permute-start.18) | collective-permute-done | bytes 262176 | tf_op jit(solution)/shard_map/ppermute | solution.py:185
  176.3 2.1 convolution_convert_fusion
  178.4 4.0 %all-to-all-start.3 = ((bf16[8,128,128]{2,1,0:T(8,128)(2,1)}), bf16[8,128,128]{2,1,0:T(8,128)(2,1)}, u32[]{:S(2)}, u32[]{:S(2)}) async-start(bf16[8,128,128]{2,1,0:T(8,128)(2,1)} %bitcast_bitcast_fusion), calls=%async_computation.3 | async-start | bytes 524288 | tf_op jit(solution)/shard_map/all_to_all | solution.py:216
  182.5 3.2 %convolution_convert_fusion.1 = bf16[1024,512]{1,0:T(8,128)(2,1)S(1)} fusion(bf16[1024,1024]{1,0:T(8,128)(2,1)} %copy-done.18, bf16[1024,512]{1,0:T(8,128)(2,1)} %copy-done.48), kind=kOutput, calls=%fused_computation.43 | convolution fusion | flops 1074266112 | bytes 4194304 | tf_op jit(solution)/shard_map/dot_general | solution.py:46
  187.3 2.9 constant_dynamic-slice_fusion.7
  190.4 2.3 pad_maximum_fusion.5
  193.0 8.0 %shard_map.264 = bf16[1024,384]{1,0:T(8,128)(2,1)} custom-call(s32[1]{0:T(128)} %bitcast.place_ref, bf16[1024,384]{1,0:T(8,128)(2,1)} %add_convert_fusion.4.refs_0_, bf16[1024,128]{1,0:T(8,128)(2,1)} %bitcast.41.refs_1_, f32[8,128,128]{2,1,0:T(8,128)} %and_convert_fusion.refs_1_.refs_2_), custom_call_target="tpu_custom_call" | custom-call | flops 335544320 | bytes 2097152 | tf_op jit(solution)/shard_map/pallas_call | solution.py:155
  201.0 3.4 %convolution_convert_fusion.2 = bf16[512,1024]{1,0:T(8,128)(2,1)} fusion(bf16[1024,384]{1,0:T(8,128)(2,1)} %shard_map.264, bf16[1024,128]{1,0:T(8,128)(2,1)} %bitcast.198, bf16[1024,128]{1,0:T(8,128)(2,1)} %bitcast.201, bf16[1024,128]{1,0:T(8,128)(2,1)} %bitcast.195), kind=kOutput, calls=%fused_computation.44 | convolution fusion | flops 405536768 | bytes 2228224 | tf_op jit(solution)/shard_map/dot_general | solution.py:46
  207.0 7.4 %collective-permute-start.28 = (bf16[8,32,384]{2,1,0:T(8,128)(2,1)}, bf16[8,32,384]{2,1,0:T(8,128)(2,1)}, u32[]{:S(2)}, u32[]{:S(2)}) collective-permute-start(bf16[8,32,384]{2,1,0:T(8,128)(2,1)} %get-tuple-element.84), channel_id=1, source_target_pairs={{0,8},{1,9},{2,10},{3,11},{4,12},{5,13},{6,14},{7,15},{8,16},{9,17... | collective-permute-start | bytes 589832 | tf_op jit(solution)/shard_map/ppermute | solution.py:189
  214.4 3.6 %collective-permute-start.29 = (bf16[8,32,384]{2,1,0:T(8,128)(2,1)}, bf16[8,32,384]{2,1,0:T(8,128)(2,1)}, u32[]{:S(2)}, u32[]{:S(2)}) collective-permute-start(bf16[8,32,384]{2,1,0:T(8,128)(2,1)} %get-tuple-element.86), channel_id=1, source_target_pairs={{0,16},{1,17},{2,18},{3,19},{4,20},{5,21},{6,22},{7,23},{8,24},{9,... | collective-permute-start | bytes 589832 | tf_op jit(solution)/shard_map/ppermute | solution.py:189
  218.9 2.1 add_convert_fusion.1
  222.2 2.8 collective-permute-start.21
  224.9 2.7 collective-permute-done.28
  231.0 3.6 %fusion.3 = (f32[1024]{0:T(1024)S(1)}, f32[1024]{0:T(1024)S(1)}, f32[1024]{0:T(1024)S(1)}, f32[1024]{0:T(1024)S(1)}, bf16[512,1024]{1,0:T(8,128)(2,1)}) fusion(bf16[512,1024]{1,0:T(8,128)(2,1)} %convolution_convert_fusion.2, f32[1024,1024]{1,0:T(8,128)S(1)} %copy-done.2, bf16[512,1024]{1,0:T(8,128)(2,1)} %collective-permute-done.24, ...), kind=kOutput, calls=%fused_computation.24 | convolution fusion | flops 411299840 | bytes 8536064 | tf_op jit(solution)/shard_map/dot_general | solution.py:46
  236.3 6.5 %all-to-all-start.4 = ((f32[32,1,384]{2,1,0:T(1,128)}), f32[32,1,384]{2,1,0:T(1,128)S(1)}, u32[]{:S(2)}, u32[]{:S(2)}) async-start(f32[32,1,384]{2,1,0:T(1,128)} %all_to_all.28), calls=%async_computation.4 | async-start | bytes 98304 | tf_op jit(solution)/shard_map/all_to_all | solution.py:460
  242.8 2.0 fusion.48
  244.8 13.0 %all-to-all-done.4 = f32[32,1,384]{2,1,0:T(1,128)S(1)} async-done(((f32[32,1,384]{2,1,0:T(1,128)}), f32[32,1,384]{2,1,0:T(1,128)S(1)}, u32[]{:S(2)}, u32[]{:S(2)}) %all-to-all-start.4) | async-done | bytes 49184 | tf_op jit(solution)/shard_map/all_to_all | solution.py:460
  266.5 3.4 %all-to-all-start.6 = ((bf16[4,32,1024]{2,1,0:T(8,128)(2,1)}), bf16[4,32,1024]{2,1,0:T(8,128)(2,1)S(1)}, u32[]{:S(2)}, u32[]{:S(2)}) async-start(bf16[4,32,1024]{2,1,0:T(8,128)(2,1)} %bitcast.61), calls=%async_computation.7 | async-start | bytes 524288 | tf_op jit(solution)/shard_map/all_to_all | solution.py:211
  270.0 1.9 fusion.35
  271.8 2.9 collective-permute-done.26
  278.2 3.5 %all-to-all-start.5 = ((bf16[8,32,896]{2,1,0:T(8,128)(2,1)}), bf16[8,32,896]{2,1,0:T(8,128)(2,1)S(1)}, u32[]{:S(2)}, u32[]{:S(2)}) async-start(bf16[8,32,896]{2,1,0:T(8,128)(2,1)} %pad_maximum_fusion.7), calls=%async_computation.6 | async-start | bytes 917504 | tf_op jit(solution)/shard_map/all_to_all | solution.py:216
  284.6 6.1 %all-to-all-done.5 = bf16[8,32,896]{2,1,0:T(8,128)(2,1)S(1)} async-done(((bf16[8,32,896]{2,1,0:T(8,128)(2,1)}), bf16[8,32,896]{2,1,0:T(8,128)(2,1)S(1)}, u32[]{:S(2)}, u32[]{:S(2)}) %all-to-all-start.5) | async-done | bytes 458784 | tf_op jit(solution)/shard_map/all_to_all | solution.py:216
  (272 shorter events, 83.2 us)
Async XLA Ops:
  7.3 99.8 %all-gather.3.cloned.1.call-start = ((), (), s32[]{:S(2)}) async-start(), calls=%async_computation.8 | async-start | bytes 2162688 | tf_op jit(solution)/shard_map/all_gather | solution.py:303
  9.9 12.1 %all-to-all-start = ((bf16[8,32,512]{2,1,0:T(8,128)(2,1)}), bf16[8,32,512]{2,1,0:T(8,128)(2,1)S(1)}, u32[]{:S(2)}, u32[]{:S(2)}) async-start(bf16[8,32,512]{2,1,0:T(8,128)(2,1)} %reshape.329), calls=%async_computation | async-start | bytes 524288 | tf_op jit(solution)/shard_map/all_to_all | solution.py:216
  15.1 15.6 %copy-start.11 = (bf16[128,1024]{1,0:T(8,128)(2,1)S(1)}, bf16[128,1024]{1,0:T(8,128)(2,1)}, u32[]{:S(2)}) copy-start(bf16[128,1024]{1,0:T(8,128)(2,1)} %param.31) | copy-start | bytes 786436
  23.1 47.3 %all-to-all-start.1 = ((bf16[32,104,128]{2,1,0:T(8,128)(2,1)}), bf16[32,104,128]{2,1,0:T(8,128)(2,1)S(1)}, u32[]{:S(2)}, u32[]{:S(2)}) async-start(bf16[32,104,128]{2,1,0:T(8,128)(2,1)} %bitcast.7), calls=%async_computation.1 | async-start | bytes 1703936 | tf_op jit(solution)/shard_map/all_to_all | solution.py:301
  27.0 107.5 %all-gather.5.cloned.1.call-start = ((), (), s32[]{:S(2)}) async-start(), calls=%async_computation.9 | async-start | bytes 1310720 | tf_op jit(solution)/shard_map/all_gather | solution.py:304
  27.1 18.2 %collective-permute-start = (bf16[128,1024]{1,0:T(8,128)(2,1)S(1)}, bf16[128,1024]{1,0:T(8,128)(2,1)S(1)}, u32[]{:S(2)}, u32[]{:S(2)}) collective-permute-start(bf16[128,1024]{1,0:T(8,128)(2,1)S(1)} %copy-done), channel_id=1, source_target_pairs={{0,2},{1,3},{2,0},{3,1},{4,6},{5,7},{6,4},{7,5},{8,10},{9,11},{10,... | collective-permute-start | bytes 786440 | tf_op jit(solution)/shard_map/ppermute | solution.py:185
  28.9 19.4 %collective-permute-start.1 = (bf16[128,1024]{1,0:T(8,128)(2,1)S(1)}, bf16[128,1024]{1,0:T(8,128)(2,1)S(1)}, u32[]{:S(2)}, u32[]{:S(2)}) collective-permute-start(bf16[128,1024]{1,0:T(8,128)(2,1)S(1)} %copy-done), channel_id=1, source_target_pairs={{0,4},{1,5},{2,6},{3,7},{4,0},{5,1},{6,2},{7,3},{8,12},{9,13},{10,... | collective-permute-start | bytes 786440 | tf_op jit(solution)/shard_map/ppermute | solution.py:185
  30.4 22.0 %collective-permute-start.2 = (bf16[128,1024]{1,0:T(8,128)(2,1)S(1)}, bf16[128,1024]{1,0:T(8,128)(2,1)}, u32[]{:S(2)}, u32[]{:S(2)}) collective-permute-start(bf16[128,1024]{1,0:T(8,128)(2,1)S(1)} %copy-done), channel_id=1, source_target_pairs={{0,6},{1,7},{2,4},{3,5},{4,2},{5,3},{6,0},{7,1},{8,14},{9,15},{10,... | collective-permute-start | bytes 786440 | tf_op jit(solution)/shard_map/ppermute | solution.py:185
  30.9 23.5 %collective-permute-start.10 = (bf16[8,32,512]{2,1,0:T(8,128)(2,1)S(1)}, bf16[8,32,512]{2,1,0:T(8,128)(2,1)S(1)}, u32[]{:S(2)}, u32[]{:S(2)}) collective-permute-start(bf16[8,32,512]{2,1,0:T(8,128)(2,1)S(1)} %all-to-all-done), channel_id=1, source_target_pairs={{0,8},{1,9},{2,10},{3,11},{4,12},{5,13},{6,14},{7,15},{8,16},{9,17... | collective-permute-start | bytes 786440 | tf_op jit(solution)/shard_map/ppermute | solution.py:189
  32.8 36.8 %collective-permute-start.11 = (bf16[8,32,512]{2,1,0:T(8,128)(2,1)S(1)}, bf16[8,32,512]{2,1,0:T(8,128)(2,1)S(1)}, u32[]{:S(2)}, u32[]{:S(2)}) collective-permute-start(bf16[8,32,512]{2,1,0:T(8,128)(2,1)S(1)} %all-to-all-done), channel_id=1, source_target_pairs={{0,16},{1,17},{2,18},{3,19},{4,20},{5,21},{6,22},{7,23},{8,24},{9,... | collective-permute-start | bytes 786440 | tf_op jit(solution)/shard_map/ppermute | solution.py:189
  45.3 55.0 %collective-permute-start.12 = (bf16[8,32,512]{2,1,0:T(8,128)(2,1)S(1)}, bf16[8,32,512]{2,1,0:T(8,128)(2,1)S(1)}, u32[]{:S(2)}, u32[]{:S(2)}) collective-permute-start(bf16[8,32,512]{2,1,0:T(8,128)(2,1)S(1)} %all-to-all-done), channel_id=1, source_target_pairs={{0,24},{1,25},{2,26},{3,27},{4,28},{5,29},{6,30},{7,31},{8,0},{9,1... | collective-permute-start | bytes 786440 | tf_op jit(solution)/shard_map/ppermute | solution.py:189
  71.3 2.7 collective-permute-start.3
  71.4 133.1 %copy-start.30 = (f32[1024]{0:T(1024)}, f32[1024]{0:T(1024)S(1)}, u32[]{:S(2)}) copy-start(f32[1024]{0:T(1024)S(1)} %reshape.351) | copy-start | bytes 12292
  77.3 12.0 %collective-permute-start.4 = (bf16[128,1024]{1,0:T(8,128)(2,1)S(1)}, bf16[128,1024]{1,0:T(8,128)(2,1)}, u32[]{:S(2)}, u32[]{:S(2)}) collective-permute-start(bf16[128,1024]{1,0:T(8,128)(2,1)S(1)} %get-tuple-element.28), channel_id=1, source_target_pairs={{0,2},{1,3},{2,0},{3,1},{4,6},{5,7},{6,4},{7,5},{8,10},{9,11},{10,... | collective-permute-start | bytes 786440 | tf_op jit(solution)/shard_map/ppermute | solution.py:185
  78.7 13.8 %collective-permute-start.5 = (bf16[128,1024]{1,0:T(8,128)(2,1)S(1)}, bf16[128,1024]{1,0:T(8,128)(2,1)S(1)}, u32[]{:S(2)}, u32[]{:S(2)}) collective-permute-start(bf16[128,1024]{1,0:T(8,128)(2,1)S(1)} %get-tuple-element.28), channel_id=1, source_target_pairs={{0,4},{1,5},{2,6},{3,7},{4,0},{5,1},{6,2},{7,3},{8,12},{9,13},{10,... | collective-permute-start | bytes 786440 | tf_op jit(solution)/shard_map/ppermute | solution.py:185
  81.2 12.1 %collective-permute-start.6 = (bf16[128,1024]{1,0:T(8,128)(2,1)S(1)}, bf16[128,1024]{1,0:T(8,128)(2,1)}, u32[]{:S(2)}, u32[]{:S(2)}) collective-permute-start(bf16[128,1024]{1,0:T(8,128)(2,1)S(1)} %get-tuple-element.28), channel_id=1, source_target_pairs={{0,6},{1,7},{2,4},{3,5},{4,2},{5,3},{6,0},{7,1},{8,14},{9,15},{10,... | collective-permute-start | bytes 786440 | tf_op jit(solution)/shard_map/ppermute | solution.py:185
  96.8 10.3 %all-to-all-start.2 = ((bf16[8,128,128]{1,2,0:T(8,128)(2,1)}), bf16[8,128,128]{1,2,0:T(8,128)(2,1)S(1)}, u32[]{:S(2)}, u32[]{:S(2)}) async-start(bf16[8,128,128]{1,2,0:T(8,128)(2,1)} %copy.69), calls=%async_computation.2 | async-start | bytes 524288 | tf_op jit(solution)/shard_map/all_to_all | solution.py:216
  101.3 12.1 %collective-permute-start.13 = (bf16[512,1024]{1,0:T(8,128)(2,1)}, bf16[512,1024]{1,0:T(8,128)(2,1)}, u32[]{:S(2)}, u32[]{:S(2)}) collective-permute-start(bf16[512,1024]{1,0:T(8,128)(2,1)} %constant_dynamic-update-slice_fusion), channel_id=1, source_target_pairs={{0,1},{1,0},{2,3},{3,2},{4,5},{5,4},{6,7},{7,6},{8,9},{9,8},{10,11... | collective-permute-start | bytes 3145736 | tf_op jit(solution)/shard_map/ppermute | solution.py:185
  109.8 9.3 %collective-permute-start.7 = (bf16[128,1024]{1,0:T(8,128)(2,1)S(1)}, bf16[128,1024]{1,0:T(8,128)(2,1)S(1)}, u32[]{:S(2)}, u32[]{:S(2)}) collective-permute-start(bf16[128,1024]{1,0:T(8,128)(2,1)S(1)} %add_convert_fusion.7), channel_id=1, source_target_pairs={{0,2},{1,3},{2,0},{3,1},{4,6},{5,7},{6,4},{7,5},{8,10},{9,11},{10,... | collective-permute-start | bytes 786440 | tf_op jit(solution)/shard_map/ppermute | solution.py:185
  110.4 13.6 %collective-permute-start.8 = (bf16[128,1024]{1,0:T(8,128)(2,1)S(1)}, bf16[128,1024]{1,0:T(8,128)(2,1)S(1)}, u32[]{:S(2)}, u32[]{:S(2)}) collective-permute-start(bf16[128,1024]{1,0:T(8,128)(2,1)S(1)} %add_convert_fusion.7), channel_id=1, source_target_pairs={{0,4},{1,5},{2,6},{3,7},{4,0},{5,1},{6,2},{7,3},{8,12},{9,13},{10,... | collective-permute-start | bytes 786440 | tf_op jit(solution)/shard_map/ppermute | solution.py:185
  110.9 13.0 %collective-permute-start.9 = (bf16[128,1024]{1,0:T(8,128)(2,1)S(1)}, bf16[128,1024]{1,0:T(8,128)(2,1)S(1)}, u32[]{:S(2)}, u32[]{:S(2)}) collective-permute-start(bf16[128,1024]{1,0:T(8,128)(2,1)S(1)} %add_convert_fusion.7), channel_id=1, source_target_pairs={{0,6},{1,7},{2,4},{3,5},{4,2},{5,3},{6,0},{7,1},{8,14},{9,15},{10,... | collective-permute-start | bytes 786440 | tf_op jit(solution)/shard_map/ppermute | solution.py:185
  125.1 3.0 %collective-permute-start.14 = (bf16[512,1024]{1,0:T(8,128)(2,1)}, bf16[512,1024]{1,0:T(8,128)(2,1)}, u32[]{:S(2)}, u32[]{:S(2)}) collective-permute-start(bf16[512,1024]{1,0:T(8,128)(2,1)} %pad_maximum_fusion.4), channel_id=1, source_target_pairs={{0,1},{1,0},{2,3},{3,2},{4,5},{5,4},{6,7},{7,6},{8,9},{9,8},{10,11... | collective-permute-start | bytes 3145736 | tf_op jit(solution)/shard_map/ppermute | solution.py:185
  144.4 9.7 %collective-permute-start.16 = (bf16[512,1024]{1,0:T(8,128)(2,1)}, bf16[512,1024]{1,0:T(8,128)(2,1)}, u32[]{:S(2)}, u32[]{:S(2)}) collective-permute-start(bf16[512,1024]{1,0:T(8,128)(2,1)} %convolution_convert_fusion.4), channel_id=1, source_target_pairs={{0,1},{1,0},{2,3},{3,2},{4,5},{5,4},{6,7},{7,6},{8,9},{9,8},{10,11... | collective-permute-start | bytes 3145736 | tf_op jit(solution)/shard_map/ppermute | solution.py:185
  148.9 10.7 %collective-permute-start.15 = (bf16[512,1024]{1,0:T(8,128)(2,1)}, bf16[512,1024]{1,0:T(8,128)(2,1)}, u32[]{:S(2)}, u32[]{:S(2)}) collective-permute-start(bf16[512,1024]{1,0:T(8,128)(2,1)} %convolution_convert_fusion.6), channel_id=1, source_target_pairs={{0,1},{1,0},{2,3},{3,2},{4,5},{5,4},{6,7},{7,6},{8,9},{9,8},{10,11... | collective-permute-start | bytes 3145736 | tf_op jit(solution)/shard_map/ppermute | solution.py:185
  156.0 10.2 %collective-permute-start.17 = (bf16[128,1024]{1,0:T(8,128)(2,1)S(1)}, bf16[128,1024]{1,0:T(8,128)(2,1)S(1)}, u32[]{:S(2)}, u32[]{:S(2)}) collective-permute-start(bf16[128,1024]{1,0:T(8,128)(2,1)S(1)} %get-tuple-element.76), channel_id=1, source_target_pairs={{0,6},{1,7},{2,4},{3,5},{4,2},{5,3},{6,0},{7,1},{8,14},{9,15},{10,... | collective-permute-start | bytes 786440 | tf_op jit(solution)/shard_map/ppermute | solution.py:185
  157.2 12.7 %collective-permute-start.18 = (bf16[128,1024]{1,0:T(8,128)(2,1)S(1)}, bf16[128,1024]{1,0:T(8,128)(2,1)S(1)}, u32[]{:S(2)}, u32[]{:S(2)}) collective-permute-start(bf16[128,1024]{1,0:T(8,128)(2,1)S(1)} %get-tuple-element.78), channel_id=1, source_target_pairs={{0,2},{1,3},{2,0},{3,1},{4,6},{5,7},{6,4},{7,5},{8,10},{9,11},{10,... | collective-permute-start | bytes 786440 | tf_op jit(solution)/shard_map/ppermute | solution.py:185
  157.9 13.4 %copy-start.12 = (bf16[128,1024]{1,0:T(8,128)(2,1)S(1)}, bf16[128,1024]{1,0:T(8,128)(2,1)}, u32[]{:S(2)}) copy-start(bf16[128,1024]{1,0:T(8,128)(2,1)} %param.31) | copy-start | bytes 786436
  157.9 13.0 %collective-permute-start.19 = (bf16[128,1024]{1,0:T(8,128)(2,1)S(1)}, bf16[128,1024]{1,0:T(8,128)(2,1)S(1)}, u32[]{:S(2)}, u32[]{:S(2)}) collective-permute-start(bf16[128,1024]{1,0:T(8,128)(2,1)S(1)} %get-tuple-element.77), channel_id=1, source_target_pairs={{0,4},{1,5},{2,6},{3,7},{4,0},{5,1},{6,2},{7,3},{8,12},{9,13},{10,... | collective-permute-start | bytes 786440 | tf_op jit(solution)/shard_map/ppermute | solution.py:185
  178.4 14.6 %all-to-all-start.3 = ((bf16[8,128,128]{2,1,0:T(8,128)(2,1)}), bf16[8,128,128]{2,1,0:T(8,128)(2,1)}, u32[]{:S(2)}, u32[]{:S(2)}) async-start(bf16[8,128,128]{2,1,0:T(8,128)(2,1)} %bitcast_bitcast_fusion), calls=%async_computation.3 | async-start | bytes 524288 | tf_op jit(solution)/shard_map/all_to_all | solution.py:216
  182.4 93.9 %reduce-scatter.2.cloned.1.call-start = ((), (), s32[]{:S(2)}) async-start(), calls=%async_computation.10 | async-start | bytes 2621440 | tf_op jit(solution)/shard_map/reduce_scatter | solution.py:398
  192.7 26.2 %collective-permute-start.20 = (bf16[4,128,1024]{2,1,0:T(8,128)(2,1)}, bf16[4,128,1024]{2,1,0:T(8,128)(2,1)}, u32[]{:S(2)}, u32[]{:S(2)}) collective-permute-start(bf16[4,128,1024]{2,1,0:T(8,128)(2,1)} %pad_maximum_fusion.5), channel_id=1, source_target_pairs={{0,1},{1,0},{2,3},{3,2},{4,5},{5,4},{6,7},{7,6},{8,9},{9,8},{10,11... | collective-permute-start | bytes 3145736 | tf_op jit(solution)/shard_map/ppermute | solution.py:185
  204.4 25.1 %collective-permute-start.24 = (bf16[512,1024]{1,0:T(8,128)(2,1)}, bf16[512,1024]{1,0:T(8,128)(2,1)}, u32[]{:S(2)}, u32[]{:S(2)}) collective-permute-start(bf16[512,1024]{1,0:T(8,128)(2,1)} %convolution_convert_fusion.2), channel_id=1, source_target_pairs={{0,1},{1,0},{2,3},{3,2},{4,5},{5,4},{6,7},{7,6},{8,9},{9,8},{10,11... | collective-permute-start | bytes 3145736 | tf_op jit(solution)/shard_map/ppermute | solution.py:185
  207.0 14.0 %copy-start.3 = (bf16[512,1024]{1,0:T(8,128)(2,1)S(1)}, bf16[512,1024]{1,0:T(8,128)(2,1)}, u32[]{:S(2)}) copy-start(bf16[512,1024]{1,0:T(8,128)(2,1)} %add_convert_fusion.3) | copy-start | bytes 3145732
  207.0 20.7 %collective-permute-start.28 = (bf16[8,32,384]{2,1,0:T(8,128)(2,1)}, bf16[8,32,384]{2,1,0:T(8,128)(2,1)}, u32[]{:S(2)}, u32[]{:S(2)}) collective-permute-start(bf16[8,32,384]{2,1,0:T(8,128)(2,1)} %get-tuple-element.84), channel_id=1, source_target_pairs={{0,8},{1,9},{2,10},{3,11},{4,12},{5,13},{6,14},{7,15},{8,16},{9,17... | collective-permute-start | bytes 589832 | tf_op jit(solution)/shard_map/ppermute | solution.py:189
  214.4 28.4 %collective-permute-start.29 = (bf16[8,32,384]{2,1,0:T(8,128)(2,1)}, bf16[8,32,384]{2,1,0:T(8,128)(2,1)}, u32[]{:S(2)}, u32[]{:S(2)}) collective-permute-start(bf16[8,32,384]{2,1,0:T(8,128)(2,1)} %get-tuple-element.86), channel_id=1, source_target_pairs={{0,16},{1,17},{2,18},{3,19},{4,20},{5,21},{6,22},{7,23},{8,24},{9,... | collective-permute-start | bytes 589832 | tf_op jit(solution)/shard_map/ppermute | solution.py:189
  218.0 24.8 %collective-permute-start.30 = (bf16[8,32,384]{2,1,0:T(8,128)(2,1)}, bf16[8,32,384]{2,1,0:T(8,128)(2,1)}, u32[]{:S(2)}, u32[]{:S(2)}) collective-permute-start(bf16[8,32,384]{2,1,0:T(8,128)(2,1)} %get-tuple-element.85), channel_id=1, source_target_pairs={{0,24},{1,25},{2,26},{3,27},{4,28},{5,29},{6,30},{7,31},{8,0},{9,1... | collective-permute-start | bytes 589832 | tf_op jit(solution)/shard_map/ppermute | solution.py:189
  222.2 35.7 %collective-permute-start.21 = (bf16[256,1024]{1,0:T(8,128)(2,1)}, bf16[256,1024]{1,0:T(8,128)(2,1)}, u32[]{:S(2)}, u32[]{:S(2)}) collective-permute-start(bf16[256,1024]{1,0:T(8,128)(2,1)} %get-tuple-element.61), channel_id=1, source_target_pairs={{0,6},{1,7},{2,4},{3,5},{4,2},{5,3},{6,0},{7,1},{8,14},{9,15},{10,... | collective-permute-start | bytes 1572872 | tf_op jit(solution)/shard_map/ppermute | solution.py:185
  227.7 30.2 %collective-permute-start.22 = (bf16[256,1024]{1,0:T(8,128)(2,1)}, bf16[256,1024]{1,0:T(8,128)(2,1)}, u32[]{:S(2)}, u32[]{:S(2)}) collective-permute-start(bf16[256,1024]{1,0:T(8,128)(2,1)} %get-tuple-element.62), channel_id=1, source_target_pairs={{0,2},{1,3},{2,0},{3,1},{4,6},{5,7},{6,4},{7,5},{8,10},{9,11},{10,... | collective-permute-start | bytes 1572872 | tf_op jit(solution)/shard_map/ppermute | solution.py:185
  229.5 28.4 %collective-permute-start.23 = (bf16[256,1024]{1,0:T(8,128)(2,1)}, bf16[256,1024]{1,0:T(8,128)(2,1)}, u32[]{:S(2)}, u32[]{:S(2)}) collective-permute-start(bf16[256,1024]{1,0:T(8,128)(2,1)} %get-tuple-element.63), channel_id=1, source_target_pairs={{0,4},{1,5},{2,6},{3,7},{4,0},{5,1},{6,2},{7,3},{8,12},{9,13},{10,... | collective-permute-start | bytes 1572872 | tf_op jit(solution)/shard_map/ppermute | solution.py:185
  236.3 21.6 %all-to-all-start.4 = ((f32[32,1,384]{2,1,0:T(1,128)}), f32[32,1,384]{2,1,0:T(1,128)S(1)}, u32[]{:S(2)}, u32[]{:S(2)}) async-start(f32[32,1,384]{2,1,0:T(1,128)} %all_to_all.28), calls=%async_computation.4 | async-start | bytes 98304 | tf_op jit(solution)/shard_map/all_to_all | solution.py:460
  259.7 15.3 %copy-start.31 = (f32[1024]{0:T(1024)S(1)}, f32[1024]{0:T(1024)}, u32[]{:S(2)}) copy-start(f32[1024]{0:T(1024)} %copy-done.30) | copy-start | bytes 12292
  259.7 15.3 %copy-start.34 = (f32[128]{0:T(128)S(1)}, f32[128]{0:T(128)}, u32[]{:S(2)}) copy-start(f32[128]{0:T(128)} %copy-done.33) | copy-start | bytes 1540
  259.7 15.3 %copy-start.35 = (f32[128]{0:T(128)S(1)}, f32[128]{0:T(128)}, u32[]{:S(2)}) copy-start(f32[128]{0:T(128)} %add_rsqrt_fusion.1) | copy-start | bytes 1540
  260.6 11.2 %collective-permute-start.25 = (bf16[128,1024]{1,0:T(8,128)(2,1)}, bf16[128,1024]{1,0:T(8,128)(2,1)S(1)}, u32[]{:S(2)}, u32[]{:S(2)}) collective-permute-start(bf16[128,1024]{1,0:T(8,128)(2,1)} %get-tuple-element.73), channel_id=1, source_target_pairs={{0,6},{1,7},{2,4},{3,5},{4,2},{5,3},{6,0},{7,1},{8,14},{9,15},{10,... | collective-permute-start | bytes 786440 | tf_op jit(solution)/shard_map/ppermute | solution.py:185
  261.4 13.3 %collective-permute-start.26 = (bf16[128,1024]{1,0:T(8,128)(2,1)S(1)}, bf16[128,1024]{1,0:T(8,128)(2,1)S(1)}, u32[]{:S(2)}, u32[]{:S(2)}) collective-permute-start(bf16[128,1024]{1,0:T(8,128)(2,1)S(1)} %get-tuple-element.75), channel_id=1, source_target_pairs={{0,2},{1,3},{2,0},{3,1},{4,6},{5,7},{6,4},{7,5},{8,10},{9,11},{10,... | collective-permute-start | bytes 786440 | tf_op jit(solution)/shard_map/ppermute | solution.py:185
  262.7 12.3 %collective-permute-start.27 = (bf16[128,1024]{1,0:T(8,128)(2,1)S(1)}, bf16[128,1024]{1,0:T(8,128)(2,1)S(1)}, u32[]{:S(2)}, u32[]{:S(2)}) collective-permute-start(bf16[128,1024]{1,0:T(8,128)(2,1)S(1)} %get-tuple-element.74), channel_id=1, source_target_pairs={{0,4},{1,5},{2,6},{3,7},{4,0},{5,1},{6,2},{7,3},{8,12},{9,13},{10,... | collective-permute-start | bytes 786440 | tf_op jit(solution)/shard_map/ppermute | solution.py:185
  266.5 11.7 %all-to-all-start.6 = ((bf16[4,32,1024]{2,1,0:T(8,128)(2,1)}), bf16[4,32,1024]{2,1,0:T(8,128)(2,1)S(1)}, u32[]{:S(2)}, u32[]{:S(2)}) async-start(bf16[4,32,1024]{2,1,0:T(8,128)(2,1)} %bitcast.61), calls=%async_computation.7 | async-start | bytes 524288 | tf_op jit(solution)/shard_map/all_to_all | solution.py:211
  278.2 12.5 %all-to-all-start.5 = ((bf16[8,32,896]{2,1,0:T(8,128)(2,1)}), bf16[8,32,896]{2,1,0:T(8,128)(2,1)S(1)}, u32[]{:S(2)}, u32[]{:S(2)}) async-start(bf16[8,32,896]{2,1,0:T(8,128)(2,1)} %pad_maximum_fusion.7), calls=%async_computation.6 | async-start | bytes 917504 | tf_op jit(solution)/shard_map/all_to_all | solution.py:216
  (42 other events, 260.7 us)
Sparse Core Ops, SparseCore 0:
  11.0 72.8 all-gather.2
  85.5 26.7 all-gather.4
  187.4 65.6 reduce-scatter.1
where the time goes:
time: 302 us; the launch traced here: 300 us
  waiting for transfers between devices  85.8 us (28%)
  starting transfers between devices  73.4 us (24%)
  matrix products  44 us (15%)
  local copies, waits for them, and re-layouts  38.4 us (13%)
  other arithmetic  28.9 us (10%)
  between operations  14.9 us (5%)
  Pallas kernels  14.8 us (5%)
    dot_general x16, matrix products, dot(): lax.dot_general(first, second, (dims, ((), ())), preferred_element_type=j...  44 us
    ppermute x25, waiting for transfers between devices, swap(): return lax.ppermute(array, 'dp', [(i, i ^ flip) for i in range(self.count)])  35.7 us
    ppermute x25, starting transfers between devices, swap(): return lax.ppermute(array, 'dp', [(i, i ^ flip) for i in range(self.count)])  24.9 us
    ppermute x6, starting transfers between devices, shift(): lax.ppermute(array, 'dp', [(i, (i + hop) % self.count) for i in range(sel...  18.2 us
    all_to_all x4, waiting for transfers between devices, exchange(): lax.all_to_all(parts, 'dp', 0, 0, axis_index_groups=self.group_lists(), t...  18.2 us
    ppermute x6, waiting for transfers between devices, shift(): lax.ppermute(array, 'dp', [(i, (i + hop) % self.count) for i in range(sel...  18.1 us
    all_to_all x4, starting transfers between devices, exchange(): lax.all_to_all(parts, 'dp', 0, 0, axis_index_groups=self.group_lists(), t...  16.3 us
    all_to_all x1, waiting for transfers between devices, local(): sums = jnp.sum(lax.all_to_all(vectors, 'dp', 0, 0, tiled=True), axis=0)  13 us
  transfers between devices with their start and end apart: 41, of which 19 were waited for; matrix products, arithmetic and copies ran while one was open for 29% of the time, Pallas kernels for 5%

commit v1 on v0

v1 whole, which is shorter than its diff:
```python
import functools
import math

import jax
import jax.numpy as jnp
from jax import lax
from jax.experimental import pallas as pl
from jax.experimental.pallas import tpu as pltpu
from jax.sharding import PartitionSpec as P

HEAD_DIM = 64
EPS = 1e-05
NEG = -1e30
GROUP = 8
DIRECT_PLANES = 8
VMEM_BYTES = 56 << 20
LOW = jnp.bfloat16
WIDE = jnp.float32


def norm_rows(inputs):
    average = jnp.mean(inputs, axis=-1, keepdims=True)
    centered = inputs - average
    variance = jnp.mean(centered * centered, axis=-1, keepdims=True)
    inverse = lax.rsqrt(variance + EPS)
    return (centered * inverse, inverse)


def norm_back(grad_in, normed, inverse, gain):
    scaled = grad_in * gain
    return inverse * (
        scaled
        - jnp.mean(scaled, axis=1, keepdims=True)
        - normed * jnp.mean(scaled * normed, axis=1, keepdims=True)
    )


def gelu_tanh(inputs):
    return (
        0.5
        * inputs
        * (1.0 + jnp.tanh(0.7978845608028654 * (inputs + 0.044715 * inputs * inputs * inputs)))
    )


def dot(first, second, dims):
    return lax.dot_general(first, second, (dims, ((), ())), preferred_element_type=jnp.float32)


def plain_dot(first, second):
    return dot(first, second, ((1,), (0,)))


def left_dot(first, second):
    return dot(first, second, ((0,), (0,)))


def right_dot(first, second):
    return dot(first, second, ((1,), (1,)))


def head_masks():
    lane = lax.broadcasted_iota(jnp.int32, (1, 2 * HEAD_DIM), 1)
    return [((lane // HEAD_DIM) == h).astype(LOW) for h in range(2)]


def softmax_rows(query, key, allowed):
    scores = right_dot(query, key) * (1.0 / math.sqrt(HEAD_DIM))
    scores = jnp.where(allowed, scores, NEG)
    top = jnp.max(scores, axis=1, keepdims=True)
    raw = jnp.exp(scores - top)
    return raw / jnp.sum(raw, axis=1, keepdims=True)


def pick_block(step, refs, target_ref):
    for k, ref in enumerate(refs):

        @pl.when(step == k)
        def _(ref=ref):
            target_ref[...] = ref[...]


def attention_kernel(place_ref, *refs):
    token_refs, refs = refs[:GROUP], refs[GROUP:]
    gain_ref, offset_ref, bias_ref, pieces_ref, allowed_ref, *refs = refs
    hidden_ref, normed_ref, packed_ref, weight_ref, out_ref, block_ref = refs
    step = pl.program_id(0)
    width = 2 * HEAD_DIM
    own_rows = weight_ref.shape[0] // pieces_ref.shape[0]

    @pl.when(step == 0)
    def _():
        for part in range(3):
            piece = pieces_ref[:, part * own_rows : (part + 1) * own_rows, :]
            weight_ref[:, part * width : (part + 1) * width] = piece.reshape(-1, width)

    pick_block(step, token_refs, block_ref)
    normed, _ = norm_rows(block_ref[...].astype(WIDE))
    hidden = (normed * gain_ref[...] + offset_ref[...]).astype(LOW)
    normed_ref[...] = normed.astype(LOW)
    hidden_ref[...] = hidden
    packed = (plain_dot(hidden, weight_ref[...]) + bias_ref[...]).astype(LOW)
    packed_ref[...] = packed
    key, value = packed[:, width : 2 * width], packed[:, 2 * width :]
    allowed = allowed_ref[0] > 0
    total = None
    for mask in head_masks():
        weights = softmax_rows(packed[:, :width] * mask, key, allowed).astype(LOW)
        term = plain_dot(weights, value * mask)
        total = term if total is None else total + term
    out_ref[...] = total.astype(LOW)


def attention_back_kernel(
    packed_ref,
    grad_ref,
    allowed_ref,
    weight_ref,
    normed_ref,
    out_ref,
    near_ref,
    far_ref,
    norm_sums_ref,
    bias_sums_ref,
):
    masks = head_masks()
    rows = allowed_ref.shape[1]
    width = 2 * HEAD_DIM
    scale = 1.0 / math.sqrt(HEAD_DIM)
    for block in range(allowed_ref.shape[0]):
        part = pl.ds(block * rows, rows)
        query = packed_ref[part, :width]
        key = packed_ref[part, width : 2 * width]
        value = packed_ref[part, 2 * width :]
        grad = grad_ref[part, :]
        allowed = allowed_ref[block] > 0
        sums = [None, None, None]
        for mask in masks:
            query_head = query * mask
            grad_head = grad * mask
            weights = softmax_rows(query_head, key, allowed)
            grad_weights = right_dot(grad_head, value)
            grad_scores = weights * (
                grad_weights - jnp.sum(grad_weights * weights, axis=1, keepdims=True)
            )
            grad_scores = grad_scores.astype(LOW)
            terms = (
                plain_dot(grad_scores, key * mask),
                left_dot(grad_scores, query_head),
                left_dot(weights.astype(LOW), grad_head),
            )
            sums = [t if s is None else s + t for s, t in zip(sums, terms)]
        out_ref[part, :width] = (sums[0] * scale).astype(LOW)
        out_ref[part, width : 2 * width] = (sums[1] * scale).astype(LOW)
        out_ref[part, 2 * width :] = sums[2].astype(LOW)
    grad_hidden = right_dot(out_ref[...], weight_ref[...])
    hidden = grad_hidden.astype(LOW)
    step = pl.program_id(0)
    gain_sums = jnp.sum(grad_hidden * normed_ref[...].astype(WIDE), axis=0, keepdims=True)
    plain_sums = jnp.sum(grad_hidden, axis=0, keepdims=True)
    norm_sums = jnp.concatenate([gain_sums, plain_sums], axis=0)
    bias_sums = jnp.sum(out_ref[...].astype(WIDE), axis=0, keepdims=True)

    @pl.when(step == 0)
    def _():
        norm_sums_ref[...] = norm_sums
        bias_sums_ref[...] = bias_sums

    @pl.when(step > 0)
    def _():
        norm_sums_ref[...] += norm_sums
        bias_sums_ref[...] += bias_sums

    @pl.when(step < pl.num_programs(0) // 2)
    def _():
        near_ref[...] = hidden

    @pl.when(step >= pl.num_programs(0) // 2)
    def _():
        far_ref[...] = hidden


def block_place(i, place_ref):
    return place_ref[0] ^ (((i & 3) << 1) | (i >> 2))


def fixed(shape):
    return pl.BlockSpec(shape, lambda i, p: (0,) * len(shape))


def attention(blocks, gain, offset, bias, pieces, allowed, places):
    rows, model_width = blocks[0].shape
    width = 2 * HEAD_DIM
    count = len(blocks)
    return pl.pallas_call(
        attention_kernel,
        grid_spec=pltpu.PrefetchScalarGridSpec(
            num_scalar_prefetch=1,
            grid=(count,),
            in_specs=[fixed((rows, model_width))] * count
            + [
                fixed((1, model_width)),
                fixed((1, model_width)),
                fixed((1, 3 * width)),
                fixed(pieces.shape),
                pl.BlockSpec((1, rows, rows), lambda i, p: (block_place(i, p), 0, 0)),
            ],
            out_specs=[
                pl.BlockSpec((rows, model_width), lambda i, p: (i, 0)),
                pl.BlockSpec((rows, model_width), lambda i, p: (i, 0)),
                pl.BlockSpec((rows, 3 * width), lambda i, p: (i, 0)),
                fixed((model_width, 3 * width)),
                pl.BlockSpec((rows, width), lambda i, p: (block_place(i, p), 0)),
            ],
            scratch_shapes=[pltpu.VMEM((rows, model_width), LOW)],
        ),
        out_shape=[
            jax.ShapeDtypeStruct((count * rows, model_width), LOW),
            jax.ShapeDtypeStruct((count * rows, model_width), LOW),
            jax.ShapeDtypeStruct((count * rows, 3 * width), LOW),
            jax.ShapeDtypeStruct((model_width, 3 * width), LOW),
            jax.ShapeDtypeStruct((count * rows, width), LOW),
        ],
        compiler_params=pltpu.CompilerParams(vmem_limit_bytes=VMEM_BYTES),
        cost_estimate=pl.CostEstimate(
            flops=8 * count * rows * rows * width,
            bytes_accessed=count * rows * model_width,
            transcendentals=0,
        ),
    )(places, *blocks, gain, offset, bias, pieces, allowed)


def attention_back(packed, grad, allowed, weight, normed, places, earlier):
    blocks, rows, _ = allowed.shape
    width = 2 * HEAD_DIM
    model_width = weight.shape[0]
    half = blocks // 2
    return pl.pallas_call(
        lambda place_ref, a_ref, *refs: attention_back_kernel(*refs),
        grid_spec=pltpu.PrefetchScalarGridSpec(
            num_scalar_prefetch=1,
            grid=(blocks,),
            in_specs=[
                pl.BlockSpec(memory_space=pl.ANY),
                pl.BlockSpec((rows, 3 * width), lambda i, p: (i, 0)),
                pl.BlockSpec((rows, width), lambda i, p: (block_place(i, p), 0)),
                pl.BlockSpec((1, rows, rows), lambda i, p: (block_place(i, p), 0, 0)),
                pl.BlockSpec((model_width, 3 * width), lambda i, p: (0, 0)),
                pl.BlockSpec((rows, model_width), lambda i, p: (i, 0)),
            ],
            out_specs=[
                pl.BlockSpec((rows, 3 * width), lambda i, p: (i, 0)),
                pl.BlockSpec(
                    (rows, model_width), lambda i, p: ((p[0] >> 1) ^ jnp.minimum(i, half - 1), 0)
                ),
                pl.BlockSpec(
                    (rows, model_width),
                    lambda i, p: ((p[0] >> 1) ^ (jnp.maximum(i, half) - half), 0),
                ),
                pl.BlockSpec((2, model_width), lambda i, p: (0, 0)),
                pl.BlockSpec((1, 3 * width), lambda i, p: (0, 0)),
            ],
        ),
        out_shape=[
            jax.ShapeDtypeStruct((blocks * rows, 3 * width), LOW),
            jax.ShapeDtypeStruct((half * rows, model_width), LOW),
            jax.ShapeDtypeStruct((half * rows, model_width), LOW),
            jax.ShapeDtypeStruct((2, model_width), WIDE),
            jax.ShapeDtypeStruct((1, 3 * width), WIDE),
        ],
        compiler_params=pltpu.CompilerParams(vmem_limit_bytes=VMEM_BYTES),
        cost_estimate=pl.CostEstimate(
            flops=20 * blocks * rows * rows * width,
            bytes_accessed=4 * packed.size + 4 * allowed.size,
            transcendentals=2 * allowed.size,
        ),
    )(places, earlier, packed, grad, allowed, weight, normed)


def feed_kernel(place_ref, *refs):
    input_refs, grad_refs, refs = refs[:GROUP], refs[GROUP : 2 * GROUP], refs[2 * GROUP :]
    planes = len(refs) - 11
    up_refs, refs = refs[:planes], refs[planes:]
    down_ref, bias_ref, input_ref, grad_ref, act_ref, pre_ref, sums_ref, near_ref, far_ref = refs[:9]
    up_ref = refs[9]
    step = pl.program_id(0)
    rows = input_ref.shape[0] // 2
    pick_block(step, input_refs[0::2], input_ref.at[pl.ds(0, rows)])
    pick_block(step, input_refs[1::2], input_ref.at[pl.ds(rows, rows)])
    pick_block(step, grad_refs[0::2], grad_ref.at[pl.ds(0, rows)])
    pick_block(step, grad_refs[1::2], grad_ref.at[pl.ds(rows, rows)])

    @pl.when(step == 0)
    def _():
        for k, ref in enumerate(up_refs):
            depth = ref.shape[0] * ref.shape[1]
            source = lax.rem(place_ref[1] + planes - k, planes) * depth
            up_ref[pl.ds(pl.multiple_of(source, depth), depth), :] = ref[...].reshape(depth, -1)

    root, cube = 0.7978845608028654, 0.044715
    pre = plain_dot(input_ref[...], up_ref[...]) + bias_ref[...]
    square = pre * pre
    bend = jnp.tanh(root * (pre + cube * square * pre))
    act_ref[...] = (0.5 * pre * (1.0 + bend)).astype(LOW)
    slope = 0.5 * (1.0 + bend) + 0.5 * pre * (1.0 - bend * bend) * (
        root * (1.0 + 3.0 * cube * square)
    )
    grad_pre = (right_dot(grad_ref[...], down_ref[...]) * slope).astype(LOW)
    pre_ref[...] = grad_pre
    sums = jnp.sum(grad_pre.astype(WIDE), axis=0, keepdims=True)

    @pl.when(step == 0)
    def _():
        sums_ref[...] = sums

    @pl.when(step > 0)
    def _():
        sums_ref[...] += sums

    hidden = right_dot(grad_pre, up_ref[...]).astype(LOW)
    odd = (place_ref[0] >> 1) & 1
    first = pl.ds(pl.multiple_of(odd * rows, rows), rows)
    second = pl.ds(pl.multiple_of((1 - odd) * rows, rows), rows)
    for ref, wanted in (
        (near_ref, step < pl.num_programs(0) // 2),
        (far_ref, step >= pl.num_programs(0) // 2),
    ):

        @pl.when(wanted)
        def _(ref=ref):
            ref[first, :] = hidden[:rows]
            ref[second, :] = hidden[rows:]


def feed_forward(inputs, grads, up_parts, down, bias, places):
    block_rows, width = inputs[0].shape
    hidden = down.shape[0]
    tokens = GROUP * block_rows
    rows = 2 * block_rows
    steps = tokens // rows
    half = steps // 2
    return pl.pallas_call(
        feed_kernel,
        grid_spec=pltpu.PrefetchScalarGridSpec(
            num_scalar_prefetch=1,
            grid=(steps,),
            in_specs=[fixed((block_rows, width))] * (2 * GROUP)
            + [fixed(part.shape) for part in up_parts]
            + [fixed((hidden, width)), fixed((1, hidden))],
            out_specs=[
                pl.BlockSpec((rows, width), lambda i, p: (i, 0)),
                pl.BlockSpec((rows, width), lambda i, p: (i, 0)),
                pl.BlockSpec((rows, hidden), lambda i, p: (i, 0)),
                pl.BlockSpec((rows, hidden), lambda i, p: (i, 0)),
                fixed((1, hidden)),
                pl.BlockSpec((rows, width), lambda i, p: ((p[0] >> 2) ^ jnp.minimum(i, half - 1), 0)),
                pl.BlockSpec(
                    (rows, width), lambda i, p: ((p[0] >> 2) ^ (jnp.maximum(i, half) - half), 0)
                ),
            ],
            scratch_shapes=[pltpu.VMEM((width, hidden), LOW), pltpu.SMEM((1,), jnp.int32)],
        ),
        out_shape=[
            jax.ShapeDtypeStruct((tokens, width), LOW),
            jax.ShapeDtypeStruct((tokens, width), LOW),
            jax.ShapeDtypeStruct((tokens, hidden), LOW),
            jax.ShapeDtypeStruct((tokens, hidden), LOW),
            jax.ShapeDtypeStruct((1, hidden), WIDE),
            jax.ShapeDtypeStruct((tokens // 2, width), LOW),
            jax.ShapeDtypeStruct((tokens // 2, width), LOW),
        ],
        compiler_params=pltpu.CompilerParams(vmem_limit_bytes=VMEM_BYTES),
        cost_estimate=pl.CostEstimate(
            flops=tokens * width * hidden,
            bytes_accessed=tokens * width,
            transcendentals=0,
        ),
    )(places, *inputs, *grads, *up_parts, down, bias)


class Links:
    def __init__(self, count):
        self.count = count
        self.planes = count // GROUP
        index = lax.axis_index("dp")
        self.place = index & (GROUP - 1)
        self.plane = index // GROUP

    def swap(self, array, flip):
        return lax.ppermute(array, "dp", [(i, i ^ flip) for i in range(self.count)])

    def shift(self, array, steps):
        hop = steps * GROUP
        return lax.ppermute(array, "dp", [(i, (i + hop) % self.count) for i in range(self.count)])

    def group_gather(self, block):
        near = [block] + [None] * 3
        for k in (3, 1, 2):
            near[k] = self.swap(block, 2 * k)
        far = [self.swap(b, 1) for b in near]
        return near + far

    def core_sum(self, near, far, order=0.0):
        return (near.astype(WIDE) + (self.swap(far, 1).astype(WIDE) + order)).astype(LOW)

    def chip_sum(self, halves):
        total = halves[0].astype(WIDE)
        for k in (3, 1, 2):
            total = total + self.swap(halves[k], 2 * k).astype(WIDE)
        return total

    def chip_exchange(self, halves):
        chips = GROUP // 2
        groups = [
            [p * GROUP + 2 * m + c for m in range(chips)]
            for p in range(self.planes)
            for c in range(2)
        ]
        parts = halves.reshape(chips, halves.shape[0] // chips, halves.shape[1])
        terms = lax.all_to_all(parts, "dp", 0, 0, axis_index_groups=groups, tiled=True)
        return jnp.sum(terms.astype(WIDE), axis=0)

    def group_lists(self):
        return [[p * GROUP + j for j in range(GROUP)] for p in range(self.planes)]

    def plane_exchange(self, parts):
        return lax.all_to_all(
            parts, "dp", 0, 0, axis_index_groups=self.plane_groups(), tiled=True
        )

    def exchange(self, parts):
        return lax.all_to_all(
            parts, "dp", 0, 0, axis_index_groups=self.group_lists(), tiled=True
        )

    def plane_groups(self):
        return [[p * GROUP + j for p in range(self.planes)] for j in range(GROUP)]

    def plane_gather(self, block):
        if self.planes > DIRECT_PLANES:
            found = lax.all_gather(block, "dp", axis_index_groups=self.plane_groups())
            return [
                lax.dynamic_index_in_dim(found, (self.plane - k) % self.planes, 0, False)
                for k in range(self.planes)
            ]
        return [block] + [self.shift(block, k) for k in range(1, self.planes)]

    def plane_sum(self, chunks):
        if self.planes > DIRECT_PLANES:
            return lax.psum_scatter(
                chunks.astype(WIDE), "dp", axis_index_groups=self.plane_groups()
            )
        total = lax.dynamic_index_in_dim(chunks, self.plane, 0, False).astype(WIDE)
        for k in range(1, self.planes):
            target = (self.plane + k) % self.planes
            term = lax.dynamic_index_in_dim(chunks, target, 0, False)
            total = total + self.shift(term, k).astype(WIDE)
        return total


def order_zero(array):
    return array[(0,) * array.ndim].astype(WIDE) * 0.0


def local(
    tokens,
    segment_ids,
    pad_mask,
    ln1_gain,
    ln1_bias,
    qkv_weight,
    qkv_bias,
    out_weight,
    out_bias,
    ln2_gain,
    ln2_bias,
    up_weight,
    up_bias,
    down_weight,
    down_bias,
    cotangent,
):
    count = lax.axis_size("dp")
    links = Links(count)
    place, planes = links.place, links.planes
    rows, width = tokens.shape
    own_rows = qkv_weight.shape[0]
    hidden = up_weight.shape[1]
    shard = width // GROUP
    hidden_shard = hidden // GROUP
    own_hidden = hidden // count
    heads_width = 3 * shard

    code = (segment_ids * 2 + pad_mask).astype(LOW)
    fill = jnp.zeros((shard - 4 * own_rows,), LOW)
    wide_fill = jnp.zeros((shard - own_hidden,), LOW)
    empty = jnp.zeros((shard,), LOW)
    small = [
        jnp.concatenate([ln1_gain, ln1_bias, out_bias, ln2_gain, fill]),
        jnp.concatenate([ln2_bias, down_bias, qkv_bias, fill]),
        jnp.concatenate([up_bias, wide_fill]),
        code,
    ]
    small = jnp.stack(small + [empty] * 4)
    qkv_parts = qkv_weight.reshape(own_rows, 3, GROUP, shard).transpose(2, 1, 0, 3)
    qkv_parts = qkv_parts.reshape(GROUP, 3 * own_rows, shard)
    small_parts = jnp.broadcast_to(small[None], (GROUP,) + small.shape)
    sent = jnp.concatenate([qkv_parts, small_parts], axis=1)
    sent = jnp.broadcast_to(sent[None], (planes,) + sent.shape).reshape((count,) + sent.shape[1:])
    up_parts = up_weight.reshape(own_rows, planes, GROUP, own_hidden)
    up_parts = up_parts.transpose(2, 0, 1, 3).reshape(GROUP, own_rows, hidden_shard)
    up_plane = links.exchange(up_parts)
    sent = sent + order_zero(up_plane).astype(LOW)
    token_blocks = links.group_gather(tokens)
    grad_out = cotangent.astype(WIDE) * pad_mask.astype(WIDE)[:, None]
    grad_feed_own = grad_out.astype(LOW)
    grad_feed_blocks = links.group_gather(grad_feed_own)
    buffer = lax.all_to_all(sent, "dp", 0, 0, tiled=True)
    out_full = lax.all_gather(out_weight, "dp", axis=0, tiled=True)
    down_full = lax.all_gather(
        down_weight, "dp", axis_index_groups=links.plane_groups(), tiled=True
    )
    def small_vector(row, start, length):
        start = start * own_rows
        return buffer[:, 3 * own_rows + row, start : start + length].astype(WIDE)

    gain_one, bias_one, bias_out, gain_two, bias_two, bias_down = (
        small_vector(i // 4, i % 4, own_rows).reshape(width) for i in range(6)
    )
    qkv_bias_all = small_vector(1, 2, 2 * own_rows).reshape(2, width)
    bias_qv = lax.dynamic_slice_in_dim(qkv_bias_all, place * shard, shard, 1)
    bias_heads = jnp.concatenate([bias_qv[0], jnp.zeros((shard,), WIDE), bias_qv[1]])
    up_bias_all = small_vector(2, 0, own_hidden).reshape(planes, GROUP, own_hidden)
    bias_up = lax.dynamic_index_in_dim(up_bias_all, place, 1, False).reshape(hidden_shard)

    codes = lax.dynamic_slice_in_dim(small_vector(3, 0, rows), links.plane * GROUP, GROUP, 0)
    codes = codes.astype(jnp.int32)
    segments, live = codes >> 1, codes & 1
    positions = jnp.arange(rows, dtype=jnp.int32)
    allowed = (
        (segments[:, :, None] == segments[:, None, :])
        & (positions[None, :] <= positions[:, None])[None]
        & (live[:, None, :] == 1)
    ).astype(WIDE)

    places = jnp.stack([place, links.plane])
    hidden_one, normed_low, packed, qkv_full, mixed_heads = attention(
        token_blocks,
        gain_one[None],
        bias_one[None],
        bias_heads[None],
        buffer,
        allowed,
        places,
    )
    up_blocks = links.plane_gather(up_plane)
    mixed_heads = mixed_heads.reshape(GROUP, rows, shard)
    mixed = links.exchange(mixed_heads)
    mixed = mixed.transpose(1, 0, 2).reshape(rows, width)
    token_rows = tokens.astype(WIDE)
    middle = token_rows + (plain_dot(mixed, out_full) + bias_out)
    normed_two, inverse_two = norm_rows(middle)
    hidden_two_own = (normed_two * gain_two + bias_two).astype(LOW)
    up_here = sum(order_zero(b) for b in up_blocks[1:])
    hidden_two_own = (hidden_two_own.astype(WIDE) + up_here).astype(LOW)
    hidden_two_blocks = links.group_gather(hidden_two_own)

    half_rows = GROUP * rows // 2
    hidden_two, grad_feed, activated_low, grad_pre_low, up_bias_sums, near, far = feed_forward(
        hidden_two_blocks, grad_feed_blocks, up_blocks, down_full, bias_up[None], places
    )
    grad_hidden_half = links.core_sum(near, far)
    grad_hidden_two = links.chip_exchange(grad_hidden_half)
    far = plain_dot(activated_low[half_rows:], down_full).astype(LOW)
    near = plain_dot(activated_low[:half_rows], down_full).astype(LOW)
    feed_near, feed_far = near, far
    grad_middle = grad_out + norm_back(grad_hidden_two, normed_two, inverse_two, gain_two)
    grad_branch = grad_middle.astype(LOW)
    grad_mixed_own = right_dot(grad_branch, out_full).astype(LOW)
    grad_mixed_sent = grad_mixed_own.reshape(rows, GROUP, shard).transpose(1, 0, 2)
    grad_mixed = links.exchange(grad_mixed_sent)
    grad_mixed = grad_mixed.reshape(GROUP * rows, shard)

    feed_half = links.core_sum(feed_near, feed_far, order_zero(grad_mixed_sent))
    block_out = links.chip_sum(feed_half.reshape(4, rows, width))
    block_out = (middle + block_out + bias_down).astype(LOW)

    pieces = [left_dot(hidden_two, grad_pre_low).astype(LOW).reshape(planes, -1, hidden_shard)]
    for start in range(0, width, hidden_shard):
        piece = left_dot(activated_low, grad_feed[:, start : start + hidden_shard]).astype(LOW)
        pieces.append(piece.reshape(planes, own_hidden, hidden_shard))
    both_rows = lax.psum_scatter(
        jnp.concatenate(pieces, axis=1), "dp", axis_index_groups=links.plane_groups()
    )
    up_rows = both_rows[: GROUP * own_rows].reshape(GROUP, own_rows, hidden_shard)
    grad_down_w = both_rows[GROUP * own_rows :].reshape(-1, own_hidden, hidden_shard)
    grad_down_w = grad_down_w.transpose(1, 0, 2).reshape(own_hidden, width).astype(WIDE)

    grad_packed, near, far, norm_sums, packed_sums = attention_back(
        packed, grad_mixed, allowed, qkv_full, normed_low, places, block_out
    )
    proj_rows = left_dot(hidden_one, grad_packed).astype(LOW)
    proj_rows = proj_rows.reshape(planes, GROUP, own_rows, heads_width)
    proj_sum = links.plane_sum(proj_rows)
    grad_hidden_half = links.core_sum(near, far)
    grad_hidden_one = links.chip_exchange(grad_hidden_half)
    out_parts = left_dot(mixed, grad_branch).astype(LOW)
    out_parts = out_parts.reshape(planes, GROUP, own_rows, width)
    out_near, out_far = (
        jnp.stack(
            [lax.dynamic_index_in_dim(out_parts, place ^ r, 1, False) for r in order]
        ).reshape(4, planes * own_rows, width)
        for order in ((0, 2, 4, 6), (1, 3, 5, 7))
    )
    out_half = links.core_sum(out_near, out_far, order_zero(proj_sum))
    out_sum = links.chip_sum(out_half).astype(LOW)

    normed_one, inverse_one = norm_rows(token_rows)
    grad_inputs = grad_middle + norm_back(grad_hidden_one, normed_one, inverse_one, gain_one)

    proj_sums = jnp.zeros((2, width), WIDE)
    proj_sums = lax.dynamic_update_slice_in_dim(
        proj_sums,
        jnp.concatenate([packed_sums[:, :shard], packed_sums[:, 2 * shard :]], axis=0),
        place * shard,
        1,
    )
    up_sums = jnp.zeros((planes, GROUP, own_hidden), WIDE)
    up_sums = lax.dynamic_update_index_in_dim(
        up_sums, up_bias_sums.reshape(planes, own_hidden), place, 1
    )
    vectors = [
        norm_sums[0],
        norm_sums[1],
        jnp.sum(grad_branch.astype(WIDE), axis=0),
        jnp.sum(grad_hidden_two * normed_two, axis=0),
        jnp.sum(grad_hidden_two, axis=0),
        jnp.sum(grad_feed_own.astype(WIDE), axis=0),
        proj_sums,
        up_sums,
    ]
    vectors = jnp.concatenate([v.reshape(planes, GROUP, -1) for v in vectors], axis=2)
    grad_out_w = links.plane_sum(out_sum.reshape(planes, own_rows, width))
    vectors = vectors.reshape(count, -1) + order_zero(grad_hidden_one)
    sums = jnp.sum(lax.all_to_all(vectors, "dp", 0, 0, tiled=True), axis=0)
    proj_rows = (proj_sum + order_zero(sums)).astype(LOW)
    row_blocks = links.exchange(jnp.concatenate([proj_rows, up_rows], axis=2))
    row_blocks = row_blocks.astype(WIDE)
    grad_proj_w = row_blocks[:, :, :heads_width]
    grad_proj_w = grad_proj_w.reshape(GROUP, own_rows, 3, shard).transpose(1, 2, 0, 3)
    grad_proj_w = grad_proj_w.reshape(own_rows, 3 * width)
    grad_up_w = row_blocks[:, :, heads_width:]
    grad_up_w = grad_up_w.reshape(GROUP, own_rows, planes, own_hidden).transpose(1, 2, 0, 3)
    grad_up_w = grad_up_w.reshape(own_rows, hidden)

    grads = [sums[i * own_rows : (i + 1) * own_rows] for i in range(6)]
    grad_proj_b = sums[6 * own_rows : 8 * own_rows]
    grad_up_b = sums[8 * own_rows :]
    return (
        block_out,
        grad_inputs,
        grads[0],
        grads[1],
        grad_proj_w,
        grad_proj_b,
        grad_out_w,
        grads[2],
        grads[3],
        grads[4],
        grad_up_w,
        grad_up_b,
        grad_down_w,
        grads[5],
    )


def solution(mesh):
    flat, wide = P("dp"), P("dp", None)
    in_specs = (
        (wide, flat, flat, flat, flat, wide, flat, wide, flat, flat, flat, wide, flat, wide)
        + (flat, wide)
    )
    out_specs = (
        (wide, wide, flat, flat, wide, flat, wide, flat, flat, flat, wide, flat, wide, flat)
    )
    return jax.shard_map(local, mesh=mesh, in_specs=in_specs, out_specs=out_specs, check_vma=False)
```

time: 302 us -> 274 us (0.907)
  matrix products: 44 us -> 17 us
  Pallas kernels: 14.8 us -> 35.7 us
  local copies, waits for them, and re-layouts: 38.4 us -> 29.6 us
  starting transfers between devices: 73.4 us -> 65.8 us
  other arithmetic: 28.9 us -> 22.2 us
  between operations: 14.9 us -> 20.1 us
  waiting for transfers between devices: 85.8 us -> 81.5 us
    dot_general x16 -> x9, matrix products: 44 us -> 17 us  [dot(): lax.dot_general(first, second, (dims, ((), ())), preferred_element_type=j...]
    pallas_call x2 -> x3, Pallas kernels: 14.8 us -> 35.7 us  [the longest x1 12.1 us: attention_back(): pl.pallas_call(lambda place_ref, a_ref, *refs: attention_back_kernel(*ref...]
    all_to_all x1 -> x2, waiting for transfers between devices: 0.01 us -> 13.5 us  [chip_exchange(): lax.all_to_all(parts, 'dp', 0, 0, axis_index_groups=groups, tiled=True)]
    all_to_all x4, waiting for transfers between devices: 18.2 us -> 7.23 us  [exchange(): lax.all_to_all(parts, 'dp', 0, 0, axis_index_groups=self.group_lists(), t...]
    ppermute x6 -> x9, waiting for transfers between devices: 18.1 us -> 8.22 us  [shift(): lax.ppermute(array, 'dp', [(i, (i + hop) % self.count) for i in range(sel...]
    ppermute x25 -> x31, waiting for transfers between devices: 35.7 us -> 42 us  [swap(): return lax.ppermute(array, 'dp', [(i, i ^ flip) for i in range(self.count)])]
    ppermute x6 -> x9, starting transfers between devices: 18.2 us -> 13.3 us  [shift(): lax.ppermute(array, 'dp', [(i, (i + hop) % self.count) for i in range(sel...]
    unnamed x109 -> x112, local copies, waits for them, and re-layouts: 11 us -> 6.47 us
  transfers between devices with their start and end apart: 41 -> 51, of which waited for: 19 -> 19; matrix products, arithmetic and copies ran while one was open for 29% -> 22% of each run, Pallas kernels for 5% -> 9%
where the time goes in v1:
time: 274 us; the launch traced here: 272 us
  waiting for transfers between devices  81.5 us (30%)
  starting transfers between devices  65.8 us (24%)
  Pallas kernels  35.7 us (13%)
  local copies, waits for them, and re-layouts  29.6 us (11%)
  other arithmetic  22.2 us (8%)
  between operations  20.1 us (7%)
  matrix products  17 us (6%)
    ppermute x31, waiting for transfers between devices, swap(): return lax.ppermute(array, 'dp', [(i, i ^ flip) for i in range(self.count)])  42 us
    ppermute x31, starting transfers between devices, swap(): return lax.ppermute(array, 'dp', [(i, i ^ flip) for i in range(self.count)])  21.4 us
    dot_general x9, matrix products, dot(): lax.dot_general(first, second, (dims, ((), ())), preferred_element_type=j...  17 us
    all_to_all x4, starting transfers between devices, exchange(): lax.all_to_all(parts, 'dp', 0, 0, axis_index_groups=self.group_lists(), t...  15.7 us
    all_to_all x2, waiting for transfers between devices, chip_exchange(): lax.all_to_all(parts, 'dp', 0, 0, axis_index_groups=groups, tiled=True)  13.5 us
    ppermute x9, starting transfers between devices, shift(): lax.ppermute(array, 'dp', [(i, (i + hop) % self.count) for i in range(sel...  13.3 us
    pallas_call x1, Pallas kernels, attention_back(): pl.pallas_call(lambda place_ref, a_ref, *refs: attention_back_kernel(*ref...  12.1 us
    pallas_call x1, Pallas kernels, attention(): pl.pallas_call(attention_kernel, grid_spec=pltpu.PrefetchScalarGridSpec(n...  11.9 us
  transfers between devices with their start and end apart: 51, of which 19 were waited for; matrix products, arithmetic and copies ran while one was open for 22% of the time, Pallas kernels for 9%

profile of v1, /device:TPU:0, one launch (start us, length us, event | category | flops | bytes accessed | tf_op | source)
XLA Modules:
  0.0 272.0 jit_solution(10442915008022449418)
XLA Ops:
  9.9 5.2 %all-to-all-start = ((bf16[8,32,512]{2,1,0:T(8,128)(2,1)}), bf16[8,32,512]{2,1,0:T(8,128)(2,1)S(1)}, u32[]{:S(2)}, u32[]{:S(2)}) async-start(bf16[8,32,512]{2,1,0:T(8,128)(2,1)} %reshape.444), calls=%async_computation | async-start | bytes 524288 | tf_op jit(solution)/shard_map/all_to_all | solution.py:432
  15.4 6.6 %all-to-all-done.refs_16_ = bf16[8,32,512]{2,1,0:T(8,128)(2,1)S(1)} async-done(((bf16[8,32,512]{2,1,0:T(8,128)(2,1)}), bf16[8,32,512]{2,1,0:T(8,128)(2,1)S(1)}, u32[]{:S(2)}, u32[]{:S(2)}) %all-to-all-start) | async-done | bytes 262176 | tf_op jit(solution)/shard_map/all_to_all | solution.py:432
  24.4 4.0 %all-to-all-start.1 = ((bf16[32,104,128]{2,1,0:T(8,128)(2,1)}), bf16[32,104,128]{2,1,0:T(8,128)(2,1)S(1)}, u32[]{:S(2)}, u32[]{:S(2)}) async-start(bf16[32,104,128]{2,1,0:T(8,128)(2,1)} %bitcast.10), calls=%async_computation.1 | async-start | bytes 1703936 | tf_op jit(solution)/shard_map/all_to_all | solution.py:518
  28.4 2.7 %collective-permute-start.2 = (bf16[128,1024]{1,0:T(8,128)(2,1)S(1)}, bf16[128,1024]{1,0:T(8,128)(2,1)S(1)}, u32[]{:S(2)}, u32[]{:S(2)}) collective-permute-start(bf16[128,1024]{1,0:T(8,128)(2,1)S(1)} %copy-done), channel_id=1, source_target_pairs={{0,6},{1,7},{2,4},{3,5},{4,2},{5,3},{6,0},{7,1},{8,14},{9,15},{10,... | collective-permute-start | bytes 786440 | tf_op jit(solution)/shard_map/ppermute | solution.py:390
  32.1 2.7 %collective-permute-start.19 = (bf16[128,1024]{1,0:T(8,128)(2,1)S(1)}, bf16[128,1024]{1,0:T(8,128)(2,1)S(1)}, u32[]{:S(2)}, u32[]{:S(2)}) collective-permute-start(bf16[128,1024]{1,0:T(8,128)(2,1)S(1)} %get-tuple-element.66.refs_8_), channel_id=1, source_target_pairs={{0,6},{1,7},{2,4},{3,5},{4,2},{5,3},{6,0},{7,1},{8,14},{9,15},{10,... | collective-permute-start | bytes 786440 | tf_op jit(solution)/shard_map/ppermute | solution.py:390
  35.4 12.5 %collective-permute-done.2.refs_3_ = bf16[128,1024]{1,0:T(8,128)(2,1)S(1)} collective-permute-done((bf16[128,1024]{1,0:T(8,128)(2,1)S(1)}, bf16[128,1024]{1,0:T(8,128)(2,1)S(1)}, u32[]{:S(2)}, u32[]{:S(2)}) %collective-permute-start.2) | collective-permute-done | bytes 262176 | tf_op jit(solution)/shard_map/ppermute | solution.py:390
  47.9 4.8 %collective-permute-done.1.refs_2_ = bf16[128,1024]{1,0:T(8,128)(2,1)S(1)} collective-permute-done((bf16[128,1024]{1,0:T(8,128)(2,1)S(1)}, bf16[128,1024]{1,0:T(8,128)(2,1)S(1)}, u32[]{:S(2)}, u32[]{:S(2)}) %collective-permute-start.1) | collective-permute-done | bytes 262176 | tf_op jit(solution)/shard_map/ppermute | solution.py:390
  56.8 1.6 collective-permute-start.18
  58.5 3.7 %collective-permute-start.9 = (bf16[8,32,512]{2,1,0:T(8,128)(2,1)S(1)}, bf16[8,32,512]{2,1,0:T(8,128)(2,1)S(1)}, u32[]{:S(2)}, u32[]{:S(2)}) collective-permute-start(bf16[8,32,512]{2,1,0:T(8,128)(2,1)S(1)} %all-to-all-done.refs_16_), channel_id=1, source_target_pairs={{0,24},{1,25},{2,26},{3,27},{4,28},{5,29},{6,30},{7,31},{8,0},{9,1... | collective-permute-start | bytes 786440 | tf_op jit(solution)/shard_map/ppermute | solution.py:394
  62.1 1.7 collective-permute-start.7
  67.2 11.9 %shard_map.263 = (bf16[1024,1024]{1,0:T(8,128)(2,1)}, bf16[1024,1024]{1,0:T(8,128)(2,1)}, bf16[1024,384]{1,0:T(8,128)(2,1)}, bf16[1024,384]{1,0:T(8,128)(2,1)}, bf16[1024,128]{1,0:T(8,128)(2,1)}) custom-call(s32[2]{0:T(128)} %pad_add_fusion.place_ref, bf16[128,1024]{1,0:T(8,128)(2,1)} %refs_0_.1, bf16[128,1024]{1,0:T(8,128)(2,1)} %copy-done.25, ...), custom_call_target="tpu_custom_call" | custom-call | flops 134217728 | bytes 1048576 | tf_op jit(solution)/shard_map/pallas_call | solution.py:195
  79.1 1.8 copy.54
  80.9 3.4 %all-to-all-start.2 = ((bf16[8,128,128]{1,2,0:T(8,128)(2,1)}), bf16[8,128,128]{1,2,0:T(8,128)(2,1)S(1)}, u32[]{:S(2)}, u32[]{:S(2)}) async-start(bf16[8,128,128]{1,2,0:T(8,128)(2,1)} %copy.54), calls=%async_computation.2 | async-start | bytes 524288 | tf_op jit(solution)/shard_map/all_to_all | solution.py:432
  85.1 5.9 %collective-permute-done.8.refs_18_ = bf16[8,32,512]{2,1,0:T(8,128)(2,1)S(1)} collective-permute-done((bf16[8,32,512]{2,1,0:T(8,128)(2,1)S(1)}, bf16[8,32,512]{2,1,0:T(8,128)(2,1)S(1)}, u32[]{:S(2)}, u32[]{:S(2)}) %collective-permute-start.8) | collective-permute-done | bytes 262176 | tf_op jit(solution)/shard_map/ppermute | solution.py:394
  95.8 2.2 fusion.41
  98.5 1.5 collective-permute-start.12
  100.0 1.6 collective-permute-start.11
  102.6 6.2 %collective-permute-done.12.refs_3_ = bf16[128,1024]{1,0:T(8,128)(2,1)} collective-permute-done((bf16[128,1024]{1,0:T(8,128)(2,1)S(1)}, bf16[128,1024]{1,0:T(8,128)(2,1)}, u32[]{:S(2)}, u32[]{:S(2)}) %collective-permute-start.12) | collective-permute-done | bytes 262176 | tf_op jit(solution)/shard_map/ppermute | solution.py:390
  108.7 4.7 %collective-permute-done.11.refs_2_ = bf16[128,1024]{1,0:T(8,128)(2,1)S(1)} collective-permute-done((bf16[128,1024]{1,0:T(8,128)(2,1)S(1)}, bf16[128,1024]{1,0:T(8,128)(2,1)S(1)}, u32[]{:S(2)}, u32[]{:S(2)}) %collective-permute-start.11) | collective-permute-done | bytes 262176 | tf_op jit(solution)/shard_map/ppermute | solution.py:390
  116.5 11.6 %shard_map.264 = (bf16[1024,1024]{1,0:T(8,128)(2,1)}, bf16[1024,1024]{1,0:T(8,128)(2,1)}, bf16[1024,512]{1,0:T(8,128)(2,1)}, bf16[1024,512]{1,0:T(8,128)(2,1)}, ...) custom-call(s32[2]{0:T(128)} %pad_add_fusion.place_ref, bf16[128,1024]{1,0:T(8,128)(2,1)} %copy-done.12, ...), custom_call_target="tpu_custom_call" | custom-call | flops 536870912 | bytes 1048576 | tf_op jit(solution)/shard_map/pallas_call | solution.py:342
  128.7 3.1 %convolution_convert_fusion.5 = bf16[512,512]{1,0:T(8,128)(2,1)} fusion(bf16[1024,512]{1,0:T(8,128)(2,1)} %get-tuple-element.32, bf16[1024,1024]{1,0:T(8,128)(2,1)} %get-tuple-element.47), kind=kOutput, calls=%fused_computation.13 | convolution fusion | flops 537133056 | bytes 2621440 | tf_op jit(solution)/shard_map/dot_general | solution.py:47
  131.8 1.4 add_convert_fusion.3
  133.3 4.4 %all-to-all-start.3 = ((bf16[4,128,1024]{2,1,0:T(8,128)(2,1)}), bf16[4,128,1024]{2,1,0:T(8,128)(2,1)}, u32[]{:S(2)}, u32[]{:S(2)}) async-start(bf16[4,128,1024]{2,1,0:T(8,128)(2,1)} %bitcast.20), calls=%async_computation.3 | async-start | bytes 2097152 | tf_op jit(solution)/shard_map/all_to_all | solution.py:420
  137.9 1.7 convolution_convert_fusion.2
  140.1 1.7 convolution_convert_fusion.3
  141.8 2.2 convolution_convert_fusion.1
  144.0 8.3 %all-to-all-done.3 = bf16[4,128,1024]{2,1,0:T(8,128)(2,1)} async-done(((bf16[4,128,1024]{2,1,0:T(8,128)(2,1)}), bf16[4,128,1024]{2,1,0:T(8,128)(2,1)}, u32[]{:S(2)}, u32[]{:S(2)}) %all-to-all-start.3) | async-done | bytes 1048608 | tf_op jit(solution)/shard_map/all_to_all | solution.py:420
  152.3 1.7 convert_reduce_fusion
  154.6 1.5 convolution_convert_fusion.7
  160.0 2.1 add_convert_fusion.2
  164.4 1.5 collective-permute-start.28
  167.2 1.5 pad_maximum_fusion
  168.8 3.4 %all-to-all-start.4 = ((bf16[8,128,128]{2,1,0:T(8,128)(2,1)}), bf16[8,128,128]{2,1,0:T(8,128)(2,1)S(1)}, u32[]{:S(2)}, u32[]{:S(2)}) async-start(bf16[8,128,128]{2,1,0:T(8,128)(2,1)} %bitcast.22), calls=%async_computation.4 | async-start | bytes 524288 | tf_op jit(solution)/shard_map/all_to_all | solution.py:432
  173.3 4.7 %collective-permute-done.28 = bf16[128,1024]{1,0:T(8,128)(2,1)S(1)} collective-permute-done((bf16[128,1024]{1,0:T(8,128)(2,1)}, bf16[128,1024]{1,0:T(8,128)(2,1)S(1)}, u32[]{:S(2)}, u32[]{:S(2)}) %collective-permute-start.28) | collective-permute-done | bytes 262176 | tf_op jit(solution)/shard_map/ppermute | solution.py:390
  181.2 12.1 %shard_map.265 = (bf16[1024,384]{1,0:T(8,128)(2,1)}, bf16[512,1024]{1,0:T(8,128)(2,1)}, bf16[512,1024]{1,0:T(8,128)(2,1)}, f32[2,1024]{1,0:T(2,128)}, f32[1,384]{1,0:T(1,128)}) custom-call(s32[2]{0:T(128)} %pad_add_fusion.place_ref, bf16[128,1024]{1,0:T(8,128)(2,1)} %add_convert_fusion.4.a_ref, bf16[1024,384]{1,0:T(8,128)(2,1)} %get-tuple-element.35.refs_0_, ...), custom_call_target="tpu_custom_call" | custom-call | flops 335544320 | bytes 2097152 | tf_op jit(solution)/shard_map/pallas_call | solution.py:238
  198.7 3.5 %all-to-all-start.5 = ((bf16[4,128,1024]{2,1,0:T(8,128)(2,1)}), bf16[4,128,1024]{2,1,0:T(8,128)(2,1)S(1)}, u32[]{:S(2)}, u32[]{:S(2)}) async-start(bf16[4,128,1024]{2,1,0:T(8,128)(2,1)} %bitcast.25), calls=%async_computation.5 | async-start | bytes 2097152 | tf_op jit(solution)/shard_map/all_to_all | solution.py:420
  202.5 3.1 %convolution_convert_fusion.4 = bf16[1024,384]{1,0:T(8,128)(2,1)S(1)} fusion(bf16[1024,1024]{1,0:T(8,128)(2,1)} %get-tuple-element.43, bf16[1024,384]{1,0:T(8,128)(2,1)} %get-tuple-element.44), kind=kOutput, calls=%fused_computation.12 | convolution fusion | flops 805699584 | bytes 3670016 | tf_op jit(solution)/shard_map/dot_general | solution.py:47
  207.3 1.6 collective-permute-start.30
  208.9 2.2 collective-permute-start.32
  211.5 5.2 %all-to-all-done.5 = bf16[4,128,1024]{2,1,0:T(8,128)(2,1)S(1)} async-done(((bf16[4,128,1024]{2,1,0:T(8,128)(2,1)}), bf16[4,128,1024]{2,1,0:T(8,128)(2,1)S(1)}, u32[]{:S(2)}, u32[]{:S(2)}) %all-to-all-start.5) | async-done | bytes 1048608 | tf_op jit(solution)/shard_map/all_to_all | solution.py:420
  218.7 3.3 %all-to-all-start.6 = ((f32[32,1,384]{2,1,0:T(1,128)}), f32[32,1,384]{2,1,0:T(1,128)S(1)}, u32[]{:S(2)}, u32[]{:S(2)}) async-start(f32[32,1,384]{2,1,0:T(1,128)} %copy.59), calls=%async_computation.6 | async-start | bytes 98304 | tf_op jit(solution)/shard_map/all_to_all | solution.py:645
  223.3 8.8 %all-to-all-done.6 = f32[32,1,384]{2,1,0:T(1,128)S(1)} async-done(((f32[32,1,384]{2,1,0:T(1,128)}), f32[32,1,384]{2,1,0:T(1,128)S(1)}, u32[]{:S(2)}, u32[]{:S(2)}) %all-to-all-start.6) | async-done | bytes 49184 | tf_op jit(solution)/shard_map/all_to_all | solution.py:645
  235.9 1.7 add_convert_fusion
  239.7 1.5 collective-permute-start.35
  243.1 3.7 %all-to-all-start.7 = ((bf16[8,32,896]{2,1,0:T(8,128)(2,1)}), bf16[8,32,896]{2,1,0:T(8,128)(2,1)S(1)}, u32[]{:S(2)}, u32[]{:S(2)}) async-start(bf16[8,32,896]{2,1,0:T(8,128)(2,1)} %pad_maximum_fusion.2), calls=%async_computation.8 | async-start | bytes 917504 | tf_op jit(solution)/shard_map/all_to_all | solution.py:432
  247.8 4.5 %collective-permute-done.36 = bf16[128,1024]{1,0:T(8,128)(2,1)S(1)} collective-permute-done((bf16[128,1024]{1,0:T(8,128)(2,1)S(1)}, bf16[128,1024]{1,0:T(8,128)(2,1)S(1)}, u32[]{:S(2)}, u32[]{:S(2)}) %collective-permute-start.36) | collective-permute-done | bytes 262176 | tf_op jit(solution)/shard_map/ppermute | solution.py:390
  253.4 3.2 %collective-permute-start.39 = (bf16[32,1024]{1,0:T(8,128)(2,1)S(1)}, bf16[32,1024]{1,0:T(8,128)(2,1)S(1)}, u32[]{:S(2)}, u32[]{:S(2)}) collective-permute-start(bf16[32,1024]{1,0:T(8,128)(2,1)S(1)} %get-tuple-element.91), channel_id=1, source_target_pairs={{0,24},{1,25},{2,26},{3,27},{4,28},{5,29},{6,30},{7,31},{8,0},{9,1... | collective-permute-start | bytes 196616 | tf_op jit(solution)/shard_map/ppermute | solution.py:394
  259.5 2.3 collective-permute-done.38
  (288 shorter events, 59.3 us)
Async XLA Ops:
  7.3 88.5 %all-gather.3.cloned.1.call-start = ((), (), s32[]{:S(2)}) async-start(), calls=%async_computation.9 | async-start | bytes 2162688 | tf_op jit(solution)/shard_map/all_gather | solution.py:519
  9.9 12.1 %all-to-all-start = ((bf16[8,32,512]{2,1,0:T(8,128)(2,1)}), bf16[8,32,512]{2,1,0:T(8,128)(2,1)S(1)}, u32[]{:S(2)}, u32[]{:S(2)}) async-start(bf16[8,32,512]{2,1,0:T(8,128)(2,1)} %reshape.444), calls=%async_computation | async-start | bytes 524288 | tf_op jit(solution)/shard_map/all_to_all | solution.py:432
  24.4 29.5 %all-to-all-start.1 = ((bf16[32,104,128]{2,1,0:T(8,128)(2,1)}), bf16[32,104,128]{2,1,0:T(8,128)(2,1)S(1)}, u32[]{:S(2)}, u32[]{:S(2)}) async-start(bf16[32,104,128]{2,1,0:T(8,128)(2,1)} %bitcast.10), calls=%async_computation.1 | async-start | bytes 1703936 | tf_op jit(solution)/shard_map/all_to_all | solution.py:518
  28.4 19.6 %collective-permute-start.2 = (bf16[128,1024]{1,0:T(8,128)(2,1)S(1)}, bf16[128,1024]{1,0:T(8,128)(2,1)S(1)}, u32[]{:S(2)}, u32[]{:S(2)}) collective-permute-start(bf16[128,1024]{1,0:T(8,128)(2,1)S(1)} %copy-done), channel_id=1, source_target_pairs={{0,6},{1,7},{2,4},{3,5},{4,2},{5,3},{6,0},{7,1},{8,14},{9,15},{10,... | collective-permute-start | bytes 786440 | tf_op jit(solution)/shard_map/ppermute | solution.py:390
  31.1 21.6 %collective-permute-start.1 = (bf16[128,1024]{1,0:T(8,128)(2,1)S(1)}, bf16[128,1024]{1,0:T(8,128)(2,1)S(1)}, u32[]{:S(2)}, u32[]{:S(2)}) collective-permute-start(bf16[128,1024]{1,0:T(8,128)(2,1)S(1)} %copy-done), channel_id=1, source_target_pairs={{0,4},{1,5},{2,6},{3,7},{4,0},{5,1},{6,2},{7,3},{8,12},{9,13},{10,... | collective-permute-start | bytes 786440 | tf_op jit(solution)/shard_map/ppermute | solution.py:390
  31.7 22.3 %collective-permute-start = (bf16[128,1024]{1,0:T(8,128)(2,1)S(1)}, bf16[128,1024]{1,0:T(8,128)(2,1)S(1)}, u32[]{:S(2)}, u32[]{:S(2)}) collective-permute-start(bf16[128,1024]{1,0:T(8,128)(2,1)S(1)} %copy-done), channel_id=1, source_target_pairs={{0,2},{1,3},{2,0},{3,1},{4,6},{5,7},{6,4},{7,5},{8,10},{9,11},{10,... | collective-permute-start | bytes 786440 | tf_op jit(solution)/shard_map/ppermute | solution.py:390
  31.9 24.9 %collective-permute-start.3 = (bf16[128,1024]{1,0:T(8,128)(2,1)S(1)}, bf16[128,1024]{1,0:T(8,128)(2,1)}, u32[]{:S(2)}, u32[]{:S(2)}) collective-permute-start(bf16[128,1024]{1,0:T(8,128)(2,1)S(1)} %copy-done), channel_id=1, source_target_pairs={{0,1},{1,0},{2,3},{3,2},{4,5},{5,4},{6,7},{7,6},{8,9},{9,8},{10,11... | collective-permute-start | bytes 786440 | tf_op jit(solution)/shard_map/ppermute | solution.py:390
  32.1 59.5 %collective-permute-start.19 = (bf16[128,1024]{1,0:T(8,128)(2,1)S(1)}, bf16[128,1024]{1,0:T(8,128)(2,1)S(1)}, u32[]{:S(2)}, u32[]{:S(2)}) collective-permute-start(bf16[128,1024]{1,0:T(8,128)(2,1)S(1)} %get-tuple-element.66.refs_8_), channel_id=1, source_target_pairs={{0,6},{1,7},{2,4},{3,5},{4,2},{5,3},{6,0},{7,1},{8,14},{9,15},{10,... | collective-permute-start | bytes 786440 | tf_op jit(solution)/shard_map/ppermute | solution.py:390
  47.9 10.5 %collective-permute-start.6 = (bf16[128,1024]{1,0:T(8,128)(2,1)S(1)}, bf16[128,1024]{1,0:T(8,128)(2,1)}, u32[]{:S(2)}, u32[]{:S(2)}) collective-permute-start(bf16[128,1024]{1,0:T(8,128)(2,1)S(1)} %collective-permute-done.2.refs_3_), channel_id=1, source_target_pairs={{0,1},{1,0},{2,3},{3,2},{4,5},{5,4},{6,7},{7,6},{8,9},{9,8},{10,11... | collective-permute-start | bytes 786440 | tf_op jit(solution)/shard_map/ppermute | solution.py:390
  52.7 9.4 %collective-permute-start.5 = (bf16[128,1024]{1,0:T(8,128)(2,1)S(1)}, bf16[128,1024]{1,0:T(8,128)(2,1)}, u32[]{:S(2)}, u32[]{:S(2)}) collective-permute-start(bf16[128,1024]{1,0:T(8,128)(2,1)S(1)} %collective-permute-done.1.refs_2_), channel_id=1, source_target_pairs={{0,1},{1,0},{2,3},{3,2},{4,5},{5,4},{6,7},{7,6},{8,9},{9,8},{10,11... | collective-permute-start | bytes 786440 | tf_op jit(solution)/shard_map/ppermute | solution.py:390
  53.9 8.2 %collective-permute-start.4 = (bf16[128,1024]{1,0:T(8,128)(2,1)S(1)}, bf16[128,1024]{1,0:T(8,128)(2,1)}, u32[]{:S(2)}, u32[]{:S(2)}) collective-permute-start(bf16[128,1024]{1,0:T(8,128)(2,1)S(1)} %collective-permute-done.refs_1_), channel_id=1, source_target_pairs={{0,1},{1,0},{2,3},{3,2},{4,5},{5,4},{6,7},{7,6},{8,9},{9,8},{10,11... | collective-permute-start | bytes 786440 | tf_op jit(solution)/shard_map/ppermute | solution.py:390
  56.8 35.1 %collective-permute-start.18 = (bf16[128,1024]{1,0:T(8,128)(2,1)S(1)}, bf16[128,1024]{1,0:T(8,128)(2,1)S(1)}, u32[]{:S(2)}, u32[]{:S(2)}) collective-permute-start(bf16[128,1024]{1,0:T(8,128)(2,1)S(1)} %get-tuple-element.66.refs_8_), channel_id=1, source_target_pairs={{0,4},{1,5},{2,6},{3,7},{4,0},{5,1},{6,2},{7,3},{8,12},{9,13},{10,... | collective-permute-start | bytes 786440 | tf_op jit(solution)/shard_map/ppermute | solution.py:390
  58.5 35.8 %collective-permute-start.9 = (bf16[8,32,512]{2,1,0:T(8,128)(2,1)S(1)}, bf16[8,32,512]{2,1,0:T(8,128)(2,1)S(1)}, u32[]{:S(2)}, u32[]{:S(2)}) collective-permute-start(bf16[8,32,512]{2,1,0:T(8,128)(2,1)S(1)} %all-to-all-done.refs_16_), channel_id=1, source_target_pairs={{0,24},{1,25},{2,26},{3,27},{4,28},{5,29},{6,30},{7,31},{8,0},{9,1... | collective-permute-start | bytes 786440 | tf_op jit(solution)/shard_map/ppermute | solution.py:394
  62.1 28.9 %collective-permute-start.8 = (bf16[8,32,512]{2,1,0:T(8,128)(2,1)S(1)}, bf16[8,32,512]{2,1,0:T(8,128)(2,1)S(1)}, u32[]{:S(2)}, u32[]{:S(2)}) collective-permute-start(bf16[8,32,512]{2,1,0:T(8,128)(2,1)S(1)} %all-to-all-done.refs_16_), channel_id=1, source_target_pairs={{0,16},{1,17},{2,18},{3,19},{4,20},{5,21},{6,22},{7,23},{8,24},{9,... | collective-permute-start | bytes 786440 | tf_op jit(solution)/shard_map/ppermute | solution.py:394
  62.1 30.0 %collective-permute-start.7 = (bf16[8,32,512]{2,1,0:T(8,128)(2,1)S(1)}, bf16[8,32,512]{2,1,0:T(8,128)(2,1)S(1)}, u32[]{:S(2)}, u32[]{:S(2)}) collective-permute-start(bf16[8,32,512]{2,1,0:T(8,128)(2,1)S(1)} %all-to-all-done.refs_16_), channel_id=1, source_target_pairs={{0,8},{1,9},{2,10},{3,11},{4,12},{5,13},{6,14},{7,15},{8,16},{9,17... | collective-permute-start | bytes 786440 | tf_op jit(solution)/shard_map/ppermute | solution.py:394
  80.9 14.8 %all-to-all-start.2 = ((bf16[8,128,128]{1,2,0:T(8,128)(2,1)}), bf16[8,128,128]{1,2,0:T(8,128)(2,1)S(1)}, u32[]{:S(2)}, u32[]{:S(2)}) async-start(bf16[8,128,128]{1,2,0:T(8,128)(2,1)} %copy.54), calls=%async_computation.2 | async-start | bytes 524288 | tf_op jit(solution)/shard_map/all_to_all | solution.py:432
  84.4 31.3 %all-gather.5.cloned.1.call-start = ((), (), s32[]{:S(2)}) async-start(), calls=%async_computation.10 | async-start | bytes 1310720 | tf_op jit(solution)/shard_map/all_gather | solution.py:520
  91.0 9.0 %collective-permute-start.20 = (bf16[128,1024]{1,0:T(8,128)(2,1)S(1)}, bf16[128,1024]{1,0:T(8,128)(2,1)S(1)}, u32[]{:S(2)}, u32[]{:S(2)}) collective-permute-start(bf16[128,1024]{1,0:T(8,128)(2,1)S(1)} %get-tuple-element.66.refs_8_), channel_id=1, source_target_pairs={{0,1},{1,0},{2,3},{3,2},{4,5},{5,4},{6,7},{7,6},{8,9},{9,8},{10,11... | collective-permute-start | bytes 786440 | tf_op jit(solution)/shard_map/ppermute | solution.py:390
  91.6 10.1 %collective-permute-start.17 = (bf16[128,1024]{1,0:T(8,128)(2,1)S(1)}, bf16[128,1024]{1,0:T(8,128)(2,1)S(1)}, u32[]{:S(2)}, u32[]{:S(2)}) collective-permute-start(bf16[128,1024]{1,0:T(8,128)(2,1)S(1)} %get-tuple-element.66.refs_8_), channel_id=1, source_target_pairs={{0,2},{1,3},{2,0},{3,1},{4,6},{5,7},{6,4},{7,5},{8,10},{9,11},{10,... | collective-permute-start | bytes 786440 | tf_op jit(solution)/shard_map/ppermute | solution.py:390
  92.0 10.1 %collective-permute-start.23 = (bf16[128,1024]{1,0:T(8,128)(2,1)S(1)}, bf16[128,1024]{1,0:T(8,128)(2,1)}, u32[]{:S(2)}, u32[]{:S(2)}) collective-permute-start(bf16[128,1024]{1,0:T(8,128)(2,1)S(1)} %collective-permute-done.19.refs_11_), channel_id=1, source_target_pairs={{0,1},{1,0},{2,3},{3,2},{4,5},{5,4},{6,7},{7,6},{8,9},{9,8},{10,11... | collective-permute-start | bytes 786440 | tf_op jit(solution)/shard_map/ppermute | solution.py:390
  92.2 9.9 %collective-permute-start.22 = (bf16[128,1024]{1,0:T(8,128)(2,1)S(1)}, bf16[128,1024]{1,0:T(8,128)(2,1)}, u32[]{:S(2)}, u32[]{:S(2)}) collective-permute-start(bf16[128,1024]{1,0:T(8,128)(2,1)S(1)} %collective-permute-done.18.refs_10_), channel_id=1, source_target_pairs={{0,1},{1,0},{2,3},{3,2},{4,5},{5,4},{6,7},{7,6},{8,9},{9,8},{10,11... | collective-permute-start | bytes 786440 | tf_op jit(solution)/shard_map/ppermute | solution.py:390
  98.5 10.3 %collective-permute-start.12 = (bf16[128,1024]{1,0:T(8,128)(2,1)S(1)}, bf16[128,1024]{1,0:T(8,128)(2,1)}, u32[]{:S(2)}, u32[]{:S(2)}) collective-permute-start(bf16[128,1024]{1,0:T(8,128)(2,1)S(1)} %add_convert_fusion.5.refs_0_), channel_id=1, source_target_pairs={{0,6},{1,7},{2,4},{3,5},{4,2},{5,3},{6,0},{7,1},{8,14},{9,15},{10,... | collective-permute-start | bytes 786440 | tf_op jit(solution)/shard_map/ppermute | solution.py:390
  100.0 13.4 %collective-permute-start.11 = (bf16[128,1024]{1,0:T(8,128)(2,1)S(1)}, bf16[128,1024]{1,0:T(8,128)(2,1)S(1)}, u32[]{:S(2)}, u32[]{:S(2)}) collective-permute-start(bf16[128,1024]{1,0:T(8,128)(2,1)S(1)} %add_convert_fusion.5.refs_0_), channel_id=1, source_target_pairs={{0,4},{1,5},{2,6},{3,7},{4,0},{5,1},{6,2},{7,3},{8,12},{9,13},{10,... | collective-permute-start | bytes 786440 | tf_op jit(solution)/shard_map/ppermute | solution.py:390
  101.7 11.9 %collective-permute-start.10 = (bf16[128,1024]{1,0:T(8,128)(2,1)S(1)}, bf16[128,1024]{1,0:T(8,128)(2,1)S(1)}, u32[]{:S(2)}, u32[]{:S(2)}) collective-permute-start(bf16[128,1024]{1,0:T(8,128)(2,1)S(1)} %add_convert_fusion.5.refs_0_), channel_id=1, source_target_pairs={{0,2},{1,3},{2,0},{3,1},{4,6},{5,7},{6,4},{7,5},{8,10},{9,11},{10,... | collective-permute-start | bytes 786440 | tf_op jit(solution)/shard_map/ppermute | solution.py:390
  102.1 13.2 %collective-permute-start.21 = (bf16[128,1024]{1,0:T(8,128)(2,1)S(1)}, bf16[128,1024]{1,0:T(8,128)(2,1)S(1)}, u32[]{:S(2)}, u32[]{:S(2)}) collective-permute-start(bf16[128,1024]{1,0:T(8,128)(2,1)S(1)} %collective-permute-done.17.refs_9_), channel_id=1, source_target_pairs={{0,1},{1,0},{2,3},{3,2},{4,5},{5,4},{6,7},{7,6},{8,9},{9,8},{10,11... | collective-permute-start | bytes 786440 | tf_op jit(solution)/shard_map/ppermute | solution.py:390
  102.1 13.6 %collective-permute-start.13 = (bf16[128,1024]{1,0:T(8,128)(2,1)S(1)}, bf16[128,1024]{1,0:T(8,128)(2,1)S(1)}, u32[]{:S(2)}, u32[]{:S(2)}) collective-permute-start(bf16[128,1024]{1,0:T(8,128)(2,1)S(1)} %add_convert_fusion.5.refs_0_), channel_id=1, source_target_pairs={{0,1},{1,0},{2,3},{3,2},{4,5},{5,4},{6,7},{7,6},{8,9},{9,8},{10,11... | collective-permute-start | bytes 786440 | tf_op jit(solution)/shard_map/ppermute | solution.py:390
  108.7 6.9 %collective-permute-start.16 = (bf16[128,1024]{1,0:T(8,128)(2,1)}, bf16[128,1024]{1,0:T(8,128)(2,1)S(1)}, u32[]{:S(2)}, u32[]{:S(2)}) collective-permute-start(bf16[128,1024]{1,0:T(8,128)(2,1)} %collective-permute-done.12.refs_3_), channel_id=1, source_target_pairs={{0,1},{1,0},{2,3},{3,2},{4,5},{5,4},{6,7},{7,6},{8,9},{9,8},{10,11... | collective-permute-start | bytes 786440 | tf_op jit(solution)/shard_map/ppermute | solution.py:390
  133.3 19.0 %all-to-all-start.3 = ((bf16[4,128,1024]{2,1,0:T(8,128)(2,1)}), bf16[4,128,1024]{2,1,0:T(8,128)(2,1)}, u32[]{:S(2)}, u32[]{:S(2)}) async-start(bf16[4,128,1024]{2,1,0:T(8,128)(2,1)} %bitcast.20), calls=%async_computation.3 | async-start | bytes 2097152 | tf_op jit(solution)/shard_map/all_to_all | solution.py:420
  137.7 103.6 %reduce-scatter.2.cloned.1.call-start = ((), (), s32[]{:S(2)}) async-start(), calls=%async_computation.11 | async-start | bytes 2621440 | tf_op jit(solution)/shard_map/reduce_scatter | solution.py:592
  139.6 20.3 %collective-permute-start.24 = (bf16[512,1024]{1,0:T(8,128)(2,1)}, bf16[512,1024]{1,0:T(8,128)(2,1)}, u32[]{:S(2)}, u32[]{:S(2)}) collective-permute-start(bf16[512,1024]{1,0:T(8,128)(2,1)} %convolution_convert_fusion.2), channel_id=1, source_target_pairs={{0,1},{1,0},{2,3},{3,2},{4,5},{5,4},{6,7},{7,6},{8,9},{9,8},{10,11... | collective-permute-start | bytes 3145736 | tf_op jit(solution)/shard_map/ppermute | solution.py:390
  163.0 10.4 %collective-permute-start.26 = (bf16[128,1024]{1,0:T(8,128)(2,1)}, bf16[128,1024]{1,0:T(8,128)(2,1)S(1)}, u32[]{:S(2)}, u32[]{:S(2)}) collective-permute-start(bf16[128,1024]{1,0:T(8,128)(2,1)} %get-tuple-element.80), channel_id=1, source_target_pairs={{0,6},{1,7},{2,4},{3,5},{4,2},{5,3},{6,0},{7,1},{8,14},{9,15},{10,... | collective-permute-start | bytes 786440 | tf_op jit(solution)/shard_map/ppermute | solution.py:390
  164.4 13.7 %collective-permute-start.28 = (bf16[128,1024]{1,0:T(8,128)(2,1)}, bf16[128,1024]{1,0:T(8,128)(2,1)S(1)}, u32[]{:S(2)}, u32[]{:S(2)}) collective-permute-start(bf16[128,1024]{1,0:T(8,128)(2,1)} %get-tuple-element.81), channel_id=1, source_target_pairs={{0,4},{1,5},{2,6},{3,7},{4,0},{5,1},{6,2},{7,3},{8,12},{9,13},{10,... | collective-permute-start | bytes 786440 | tf_op jit(solution)/shard_map/ppermute | solution.py:390
  165.9 13.1 %collective-permute-start.27 = (bf16[128,1024]{1,0:T(8,128)(2,1)}, bf16[128,1024]{1,0:T(8,128)(2,1)S(1)}, u32[]{:S(2)}, u32[]{:S(2)}) collective-permute-start(bf16[128,1024]{1,0:T(8,128)(2,1)} %get-tuple-element.82), channel_id=1, source_target_pairs={{0,2},{1,3},{2,0},{3,1},{4,6},{5,7},{6,4},{7,5},{8,10},{9,11},{10,... | collective-permute-start | bytes 786440 | tf_op jit(solution)/shard_map/ppermute | solution.py:390
  168.8 11.7 %all-to-all-start.4 = ((bf16[8,128,128]{2,1,0:T(8,128)(2,1)}), bf16[8,128,128]{2,1,0:T(8,128)(2,1)S(1)}, u32[]{:S(2)}, u32[]{:S(2)}) async-start(bf16[8,128,128]{2,1,0:T(8,128)(2,1)} %bitcast.22), calls=%async_computation.4 | async-start | bytes 524288 | tf_op jit(solution)/shard_map/all_to_all | solution.py:432
  193.3 3.9 %collective-permute-start.29 = (bf16[512,1024]{1,0:T(8,128)(2,1)}, bf16[512,1024]{1,0:T(8,128)(2,1)S(1)}, u32[]{:S(2)}, u32[]{:S(2)}) collective-permute-start(bf16[512,1024]{1,0:T(8,128)(2,1)} %get-tuple-element.39), channel_id=1, source_target_pairs={{0,1},{1,0},{2,3},{3,2},{4,5},{5,4},{6,7},{7,6},{8,9},{9,8},{10,11... | collective-permute-start | bytes 3145736 | tf_op jit(solution)/shard_map/ppermute | solution.py:390
  196.8 39.1 %collective-permute-start.33 = (bf16[4,128,1024]{2,1,0:T(8,128)(2,1)}, bf16[4,128,1024]{2,1,0:T(8,128)(2,1)}, u32[]{:S(2)}, u32[]{:S(2)}) collective-permute-start(bf16[4,128,1024]{2,1,0:T(8,128)(2,1)} %pad_maximum_fusion.1), channel_id=1, source_target_pairs={{0,1},{1,0},{2,3},{3,2},{4,5},{5,4},{6,7},{7,6},{8,9},{9,8},{10,11... | collective-permute-start | bytes 3145736 | tf_op jit(solution)/shard_map/ppermute | solution.py:390
  198.7 18.0 %all-to-all-start.5 = ((bf16[4,128,1024]{2,1,0:T(8,128)(2,1)}), bf16[4,128,1024]{2,1,0:T(8,128)(2,1)S(1)}, u32[]{:S(2)}, u32[]{:S(2)}) async-start(bf16[4,128,1024]{2,1,0:T(8,128)(2,1)} %bitcast.25), calls=%async_computation.5 | async-start | bytes 2097152 | tf_op jit(solution)/shard_map/all_to_all | solution.py:420
  207.3 26.0 %collective-permute-start.30 = (bf16[8,32,384]{2,1,0:T(8,128)(2,1)}, bf16[8,32,384]{2,1,0:T(8,128)(2,1)}, u32[]{:S(2)}, u32[]{:S(2)}) collective-permute-start(bf16[8,32,384]{2,1,0:T(8,128)(2,1)} %get-tuple-element.85), channel_id=1, source_target_pairs={{0,8},{1,9},{2,10},{3,11},{4,12},{5,13},{6,14},{7,15},{8,16},{9,17... | collective-permute-start | bytes 589832 | tf_op jit(solution)/shard_map/ppermute | solution.py:394
  208.9 24.5 %collective-permute-start.32 = (bf16[8,32,384]{2,1,0:T(8,128)(2,1)}, bf16[8,32,384]{2,1,0:T(8,128)(2,1)}, u32[]{:S(2)}, u32[]{:S(2)}) collective-permute-start(bf16[8,32,384]{2,1,0:T(8,128)(2,1)} %get-tuple-element.86), channel_id=1, source_target_pairs={{0,24},{1,25},{2,26},{3,27},{4,28},{5,29},{6,30},{7,31},{8,0},{9,1... | collective-permute-start | bytes 589832 | tf_op jit(solution)/shard_map/ppermute | solution.py:394
  211.2 22.2 %collective-permute-start.31 = (bf16[8,32,384]{2,1,0:T(8,128)(2,1)}, bf16[8,32,384]{2,1,0:T(8,128)(2,1)}, u32[]{:S(2)}, u32[]{:S(2)}) collective-permute-start(bf16[8,32,384]{2,1,0:T(8,128)(2,1)} %get-tuple-element.87), channel_id=1, source_target_pairs={{0,16},{1,17},{2,18},{3,19},{4,20},{5,21},{6,22},{7,23},{8,24},{9,... | collective-permute-start | bytes 589832 | tf_op jit(solution)/shard_map/ppermute | solution.py:394
  218.7 13.4 %all-to-all-start.6 = ((f32[32,1,384]{2,1,0:T(1,128)}), f32[32,1,384]{2,1,0:T(1,128)S(1)}, u32[]{:S(2)}, u32[]{:S(2)}) async-start(f32[32,1,384]{2,1,0:T(1,128)} %copy.59), calls=%async_computation.6 | async-start | bytes 98304 | tf_op jit(solution)/shard_map/all_to_all | solution.py:645
  237.7 10.2 %collective-permute-start.34 = (bf16[128,1024]{1,0:T(8,128)(2,1)S(1)}, bf16[128,1024]{1,0:T(8,128)(2,1)S(1)}, u32[]{:S(2)}, u32[]{:S(2)}) collective-permute-start(bf16[128,1024]{1,0:T(8,128)(2,1)S(1)} %get-tuple-element.77), channel_id=1, source_target_pairs={{0,6},{1,7},{2,4},{3,5},{4,2},{5,3},{6,0},{7,1},{8,14},{9,15},{10,... | collective-permute-start | bytes 786440 | tf_op jit(solution)/shard_map/ppermute | solution.py:390
  238.4 14.0 %collective-permute-start.36 = (bf16[128,1024]{1,0:T(8,128)(2,1)S(1)}, bf16[128,1024]{1,0:T(8,128)(2,1)S(1)}, u32[]{:S(2)}, u32[]{:S(2)}) collective-permute-start(bf16[128,1024]{1,0:T(8,128)(2,1)S(1)} %get-tuple-element.78), channel_id=1, source_target_pairs={{0,4},{1,5},{2,6},{3,7},{4,0},{5,1},{6,2},{7,3},{8,12},{9,13},{10,... | collective-permute-start | bytes 786440 | tf_op jit(solution)/shard_map/ppermute | solution.py:390
  239.7 12.9 %collective-permute-start.35 = (bf16[128,1024]{1,0:T(8,128)(2,1)S(1)}, bf16[128,1024]{1,0:T(8,128)(2,1)S(1)}, u32[]{:S(2)}, u32[]{:S(2)}) collective-permute-start(bf16[128,1024]{1,0:T(8,128)(2,1)S(1)} %get-tuple-element.79), channel_id=1, source_target_pairs={{0,2},{1,3},{2,0},{3,1},{4,6},{5,7},{6,4},{7,5},{8,10},{9,11},{10,... | collective-permute-start | bytes 786440 | tf_op jit(solution)/shard_map/ppermute | solution.py:390
  243.1 19.4 %all-to-all-start.7 = ((bf16[8,32,896]{2,1,0:T(8,128)(2,1)}), bf16[8,32,896]{2,1,0:T(8,128)(2,1)S(1)}, u32[]{:S(2)}, u32[]{:S(2)}) async-start(bf16[8,32,896]{2,1,0:T(8,128)(2,1)} %pad_maximum_fusion.2), calls=%async_computation.8 | async-start | bytes 917504 | tf_op jit(solution)/shard_map/all_to_all | solution.py:432
  252.8 6.7 %collective-permute-start.37 = (bf16[32,1024]{1,0:T(8,128)(2,1)S(1)}, bf16[32,1024]{1,0:T(8,128)(2,1)S(1)}, u32[]{:S(2)}, u32[]{:S(2)}) collective-permute-start(bf16[32,1024]{1,0:T(8,128)(2,1)S(1)} %get-tuple-element.90), channel_id=1, source_target_pairs={{0,8},{1,9},{2,10},{3,11},{4,12},{5,13},{6,14},{7,15},{8,16},{9,17... | collective-permute-start | bytes 196616 | tf_op jit(solution)/shard_map/ppermute | solution.py:394
  253.4 6.1 %collective-permute-start.39 = (bf16[32,1024]{1,0:T(8,128)(2,1)S(1)}, bf16[32,1024]{1,0:T(8,128)(2,1)S(1)}, u32[]{:S(2)}, u32[]{:S(2)}) collective-permute-start(bf16[32,1024]{1,0:T(8,128)(2,1)S(1)} %get-tuple-element.91), channel_id=1, source_target_pairs={{0,24},{1,25},{2,26},{3,27},{4,28},{5,29},{6,30},{7,31},{8,0},{9,1... | collective-permute-start | bytes 196616 | tf_op jit(solution)/shard_map/ppermute | solution.py:394
  256.7 5.2 %collective-permute-start.38 = (bf16[32,1024]{1,0:T(8,128)(2,1)S(1)}, bf16[32,1024]{1,0:T(8,128)(2,1)S(1)}, u32[]{:S(2)}, u32[]{:S(2)}) collective-permute-start(bf16[32,1024]{1,0:T(8,128)(2,1)S(1)} %get-tuple-element.92), channel_id=1, source_target_pairs={{0,16},{1,17},{2,18},{3,19},{4,20},{5,21},{6,22},{7,23},{8,24},{9,... | collective-permute-start | bytes 196616 | tf_op jit(solution)/shard_map/ppermute | solution.py:394
  (56 other events, 514.3 us)
Sparse Core Ops, SparseCore 0:
  11.0 78.1 all-gather.2
  90.7 24.9 all-gather.4
  168.9 42.5 reduce-scatter.1

commit v2 on v1

--- a/solution.py
+++ b/solution.py
@@ -378,6 +378,38 @@
     )(places, *inputs, *grads, *up_parts, down, bias)
 
 
+def branch_kernel(place_ref, earlier_ref, act_ref, down_ref, out_ref):
+    rows = act_ref.shape[0] // 2
+    result = plain_dot(act_ref[...], down_ref[...]).astype(LOW)
+    odd = (place_ref[0] >> 1) & 1
+    out_ref[pl.ds(pl.multiple_of(odd * rows, rows), rows), :] = result[:rows]
+    out_ref[pl.ds(pl.multiple_of((1 - odd) * rows, rows), rows), :] = result[rows:]
+
+
+def branch_terms(act, down, places, earlier):
+    tokens, hidden = act.shape
+    width = down.shape[1]
+    rows = 2 * tokens // GROUP
+    return pl.pallas_call(
+        branch_kernel,
+        grid_spec=pltpu.PrefetchScalarGridSpec(
+            num_scalar_prefetch=1,
+            grid=(tokens // rows,),
+            in_specs=[
+                pl.BlockSpec(memory_space=pl.ANY),
+                pl.BlockSpec((rows, hidden), lambda i, p: (i, 0)),
+                fixed((hidden, width)),
+            ],
+            out_specs=pl.BlockSpec(
+                (rows, width),
+                lambda i, p: (2 * ((p[0] & 1) ^ (i >> 1)) + ((p[0] >> 2) ^ (i & 1)), 0),
+            ),
+        ),
+        out_shape=jax.ShapeDtypeStruct((tokens, width), LOW),
+        compiler_params=pltpu.CompilerParams(vmem_limit_bytes=VMEM_BYTES),
+    )(places, earlier, act, down)
+
+
 class Links:
     def __init__(self, count):
         self.count = count
@@ -419,6 +451,10 @@
         parts = halves.reshape(chips, halves.shape[0] // chips, halves.shape[1])
         terms = lax.all_to_all(parts, "dp", 0, 0, axis_index_groups=groups, tiled=True)
         return jnp.sum(terms.astype(WIDE), axis=0)
+
+    def core_lists(self):
+        order = [2 * m + c for c in range(2) for m in range(GROUP // 2)]
+        return [[p * GROUP + j for j in order] for p in range(self.planes)]
 
     def group_lists(self):
         return [[p * GROUP + j for j in range(GROUP)] for p in range(self.planes)]
@@ -571,9 +607,6 @@
     )
     grad_hidden_half = links.core_sum(near, far)
     grad_hidden_two = links.chip_exchange(grad_hidden_half)
-    far = plain_dot(activated_low[half_rows:], down_full).astype(LOW)
-    near = plain_dot(activated_low[:half_rows], down_full).astype(LOW)
-    feed_near, feed_far = near, far
     grad_middle = grad_out + norm_back(grad_hidden_two, normed_two, inverse_two, gain_two)
     grad_branch = grad_middle.astype(LOW)
     grad_mixed_own = right_dot(grad_branch, out_full).astype(LOW)
@@ -581,29 +614,6 @@
     grad_mixed = links.exchange(grad_mixed_sent)
     grad_mixed = grad_mixed.reshape(GROUP * rows, shard)
 
-    feed_half = links.core_sum(feed_near, feed_far, order_zero(grad_mixed_sent))
-    block_out = links.chip_sum(feed_half.reshape(4, rows, width))
-    block_out = (middle + block_out + bias_down).astype(LOW)
-
-    pieces = [left_dot(hidden_two, grad_pre_low).astype(LOW).reshape(planes, -1, hidden_shard)]
-    for start in range(0, width, hidden_shard):
-        piece = left_dot(activated_low, grad_feed[:, start : start + hidden_shard]).astype(LOW)
-        pieces.append(piece.reshape(planes, own_hidden, hidden_shard))
-    both_rows = lax.psum_scatter(
-        jnp.concatenate(pieces, axis=1), "dp", axis_index_groups=links.plane_groups()
-    )
-    up_rows = both_rows[: GROUP * own_rows].reshape(GROUP, own_rows, hidden_shard)
-    grad_down_w = both_rows[GROUP * own_rows :].reshape(-1, own_hidden, hidden_shard)
-    grad_down_w = grad_down_w.transpose(1, 0, 2).reshape(own_hidden, width).astype(WIDE)
-
-    grad_packed, near, far, norm_sums, packed_sums = attention_back(
-        packed, grad_mixed, allowed, qkv_full, normed_low, places, block_out
-    )
-    proj_rows = left_dot(hidden_one, grad_packed).astype(LOW)
-    proj_rows = proj_rows.reshape(planes, GROUP, own_rows, heads_width)
-    proj_sum = links.plane_sum(proj_rows)
-    grad_hidden_half = links.core_sum(near, far)
-    grad_hidden_one = links.chip_exchange(grad_hidden_half)
     out_parts = left_dot(mixed, grad_branch).astype(LOW)
     out_parts = out_parts.reshape(planes, GROUP, own_rows, width)
     out_near, out_far = (
@@ -612,9 +622,34 @@
         ).reshape(4, planes * own_rows, width)
         for order in ((0, 2, 4, 6), (1, 3, 5, 7))
     )
-    out_half = links.core_sum(out_near, out_far, order_zero(proj_sum))
-    out_sum = links.chip_sum(out_half).astype(LOW)
-
+    out_half = links.core_sum(out_near, out_far)
+
+    pieces = [left_dot(hidden_two, grad_pre_low).astype(LOW).reshape(planes, -1, hidden_shard)]
+    for start in range(0, width, hidden_shard):
+        piece = left_dot(activated_low, grad_feed[:, start : start + hidden_shard]).astype(LOW)
+        pieces.append(piece.reshape(planes, own_hidden, hidden_shard))
+    both_rows = lax.psum_scatter(
+        jnp.concatenate(pieces, axis=1), "dp", axis_index_groups=links.plane_groups()
+    )
+    up_rows = both_rows[: GROUP * own_rows].reshape(GROUP, own_rows, hidden_shard)
+    grad_down_w = both_rows[GROUP * own_rows :].reshape(-1, own_hidden, hidden_shard)
+    grad_down_w = grad_down_w.transpose(1, 0, 2).reshape(own_hidden, width).astype(WIDE)
+
+    grad_packed, near, far, norm_sums, packed_sums = attention_back(
+        packed, grad_mixed, allowed, qkv_full, normed_low, places, out_half
+    )
+    proj_rows = left_dot(hidden_one, grad_packed).astype(LOW)
+    proj_rows = proj_rows.reshape(planes, GROUP, own_rows, heads_width)
+    proj_sum = links.plane_sum(proj_rows)
+    grad_hidden_half = links.core_sum(near, far)
+    grad_hidden_one = links.chip_exchange(grad_hidden_half)
+    feed_parts = branch_terms(activated_low, down_full, places, grad_hidden_half)
+    feed = lax.psum_scatter(
+        feed_parts, "dp", axis_index_groups=links.core_lists(), scatter_dimension=0, tiled=True
+    )
+    block_out = (middle + feed.astype(WIDE) + bias_down).astype(LOW)
+    out_chips = (out_half + order_zero(grad_hidden_one).astype(LOW)).reshape(4, -1, width)
+    out_sum = links.chip_sum(out_chips).astype(LOW)
     normed_one, inverse_one = norm_rows(token_rows)
     grad_inputs = grad_middle + norm_back(grad_hidden_one, normed_one, inverse_one, gain_one)
 

time: 274 us -> 264 us (0.964)
  waiting for transfers between devices: 81.5 us -> 74.5 us
  Pallas kernels: 35.7 us -> 41.1 us
  matrix products: 17 us -> 13.2 us
    all_to_all x1, waiting for transfers between devices: 8.81 us -> 0.1 us  [local(): sums = jnp.sum(lax.all_to_all(vectors, 'dp', 0, 0, tiled=True), axis=0)]
    pallas_call x0 -> x1, Pallas kernels: none -> 5.43 us  [branch_terms(): pl.pallas_call(branch_kernel, grid_spec=pltpu.PrefetchScalarGridSpec(num_...]
    all_to_all x2, waiting for transfers between devices: 13.5 us -> 9.17 us  [chip_exchange(): lax.all_to_all(parts, 'dp', 0, 0, axis_index_groups=groups, tiled=True)]
    ppermute x31 -> x27, starting transfers between devices: 21.4 us -> 17.3 us  [swap(): return lax.ppermute(array, 'dp', [(i, i ^ flip) for i in range(self.count)])]
    dot_general x9 -> x7, matrix products: 17 us -> 13.2 us  [dot(): lax.dot_general(first, second, (dims, ((), ())), preferred_element_type=j...]
    all_to_all x4, waiting for transfers between devices: 7.23 us -> 10.6 us  [exchange(): lax.all_to_all(parts, 'dp', 0, 0, axis_index_groups=self.group_lists(), t...]
    ppermute x31 -> x27, waiting for transfers between devices: 42 us -> 39.3 us  [swap(): return lax.ppermute(array, 'dp', [(i, i ^ flip) for i in range(self.count)])]
    unnamed x112 -> x96, local copies, waits for them, and re-layouts: 6.47 us -> 6.91 us
  transfers between devices with their start and end apart: 51 -> 48, of which waited for: 19 -> 18; matrix products, arithmetic and copies ran while one was open for 22% -> 22% of each run, Pallas kernels for 9% -> 11%
where the time goes in v2:
time: 264 us; the launch traced here: 262 us
  waiting for transfers between devices  74.5 us (28%)
  starting transfers between devices  63.5 us (24%)
  Pallas kernels  41.1 us (16%)
  local copies, waits for them, and re-layouts  27.7 us (10%)
  other arithmetic  23.5 us (9%)
  between operations  18.7 us (7%)
  matrix products  13.2 us (5%)
    ppermute x27, waiting for transfers between devices, swap(): return lax.ppermute(array, 'dp', [(i, i ^ flip) for i in range(self.count)])  39.3 us
    ppermute x27, starting transfers between devices, swap(): return lax.ppermute(array, 'dp', [(i, i ^ flip) for i in range(self.count)])  17.3 us
    all_to_all x4, starting transfers between devices, exchange(): lax.all_to_all(parts, 'dp', 0, 0, axis_index_groups=self.group_lists(), t...  15.6 us
    ppermute x9, starting transfers between devices, shift(): lax.ppermute(array, 'dp', [(i, (i + hop) % self.count) for i in range(sel...  13.6 us
    dot_general x7, matrix products, dot(): lax.dot_general(first, second, (dims, ((), ())), preferred_element_type=j...  13.2 us
    pallas_call x1, Pallas kernels, attention_back(): pl.pallas_call(lambda place_ref, a_ref, *refs: attention_back_kernel(*ref...  12.1 us
    pallas_call x1, Pallas kernels, attention(): pl.pallas_call(attention_kernel, grid_spec=pltpu.PrefetchScalarGridSpec(n...  11.9 us
    pallas_call x1, Pallas kernels, feed_forward(): pl.pallas_call(feed_kernel, grid_spec=pltpu.PrefetchScalarGridSpec(num_sc...  11.7 us
  transfers between devices with their start and end apart: 48, of which 18 were waited for; matrix products, arithmetic and copies ran while one was open for 22% of the time, Pallas kernels for 11%

profile of v2, /device:TPU:0, one launch (start us, length us, event | category | flops | bytes accessed | tf_op | source)
XLA Modules:
  0.0 262.1 jit_solution(9375261743205903157)
XLA Ops:
  9.9 5.2 %all-to-all-start = ((bf16[8,32,512]{2,1,0:T(8,128)(2,1)}), bf16[8,32,512]{2,1,0:T(8,128)(2,1)S(1)}, u32[]{:S(2)}, u32[]{:S(2)}) async-start(bf16[8,32,512]{2,1,0:T(8,128)(2,1)} %reshape.430), calls=%async_computation | async-start | bytes 524288 | tf_op jit(solution)/shard_map/all_to_all | solution.py:468
  15.4 6.6 %all-to-all-done.refs_16_ = bf16[8,32,512]{2,1,0:T(8,128)(2,1)S(1)} async-done(((bf16[8,32,512]{2,1,0:T(8,128)(2,1)}), bf16[8,32,512]{2,1,0:T(8,128)(2,1)S(1)}, u32[]{:S(2)}, u32[]{:S(2)}) %all-to-all-start) | async-done | bytes 262176 | tf_op jit(solution)/shard_map/all_to_all | solution.py:468
  24.4 4.0 %all-to-all-start.1 = ((bf16[32,104,128]{2,1,0:T(8,128)(2,1)}), bf16[32,104,128]{2,1,0:T(8,128)(2,1)S(1)}, u32[]{:S(2)}, u32[]{:S(2)}) async-start(bf16[32,104,128]{2,1,0:T(8,128)(2,1)} %bitcast.10), calls=%async_computation.1 | async-start | bytes 1703936 | tf_op jit(solution)/shard_map/all_to_all | solution.py:554
  28.3 2.7 %collective-permute-start.2 = (bf16[128,1024]{1,0:T(8,128)(2,1)S(1)}, bf16[128,1024]{1,0:T(8,128)(2,1)S(1)}, u32[]{:S(2)}, u32[]{:S(2)}) collective-permute-start(bf16[128,1024]{1,0:T(8,128)(2,1)S(1)} %copy-done), channel_id=1, source_target_pairs={{0,6},{1,7},{2,4},{3,5},{4,2},{5,3},{6,0},{7,1},{8,14},{9,15},{10,... | collective-permute-start | bytes 786440 | tf_op jit(solution)/shard_map/ppermute | solution.py:422
  32.1 2.7 %collective-permute-start.19 = (bf16[128,1024]{1,0:T(8,128)(2,1)S(1)}, bf16[128,1024]{1,0:T(8,128)(2,1)S(1)}, u32[]{:S(2)}, u32[]{:S(2)}) collective-permute-start(bf16[128,1024]{1,0:T(8,128)(2,1)S(1)} %get-tuple-element.64.refs_8_), channel_id=1, source_target_pairs={{0,6},{1,7},{2,4},{3,5},{4,2},{5,3},{6,0},{7,1},{8,14},{9,15},{10,... | collective-permute-start | bytes 786440 | tf_op jit(solution)/shard_map/ppermute | solution.py:422
  35.4 12.5 %collective-permute-done.2.refs_3_ = bf16[128,1024]{1,0:T(8,128)(2,1)S(1)} collective-permute-done((bf16[128,1024]{1,0:T(8,128)(2,1)S(1)}, bf16[128,1024]{1,0:T(8,128)(2,1)S(1)}, u32[]{:S(2)}, u32[]{:S(2)}) %collective-permute-start.2) | collective-permute-done | bytes 262176 | tf_op jit(solution)/shard_map/ppermute | solution.py:422
  47.9 4.8 %collective-permute-done.1.refs_2_ = bf16[128,1024]{1,0:T(8,128)(2,1)S(1)} collective-permute-done((bf16[128,1024]{1,0:T(8,128)(2,1)S(1)}, bf16[128,1024]{1,0:T(8,128)(2,1)S(1)}, u32[]{:S(2)}, u32[]{:S(2)}) %collective-permute-start.1) | collective-permute-done | bytes 262176 | tf_op jit(solution)/shard_map/ppermute | solution.py:422
  55.6 1.6 collective-permute-start.18
  57.2 3.7 %collective-permute-start.9 = (bf16[8,32,512]{2,1,0:T(8,128)(2,1)S(1)}, bf16[8,32,512]{2,1,0:T(8,128)(2,1)S(1)}, u32[]{:S(2)}, u32[]{:S(2)}) collective-permute-start(bf16[8,32,512]{2,1,0:T(8,128)(2,1)S(1)} %all-to-all-done.refs_16_), channel_id=1, source_target_pairs={{0,24},{1,25},{2,26},{3,27},{4,28},{5,29},{6,30},{7,31},{8,0},{9,1... | collective-permute-start | bytes 786440 | tf_op jit(solution)/shard_map/ppermute | solution.py:426
  60.9 1.6 collective-permute-start.7
  64.4 11.9 %shard_map.263 = (bf16[1024,1024]{1,0:T(8,128)(2,1)}, bf16[1024,1024]{1,0:T(8,128)(2,1)}, bf16[1024,384]{1,0:T(8,128)(2,1)}, bf16[1024,384]{1,0:T(8,128)(2,1)}, bf16[1024,128]{1,0:T(8,128)(2,1)}) custom-call(s32[2]{0:T(128)} %pad_add_fusion.place_ref, bf16[128,1024]{1,0:T(8,128)(2,1)} %refs_0_.1, bf16[128,1024]{1,0:T(8,128)(2,1)} %copy-done.22, ...), custom_call_target="tpu_custom_call" | custom-call | flops 134217728 | bytes 1048576 | tf_op jit(solution)/shard_map/pallas_call | solution.py:195
  76.3 1.8 copy.77
  78.1 3.4 %all-to-all-start.2 = ((bf16[8,128,128]{1,2,0:T(8,128)(2,1)}), bf16[8,128,128]{1,2,0:T(8,128)(2,1)S(1)}, u32[]{:S(2)}, u32[]{:S(2)}) async-start(bf16[8,128,128]{1,2,0:T(8,128)(2,1)} %copy.77), calls=%async_computation.2 | async-start | bytes 524288 | tf_op jit(solution)/shard_map/all_to_all | solution.py:468
  82.3 7.5 %collective-permute-done.8.refs_18_ = bf16[8,32,512]{2,1,0:T(8,128)(2,1)S(1)} collective-permute-done((bf16[8,32,512]{2,1,0:T(8,128)(2,1)S(1)}, bf16[8,32,512]{2,1,0:T(8,128)(2,1)S(1)}, u32[]{:S(2)}, u32[]{:S(2)}) %collective-permute-start.8) | collective-permute-done | bytes 262176 | tf_op jit(solution)/shard_map/ppermute | solution.py:426
  95.3 2.2 fusion.40
  97.9 1.4 collective-permute-start.12
  99.4 1.7 collective-permute-start.11
  102.0 6.2 %collective-permute-done.12.refs_3_ = bf16[128,1024]{1,0:T(8,128)(2,1)} collective-permute-done((bf16[128,1024]{1,0:T(8,128)(2,1)S(1)}, bf16[128,1024]{1,0:T(8,128)(2,1)}, u32[]{:S(2)}, u32[]{:S(2)}) %collective-permute-start.12) | collective-permute-done | bytes 262176 | tf_op jit(solution)/shard_map/ppermute | solution.py:422
  108.2 4.8 %collective-permute-done.11.refs_2_ = bf16[128,1024]{1,0:T(8,128)(2,1)} collective-permute-done((bf16[128,1024]{1,0:T(8,128)(2,1)S(1)}, bf16[128,1024]{1,0:T(8,128)(2,1)}, u32[]{:S(2)}, u32[]{:S(2)}) %collective-permute-start.11) | collective-permute-done | bytes 262176 | tf_op jit(solution)/shard_map/ppermute | solution.py:422
  114.1 2.0 all-gather.5.cloned.1.call-done.refs_20_.down_ref
  116.8 11.7 %shard_map.264 = (bf16[1024,1024]{1,0:T(8,128)(2,1)}, bf16[1024,1024]{1,0:T(8,128)(2,1)}, bf16[1024,512]{1,0:T(8,128)(2,1)}, bf16[1024,512]{1,0:T(8,128)(2,1)}, ...) custom-call(s32[2]{0:T(128)} %pad_add_fusion.place_ref, bf16[128,1024]{1,0:T(8,128)(2,1)} %copy-done.10, ...), custom_call_target="tpu_custom_call" | custom-call | flops 536870912 | bytes 1048576 | tf_op jit(solution)/shard_map/pallas_call | solution.py:342
  128.6 3.1 %convolution_convert_fusion.3 = bf16[512,512]{1,0:T(8,128)(2,1)} fusion(bf16[1024,512]{1,0:T(8,128)(2,1)} %get-tuple-element.39.act_ref, bf16[1024,1024]{1,0:T(8,128)(2,1)} %get-tuple-element.47), kind=kOutput, calls=%fused_computation.10 | convolution fusion | flops 537133056 | bytes 2621440 | tf_op jit(solution)/shard_map/dot_general | solution.py:47
  133.1 3.8 %all-to-all-start.3 = ((bf16[4,128,1024]{2,1,0:T(8,128)(2,1)}), bf16[4,128,1024]{2,1,0:T(8,128)(2,1)S(1)}, u32[]{:S(2)}, u32[]{:S(2)}) async-start(bf16[4,128,1024]{2,1,0:T(8,128)(2,1)} %bitcast.21), calls=%async_computation.3 | async-start | bytes 2097152 | tf_op jit(solution)/shard_map/all_to_all | solution.py:452
  137.0 2.1 convolution_convert_fusion.4
  140.5 1.5 pad_maximum_fusion
  142.0 9.2 %all-to-all-done.3 = bf16[4,128,1024]{2,1,0:T(8,128)(2,1)S(1)} async-done(((bf16[4,128,1024]{2,1,0:T(8,128)(2,1)}), bf16[4,128,1024]{2,1,0:T(8,128)(2,1)S(1)}, u32[]{:S(2)}, u32[]{:S(2)}) %all-to-all-start.3) | async-done | bytes 1048608 | tf_op jit(solution)/shard_map/all_to_all | solution.py:452
  157.5 3.4 %all-to-all-start.4 = ((bf16[8,128,128]{2,1,0:T(8,128)(2,1)}), bf16[8,128,128]{2,1,0:T(8,128)(2,1)S(1)}, u32[]{:S(2)}, u32[]{:S(2)}) async-start(bf16[8,128,128]{2,1,0:T(8,128)(2,1)} %bitcast.143), calls=%async_computation.4 | async-start | bytes 524288 | tf_op jit(solution)/shard_map/all_to_all | solution.py:468
  161.0 2.9 %add_convert_fusion.1.a_ref = bf16[4,128,1024]{2,1,0:T(8,128)(2,1)} fusion(bf16[4,128,1024]{2,1,0:T(8,128)(2,1)} %collective-permute-done.25, bf16[1,128,1024]{2,1,0:T(8,128)(2,1)} %bitcast.149, bf16[1,128,1024]{2,1,0:T(8,128)(2,1)} %bitcast.151, bf16[1,128,1024]{2,1,0:T(8,128)(2,1)} %bitcast.153, bf16[1,128,1024]{2,1,0:T(8,128)(2,1)} %bitcast.147), kind=kLoop, calls=%fused_computation.5 | loop fusion | flops 3670016 | bytes 3145728 | tf_op jit(solution)/shard_map/convert_element_type | solution.py:436
  163.9 4.0 %all-to-all-done.4 = bf16[8,128,128]{2,1,0:T(8,128)(2,1)S(1)} async-done(((bf16[8,128,128]{2,1,0:T(8,128)(2,1)}), bf16[8,128,128]{2,1,0:T(8,128)(2,1)S(1)}, u32[]{:S(2)}, u32[]{:S(2)}) %all-to-all-start.4) | async-done | bytes 262176 | tf_op jit(solution)/shard_map/all_to_all | solution.py:468
  168.5 12.1 %shard_map.265 = (bf16[1024,384]{1,0:T(8,128)(2,1)}, bf16[512,1024]{1,0:T(8,128)(2,1)}, bf16[512,1024]{1,0:T(8,128)(2,1)}, f32[2,1024]{1,0:T(2,128)}, f32[1,384]{1,0:T(1,128)}) custom-call(s32[2]{0:T(128)} %pad_add_fusion.place_ref, bf16[4,128,1024]{2,1,0:T(8,128)(2,1)} %add_convert_fusion.1.a_ref, bf16[1024,384]{1,0:T(8,128)(2,1)} %get-tuple-element.34.refs_0_, ...), custom_call_target="tpu_custom_call" | custom-call | flops 335544320 | bytes 2097152 | tf_op jit(solution)/shard_map/pallas_call | solution.py:238
  183.5 2.7 %add_convert_fusion.earlier_ref = bf16[512,1024]{1,0:T(8,128)(2,1)} fusion(bf16[512,1024]{1,0:T(8,128)(2,1)S(1)} %collective-permute-done.26, bf16[512,1024]{1,0:T(8,128)(2,1)} %get-tuple-element.37), kind=kLoop, calls=%fused_computation.4 | loop fusion | flops 2097152 | bytes 3145728 | tf_op jit(solution)/shard_map/convert_element_type | solution.py:436
  186.2 3.5 %all-to-all-start.5 = ((bf16[4,128,1024]{2,1,0:T(8,128)(2,1)}), bf16[4,128,1024]{2,1,0:T(8,128)(2,1)S(1)}, u32[]{:S(2)}, u32[]{:S(2)}) async-start(bf16[4,128,1024]{2,1,0:T(8,128)(2,1)} %bitcast.33), calls=%async_computation.6 | async-start | bytes 2097152 | tf_op jit(solution)/shard_map/all_to_all | solution.py:452
  189.9 2.9 %convolution_convert_fusion.2 = bf16[1024,384]{1,0:T(8,128)(2,1)S(1)} fusion(bf16[1024,1024]{1,0:T(8,128)(2,1)} %get-tuple-element.43, bf16[1024,384]{1,0:T(8,128)(2,1)S(1)} %copy-done.44), kind=kOutput, calls=%fused_computation.9 | convolution fusion | flops 805699584 | bytes 3670016 | tf_op jit(solution)/shard_map/dot_general | solution.py:47
  194.5 1.4 collective-permute-start.27
  196.0 2.4 collective-permute-start.29
  198.6 5.4 %shard_map.266 = bf16[1024,1024]{1,0:T(8,128)(2,1)} custom-call(s32[2]{0:T(128)} %pad_add_fusion.place_ref, bf16[512,1024]{1,0:T(8,128)(2,1)} %add_convert_fusion.earlier_ref, bf16[1024,512]{1,0:T(8,128)(2,1)} %get-tuple-element.39.act_ref, bf16[512,1024]{1,0:T(8,128)(2,1)} %all-gather.5.cloned.1.call-done.refs_20_.down_ref), custom_call_target="tpu_custom_call" | custom-call | tf_op jit(solution)/shard_map/pallas_call | solution.py:393
  204.0 1.8 fusion.36
  209.0 5.5 %all-to-all-start.6 = ((f32[32,1,384]{2,1,0:T(1,128)}), f32[32,1,384]{2,1,0:T(1,128)S(1)}, u32[]{:S(2)}, u32[]{:S(2)}) async-start(f32[32,1,384]{2,1,0:T(1,128)} %copy.89), calls=%async_computation.7 | async-start | bytes 98304 | tf_op jit(solution)/shard_map/all_to_all | solution.py:680
  214.5 1.8 broadcast_add_fusion
  217.2 2.7 %collective-permute-start.30 = (bf16[128,1024]{1,0:T(8,128)(2,1)}, bf16[128,1024]{1,0:T(8,128)(2,1)S(1)}, u32[]{:S(2)}, u32[]{:S(2)}) collective-permute-start(bf16[128,1024]{1,0:T(8,128)(2,1)} %get-tuple-element.75), channel_id=1, source_target_pairs={{0,6},{1,7},{2,4},{3,5},{4,2},{5,3},{6,0},{7,1},{8,14},{9,15},{10,... | collective-permute-start | bytes 786440 | tf_op jit(solution)/shard_map/ppermute | solution.py:422
  225.8 3.6 %all-to-all-start.7 = ((bf16[8,32,896]{2,1,0:T(8,128)(2,1)}), bf16[8,32,896]{2,1,0:T(8,128)(2,1)S(1)}, u32[]{:S(2)}, u32[]{:S(2)}) async-start(bf16[8,32,896]{2,1,0:T(8,128)(2,1)} %pad_maximum_fusion.2), calls=%async_computation.9 | async-start | bytes 917504 | tf_op jit(solution)/shard_map/all_to_all | solution.py:468
  229.4 7.6 %collective-permute-done.32 = bf16[128,1024]{1,0:T(8,128)(2,1)} collective-permute-done((bf16[128,1024]{1,0:T(8,128)(2,1)}, bf16[128,1024]{1,0:T(8,128)(2,1)}, u32[]{:S(2)}, u32[]{:S(2)}) %collective-permute-start.32) | collective-permute-done | bytes 262176 | tf_op jit(solution)/shard_map/ppermute | solution.py:422
  237.1 1.5 collective-permute-done.31
  239.7 1.5 collective-permute-start.33
  241.2 2.4 collective-permute-start.35
  246.7 2.2 collective-permute-done.34
  252.5 1.4 reduce-scatter.3.cloned.1.call-done
  253.8 1.7 add_convert_fusion.3
  (262 shorter events, 49.3 us)
Async XLA Ops:
  7.3 87.9 %all-gather.3.cloned.1.call-start = ((), (), s32[]{:S(2)}) async-start(), calls=%async_computation.10 | async-start | bytes 2162688 | tf_op jit(solution)/shard_map/all_gather | solution.py:555
  9.9 12.1 %all-to-all-start = ((bf16[8,32,512]{2,1,0:T(8,128)(2,1)}), bf16[8,32,512]{2,1,0:T(8,128)(2,1)S(1)}, u32[]{:S(2)}, u32[]{:S(2)}) async-start(bf16[8,32,512]{2,1,0:T(8,128)(2,1)} %reshape.430), calls=%async_computation | async-start | bytes 524288 | tf_op jit(solution)/shard_map/all_to_all | solution.py:468
  24.4 29.5 %all-to-all-start.1 = ((bf16[32,104,128]{2,1,0:T(8,128)(2,1)}), bf16[32,104,128]{2,1,0:T(8,128)(2,1)S(1)}, u32[]{:S(2)}, u32[]{:S(2)}) async-start(bf16[32,104,128]{2,1,0:T(8,128)(2,1)} %bitcast.10), calls=%async_computation.1 | async-start | bytes 1703936 | tf_op jit(solution)/shard_map/all_to_all | solution.py:554
  28.3 19.6 %collective-permute-start.2 = (bf16[128,1024]{1,0:T(8,128)(2,1)S(1)}, bf16[128,1024]{1,0:T(8,128)(2,1)S(1)}, u32[]{:S(2)}, u32[]{:S(2)}) collective-permute-start(bf16[128,1024]{1,0:T(8,128)(2,1)S(1)} %copy-done), channel_id=1, source_target_pairs={{0,6},{1,7},{2,4},{3,5},{4,2},{5,3},{6,0},{7,1},{8,14},{9,15},{10,... | collective-permute-start | bytes 786440 | tf_op jit(solution)/shard_map/ppermute | solution.py:422
  31.1 21.6 %collective-permute-start.1 = (bf16[128,1024]{1,0:T(8,128)(2,1)S(1)}, bf16[128,1024]{1,0:T(8,128)(2,1)S(1)}, u32[]{:S(2)}, u32[]{:S(2)}) collective-permute-start(bf16[128,1024]{1,0:T(8,128)(2,1)S(1)} %copy-done), channel_id=1, source_target_pairs={{0,4},{1,5},{2,6},{3,7},{4,0},{5,1},{6,2},{7,3},{8,12},{9,13},{10,... | collective-permute-start | bytes 786440 | tf_op jit(solution)/shard_map/ppermute | solution.py:422
  31.6 22.3 %collective-permute-start = (bf16[128,1024]{1,0:T(8,128)(2,1)S(1)}, bf16[128,1024]{1,0:T(8,128)(2,1)S(1)}, u32[]{:S(2)}, u32[]{:S(2)}) collective-permute-start(bf16[128,1024]{1,0:T(8,128)(2,1)S(1)} %copy-done), channel_id=1, source_target_pairs={{0,2},{1,3},{2,0},{3,1},{4,6},{5,7},{6,4},{7,5},{8,10},{9,11},{10,... | collective-permute-start | bytes 786440 | tf_op jit(solution)/shard_map/ppermute | solution.py:422
  31.9 23.7 %collective-permute-start.3 = (bf16[128,1024]{1,0:T(8,128)(2,1)S(1)}, bf16[128,1024]{1,0:T(8,128)(2,1)}, u32[]{:S(2)}, u32[]{:S(2)}) collective-permute-start(bf16[128,1024]{1,0:T(8,128)(2,1)S(1)} %copy-done), channel_id=1, source_target_pairs={{0,1},{1,0},{2,3},{3,2},{4,5},{5,4},{6,7},{7,6},{8,9},{9,8},{10,11... | collective-permute-start | bytes 786440 | tf_op jit(solution)/shard_map/ppermute | solution.py:422
  32.1 58.3 %collective-permute-start.19 = (bf16[128,1024]{1,0:T(8,128)(2,1)S(1)}, bf16[128,1024]{1,0:T(8,128)(2,1)S(1)}, u32[]{:S(2)}, u32[]{:S(2)}) collective-permute-start(bf16[128,1024]{1,0:T(8,128)(2,1)S(1)} %get-tuple-element.64.refs_8_), channel_id=1, source_target_pairs={{0,6},{1,7},{2,4},{3,5},{4,2},{5,3},{6,0},{7,1},{8,14},{9,15},{10,... | collective-permute-start | bytes 786440 | tf_op jit(solution)/shard_map/ppermute | solution.py:422
  47.9 9.3 %collective-permute-start.6 = (bf16[128,1024]{1,0:T(8,128)(2,1)S(1)}, bf16[128,1024]{1,0:T(8,128)(2,1)}, u32[]{:S(2)}, u32[]{:S(2)}) collective-permute-start(bf16[128,1024]{1,0:T(8,128)(2,1)S(1)} %collective-permute-done.2.refs_3_), channel_id=1, source_target_pairs={{0,1},{1,0},{2,3},{3,2},{4,5},{5,4},{6,7},{7,6},{8,9},{9,8},{10,11... | collective-permute-start | bytes 786440 | tf_op jit(solution)/shard_map/ppermute | solution.py:422
  52.7 8.1 %collective-permute-start.5 = (bf16[128,1024]{1,0:T(8,128)(2,1)S(1)}, bf16[128,1024]{1,0:T(8,128)(2,1)}, u32[]{:S(2)}, u32[]{:S(2)}) collective-permute-start(bf16[128,1024]{1,0:T(8,128)(2,1)S(1)} %collective-permute-done.1.refs_2_), channel_id=1, source_target_pairs={{0,1},{1,0},{2,3},{3,2},{4,5},{5,4},{6,7},{7,6},{8,9},{9,8},{10,11... | collective-permute-start | bytes 786440 | tf_op jit(solution)/shard_map/ppermute | solution.py:422
  53.9 7.0 %collective-permute-start.4 = (bf16[128,1024]{1,0:T(8,128)(2,1)S(1)}, bf16[128,1024]{1,0:T(8,128)(2,1)}, u32[]{:S(2)}, u32[]{:S(2)}) collective-permute-start(bf16[128,1024]{1,0:T(8,128)(2,1)S(1)} %collective-permute-done.refs_1_), channel_id=1, source_target_pairs={{0,1},{1,0},{2,3},{3,2},{4,5},{5,4},{6,7},{7,6},{8,9},{9,8},{10,11... | collective-permute-start | bytes 786440 | tf_op jit(solution)/shard_map/ppermute | solution.py:422
  55.6 35.2 %collective-permute-start.18 = (bf16[128,1024]{1,0:T(8,128)(2,1)S(1)}, bf16[128,1024]{1,0:T(8,128)(2,1)S(1)}, u32[]{:S(2)}, u32[]{:S(2)}) collective-permute-start(bf16[128,1024]{1,0:T(8,128)(2,1)S(1)} %get-tuple-element.64.refs_8_), channel_id=1, source_target_pairs={{0,4},{1,5},{2,6},{3,7},{4,0},{5,1},{6,2},{7,3},{8,12},{9,13},{10,... | collective-permute-start | bytes 786440 | tf_op jit(solution)/shard_map/ppermute | solution.py:422
  57.2 36.6 %collective-permute-start.9 = (bf16[8,32,512]{2,1,0:T(8,128)(2,1)S(1)}, bf16[8,32,512]{2,1,0:T(8,128)(2,1)S(1)}, u32[]{:S(2)}, u32[]{:S(2)}) collective-permute-start(bf16[8,32,512]{2,1,0:T(8,128)(2,1)S(1)} %all-to-all-done.refs_16_), channel_id=1, source_target_pairs={{0,24},{1,25},{2,26},{3,27},{4,28},{5,29},{6,30},{7,31},{8,0},{9,1... | collective-permute-start | bytes 786440 | tf_op jit(solution)/shard_map/ppermute | solution.py:426
  60.9 29.0 %collective-permute-start.8 = (bf16[8,32,512]{2,1,0:T(8,128)(2,1)S(1)}, bf16[8,32,512]{2,1,0:T(8,128)(2,1)S(1)}, u32[]{:S(2)}, u32[]{:S(2)}) collective-permute-start(bf16[8,32,512]{2,1,0:T(8,128)(2,1)S(1)} %all-to-all-done.refs_16_), channel_id=1, source_target_pairs={{0,16},{1,17},{2,18},{3,19},{4,20},{5,21},{6,22},{7,23},{8,24},{9,... | collective-permute-start | bytes 786440 | tf_op jit(solution)/shard_map/ppermute | solution.py:426
  60.9 30.1 %collective-permute-start.7 = (bf16[8,32,512]{2,1,0:T(8,128)(2,1)S(1)}, bf16[8,32,512]{2,1,0:T(8,128)(2,1)}, u32[]{:S(2)}, u32[]{:S(2)}) collective-permute-start(bf16[8,32,512]{2,1,0:T(8,128)(2,1)S(1)} %all-to-all-done.refs_16_), channel_id=1, source_target_pairs={{0,8},{1,9},{2,10},{3,11},{4,12},{5,13},{6,14},{7,15},{8,16},{9,17... | collective-permute-start | bytes 786440 | tf_op jit(solution)/shard_map/ppermute | solution.py:426
  78.1 17.1 %all-to-all-start.2 = ((bf16[8,128,128]{1,2,0:T(8,128)(2,1)}), bf16[8,128,128]{1,2,0:T(8,128)(2,1)S(1)}, u32[]{:S(2)}, u32[]{:S(2)}) async-start(bf16[8,128,128]{1,2,0:T(8,128)(2,1)} %copy.77), calls=%async_computation.2 | async-start | bytes 524288 | tf_op jit(solution)/shard_map/all_to_all | solution.py:468
  81.6 34.5 %all-gather.5.cloned.1.call-start = ((), (), s32[]{:S(2)}) async-start(), calls=%async_computation.11 | async-start | bytes 1310720 | tf_op jit(solution)/shard_map/all_gather | solution.py:556
  89.8 9.5 %collective-permute-start.20 = (bf16[128,1024]{1,0:T(8,128)(2,1)S(1)}, bf16[128,1024]{1,0:T(8,128)(2,1)S(1)}, u32[]{:S(2)}, u32[]{:S(2)}) collective-permute-start(bf16[128,1024]{1,0:T(8,128)(2,1)S(1)} %get-tuple-element.64.refs_8_), channel_id=1, source_target_pairs={{0,1},{1,0},{2,3},{3,2},{4,5},{5,4},{6,7},{7,6},{8,9},{9,8},{10,11... | collective-permute-start | bytes 786440 | tf_op jit(solution)/shard_map/ppermute | solution.py:422
  90.4 10.7 %collective-permute-start.17 = (bf16[128,1024]{1,0:T(8,128)(2,1)S(1)}, bf16[128,1024]{1,0:T(8,128)(2,1)S(1)}, u32[]{:S(2)}, u32[]{:S(2)}) collective-permute-start(bf16[128,1024]{1,0:T(8,128)(2,1)S(1)} %get-tuple-element.64.refs_8_), channel_id=1, source_target_pairs={{0,2},{1,3},{2,0},{3,1},{4,6},{5,7},{6,4},{7,5},{8,10},{9,11},{10,... | collective-permute-start | bytes 786440 | tf_op jit(solution)/shard_map/ppermute | solution.py:422
  90.8 10.7 %collective-permute-start.23 = (bf16[128,1024]{1,0:T(8,128)(2,1)S(1)}, bf16[128,1024]{1,0:T(8,128)(2,1)S(1)}, u32[]{:S(2)}, u32[]{:S(2)}) collective-permute-start(bf16[128,1024]{1,0:T(8,128)(2,1)S(1)} %collective-permute-done.19.refs_11_), channel_id=1, source_target_pairs={{0,1},{1,0},{2,3},{3,2},{4,5},{5,4},{6,7},{7,6},{8,9},{9,8},{10,11... | collective-permute-start | bytes 786440 | tf_op jit(solution)/shard_map/ppermute | solution.py:422
  91.0 10.5 %collective-permute-start.22 = (bf16[128,1024]{1,0:T(8,128)(2,1)S(1)}, bf16[128,1024]{1,0:T(8,128)(2,1)S(1)}, u32[]{:S(2)}, u32[]{:S(2)}) collective-permute-start(bf16[128,1024]{1,0:T(8,128)(2,1)S(1)} %collective-permute-done.18.refs_10_), channel_id=1, source_target_pairs={{0,1},{1,0},{2,3},{3,2},{4,5},{5,4},{6,7},{7,6},{8,9},{9,8},{10,11... | collective-permute-start | bytes 786440 | tf_op jit(solution)/shard_map/ppermute | solution.py:422
  97.9 10.3 %collective-permute-start.12 = (bf16[128,1024]{1,0:T(8,128)(2,1)S(1)}, bf16[128,1024]{1,0:T(8,128)(2,1)}, u32[]{:S(2)}, u32[]{:S(2)}) collective-permute-start(bf16[128,1024]{1,0:T(8,128)(2,1)S(1)} %add_convert_fusion.4.refs_0_), channel_id=1, source_target_pairs={{0,6},{1,7},{2,4},{3,5},{4,2},{5,3},{6,0},{7,1},{8,14},{9,15},{10,... | collective-permute-start | bytes 786440 | tf_op jit(solution)/shard_map/ppermute | solution.py:422
  99.4 13.6 %collective-permute-start.11 = (bf16[128,1024]{1,0:T(8,128)(2,1)S(1)}, bf16[128,1024]{1,0:T(8,128)(2,1)}, u32[]{:S(2)}, u32[]{:S(2)}) collective-permute-start(bf16[128,1024]{1,0:T(8,128)(2,1)S(1)} %add_convert_fusion.4.refs_0_), channel_id=1, source_target_pairs={{0,4},{1,5},{2,6},{3,7},{4,0},{5,1},{6,2},{7,3},{8,12},{9,13},{10,... | collective-permute-start | bytes 786440 | tf_op jit(solution)/shard_map/ppermute | solution.py:422
  101.1 11.9 %collective-permute-start.10 = (bf16[128,1024]{1,0:T(8,128)(2,1)S(1)}, bf16[128,1024]{1,0:T(8,128)(2,1)}, u32[]{:S(2)}, u32[]{:S(2)}) collective-permute-start(bf16[128,1024]{1,0:T(8,128)(2,1)S(1)} %add_convert_fusion.4.refs_0_), channel_id=1, source_target_pairs={{0,2},{1,3},{2,0},{3,1},{4,6},{5,7},{6,4},{7,5},{8,10},{9,11},{10,... | collective-permute-start | bytes 786440 | tf_op jit(solution)/shard_map/ppermute | solution.py:422
  101.5 12.6 %collective-permute-start.21 = (bf16[128,1024]{1,0:T(8,128)(2,1)S(1)}, bf16[128,1024]{1,0:T(8,128)(2,1)S(1)}, u32[]{:S(2)}, u32[]{:S(2)}) collective-permute-start(bf16[128,1024]{1,0:T(8,128)(2,1)S(1)} %collective-permute-done.17.refs_9_), channel_id=1, source_target_pairs={{0,1},{1,0},{2,3},{3,2},{4,5},{5,4},{6,7},{7,6},{8,9},{9,8},{10,11... | collective-permute-start | bytes 786440 | tf_op jit(solution)/shard_map/ppermute | solution.py:422
  101.5 14.5 %collective-permute-start.13 = (bf16[128,1024]{1,0:T(8,128)(2,1)S(1)}, bf16[128,1024]{1,0:T(8,128)(2,1)S(1)}, u32[]{:S(2)}, u32[]{:S(2)}) collective-permute-start(bf16[128,1024]{1,0:T(8,128)(2,1)S(1)} %add_convert_fusion.4.refs_0_), channel_id=1, source_target_pairs={{0,1},{1,0},{2,3},{3,2},{4,5},{5,4},{6,7},{7,6},{8,9},{9,8},{10,11... | collective-permute-start | bytes 786440 | tf_op jit(solution)/shard_map/ppermute | solution.py:422
  108.2 7.9 %collective-permute-start.16 = (bf16[128,1024]{1,0:T(8,128)(2,1)}, bf16[128,1024]{1,0:T(8,128)(2,1)}, u32[]{:S(2)}, u32[]{:S(2)}) collective-permute-start(bf16[128,1024]{1,0:T(8,128)(2,1)} %collective-permute-done.12.refs_3_), channel_id=1, source_target_pairs={{0,1},{1,0},{2,3},{3,2},{4,5},{5,4},{6,7},{7,6},{8,9},{9,8},{10,11... | collective-permute-start | bytes 786440 | tf_op jit(solution)/shard_map/ppermute | solution.py:422
  113.0 3.1 %collective-permute-start.15 = (bf16[128,1024]{1,0:T(8,128)(2,1)}, bf16[128,1024]{1,0:T(8,128)(2,1)}, u32[]{:S(2)}, u32[]{:S(2)}) collective-permute-start(bf16[128,1024]{1,0:T(8,128)(2,1)} %collective-permute-done.11.refs_2_), channel_id=1, source_target_pairs={{0,1},{1,0},{2,3},{3,2},{4,5},{5,4},{6,7},{7,6},{8,9},{9,8},{10,11... | collective-permute-start | bytes 786440 | tf_op jit(solution)/shard_map/ppermute | solution.py:422
  113.0 3.1 %collective-permute-start.14 = (bf16[128,1024]{1,0:T(8,128)(2,1)}, bf16[128,1024]{1,0:T(8,128)(2,1)}, u32[]{:S(2)}, u32[]{:S(2)}) collective-permute-start(bf16[128,1024]{1,0:T(8,128)(2,1)} %collective-permute-done.10.refs_1_), channel_id=1, source_target_pairs={{0,1},{1,0},{2,3},{3,2},{4,5},{5,4},{6,7},{7,6},{8,9},{9,8},{10,11... | collective-permute-start | bytes 786440 | tf_op jit(solution)/shard_map/ppermute | solution.py:422
  128.5 3.3 %collective-permute-start.24 = (bf16[512,1024]{1,0:T(8,128)(2,1)}, bf16[512,1024]{1,0:T(8,128)(2,1)S(1)}, u32[]{:S(2)}, u32[]{:S(2)}) collective-permute-start(bf16[512,1024]{1,0:T(8,128)(2,1)} %get-tuple-element.33), channel_id=1, source_target_pairs={{0,1},{1,0},{2,3},{3,2},{4,5},{5,4},{6,7},{7,6},{8,9},{9,8},{10,11... | collective-permute-start | bytes 3145736 | tf_op jit(solution)/shard_map/ppermute | solution.py:422
  133.1 18.1 %all-to-all-start.3 = ((bf16[4,128,1024]{2,1,0:T(8,128)(2,1)}), bf16[4,128,1024]{2,1,0:T(8,128)(2,1)S(1)}, u32[]{:S(2)}, u32[]{:S(2)}) async-start(bf16[4,128,1024]{2,1,0:T(8,128)(2,1)} %bitcast.21), calls=%async_computation.3 | async-start | bytes 2097152 | tf_op jit(solution)/shard_map/all_to_all | solution.py:452
  136.9 67.1 %reduce-scatter.5.cloned.1.call-start = ((), (), s32[]{:S(2)}) async-start(), calls=%async_computation.13 | async-start | bytes 2621440 | tf_op jit(solution)/shard_map/reduce_scatter | solution.py:631
  155.1 5.9 %collective-permute-start.25 = (bf16[4,128,1024]{2,1,0:T(8,128)(2,1)}, bf16[4,128,1024]{2,1,0:T(8,128)(2,1)}, u32[]{:S(2)}, u32[]{:S(2)}) collective-permute-start(bf16[4,128,1024]{2,1,0:T(8,128)(2,1)} %pad_maximum_fusion.1), channel_id=1, source_target_pairs={{0,1},{1,0},{2,3},{3,2},{4,5},{5,4},{6,7},{7,6},{8,9},{9,8},{10,11... | collective-permute-start | bytes 3145736 | tf_op jit(solution)/shard_map/ppermute | solution.py:422
  157.5 10.3 %all-to-all-start.4 = ((bf16[8,128,128]{2,1,0:T(8,128)(2,1)}), bf16[8,128,128]{2,1,0:T(8,128)(2,1)S(1)}, u32[]{:S(2)}, u32[]{:S(2)}) async-start(bf16[8,128,128]{2,1,0:T(8,128)(2,1)} %bitcast.143), calls=%async_computation.4 | async-start | bytes 524288 | tf_op jit(solution)/shard_map/all_to_all | solution.py:468
  180.6 2.9 %collective-permute-start.26 = (bf16[512,1024]{1,0:T(8,128)(2,1)}, bf16[512,1024]{1,0:T(8,128)(2,1)S(1)}, u32[]{:S(2)}, u32[]{:S(2)}) collective-permute-start(bf16[512,1024]{1,0:T(8,128)(2,1)} %get-tuple-element.38), channel_id=1, source_target_pairs={{0,1},{1,0},{2,3},{3,2},{4,5},{5,4},{6,7},{7,6},{8,9},{9,8},{10,11... | collective-permute-start | bytes 3145736 | tf_op jit(solution)/shard_map/ppermute | solution.py:422
  186.2 20.8 %all-to-all-start.5 = ((bf16[4,128,1024]{2,1,0:T(8,128)(2,1)}), bf16[4,128,1024]{2,1,0:T(8,128)(2,1)S(1)}, u32[]{:S(2)}, u32[]{:S(2)}) async-start(bf16[4,128,1024]{2,1,0:T(8,128)(2,1)} %bitcast.33), calls=%async_computation.6 | async-start | bytes 2097152 | tf_op jit(solution)/shard_map/all_to_all | solution.py:452
  189.7 64.2 %reduce-scatter.3.cloned.1.call-start = ((), (), s32[]{:S(2)}) async-start(), calls=%async_computation.12 | async-start | bytes 2359296 | tf_op jit(solution)/shard_map/reduce_scatter | solution.py:647
  194.5 28.6 %collective-permute-start.27 = (bf16[8,32,384]{2,1,0:T(8,128)(2,1)}, bf16[8,32,384]{2,1,0:T(8,128)(2,1)}, u32[]{:S(2)}, u32[]{:S(2)}) collective-permute-start(bf16[8,32,384]{2,1,0:T(8,128)(2,1)} %get-tuple-element.80), channel_id=1, source_target_pairs={{0,8},{1,9},{2,10},{3,11},{4,12},{5,13},{6,14},{7,15},{8,16},{9,17... | collective-permute-start | bytes 589832 | tf_op jit(solution)/shard_map/ppermute | solution.py:426
  196.0 27.7 %collective-permute-start.29 = (bf16[8,32,384]{2,1,0:T(8,128)(2,1)}, bf16[8,32,384]{2,1,0:T(8,128)(2,1)}, u32[]{:S(2)}, u32[]{:S(2)}) collective-permute-start(bf16[8,32,384]{2,1,0:T(8,128)(2,1)} %get-tuple-element.81), channel_id=1, source_target_pairs={{0,24},{1,25},{2,26},{3,27},{4,28},{5,29},{6,30},{7,31},{8,0},{9,1... | collective-permute-start | bytes 589832 | tf_op jit(solution)/shard_map/ppermute | solution.py:426
  198.4 25.3 %collective-permute-start.28 = (bf16[8,32,384]{2,1,0:T(8,128)(2,1)}, bf16[8,32,384]{2,1,0:T(8,128)(2,1)}, u32[]{:S(2)}, u32[]{:S(2)}) collective-permute-start(bf16[8,32,384]{2,1,0:T(8,128)(2,1)} %get-tuple-element.82), channel_id=1, source_target_pairs={{0,16},{1,17},{2,18},{3,19},{4,20},{5,21},{6,22},{7,23},{8,24},{9,... | collective-permute-start | bytes 589832 | tf_op jit(solution)/shard_map/ppermute | solution.py:426
  209.0 12.8 %all-to-all-start.6 = ((f32[32,1,384]{2,1,0:T(1,128)}), f32[32,1,384]{2,1,0:T(1,128)S(1)}, u32[]{:S(2)}, u32[]{:S(2)}) async-start(f32[32,1,384]{2,1,0:T(1,128)} %copy.89), calls=%async_computation.7 | async-start | bytes 98304 | tf_op jit(solution)/shard_map/all_to_all | solution.py:680
  217.2 12.2 %collective-permute-start.30 = (bf16[128,1024]{1,0:T(8,128)(2,1)}, bf16[128,1024]{1,0:T(8,128)(2,1)S(1)}, u32[]{:S(2)}, u32[]{:S(2)}) collective-permute-start(bf16[128,1024]{1,0:T(8,128)(2,1)} %get-tuple-element.75), channel_id=1, source_target_pairs={{0,6},{1,7},{2,4},{3,5},{4,2},{5,3},{6,0},{7,1},{8,14},{9,15},{10,... | collective-permute-start | bytes 786440 | tf_op jit(solution)/shard_map/ppermute | solution.py:422
  219.9 17.2 %collective-permute-start.32 = (bf16[128,1024]{1,0:T(8,128)(2,1)}, bf16[128,1024]{1,0:T(8,128)(2,1)}, u32[]{:S(2)}, u32[]{:S(2)}) collective-permute-start(bf16[128,1024]{1,0:T(8,128)(2,1)} %get-tuple-element.76), channel_id=1, source_target_pairs={{0,4},{1,5},{2,6},{3,7},{4,0},{5,1},{6,2},{7,3},{8,12},{9,13},{10,... | collective-permute-start | bytes 786440 | tf_op jit(solution)/shard_map/ppermute | solution.py:422
  223.1 15.5 %collective-permute-start.31 = (bf16[128,1024]{1,0:T(8,128)(2,1)}, bf16[128,1024]{1,0:T(8,128)(2,1)S(1)}, u32[]{:S(2)}, u32[]{:S(2)}) collective-permute-start(bf16[128,1024]{1,0:T(8,128)(2,1)} %get-tuple-element.77), channel_id=1, source_target_pairs={{0,2},{1,3},{2,0},{3,1},{4,6},{5,7},{6,4},{7,5},{8,10},{9,11},{10,... | collective-permute-start | bytes 786440 | tf_op jit(solution)/shard_map/ppermute | solution.py:422
  225.8 23.7 %all-to-all-start.7 = ((bf16[8,32,896]{2,1,0:T(8,128)(2,1)}), bf16[8,32,896]{2,1,0:T(8,128)(2,1)S(1)}, u32[]{:S(2)}, u32[]{:S(2)}) async-start(bf16[8,32,896]{2,1,0:T(8,128)(2,1)} %pad_maximum_fusion.2), calls=%async_computation.9 | async-start | bytes 917504 | tf_op jit(solution)/shard_map/all_to_all | solution.py:468
  239.7 6.2 %collective-permute-start.33 = (bf16[32,1024]{1,0:T(8,128)(2,1)S(1)}, bf16[32,1024]{1,0:T(8,128)(2,1)S(1)}, u32[]{:S(2)}, u32[]{:S(2)}) collective-permute-start(bf16[32,1024]{1,0:T(8,128)(2,1)S(1)} %get-tuple-element.85), channel_id=1, source_target_pairs={{0,8},{1,9},{2,10},{3,11},{4,12},{5,13},{6,14},{7,15},{8,16},{9,17... | collective-permute-start | bytes 196616 | tf_op jit(solution)/shard_map/ppermute | solution.py:426
  241.2 5.4 %collective-permute-start.35 = (bf16[32,1024]{1,0:T(8,128)(2,1)S(1)}, bf16[32,1024]{1,0:T(8,128)(2,1)S(1)}, u32[]{:S(2)}, u32[]{:S(2)}) collective-permute-start(bf16[32,1024]{1,0:T(8,128)(2,1)S(1)} %get-tuple-element.86), channel_id=1, source_target_pairs={{0,24},{1,25},{2,26},{3,27},{4,28},{5,29},{6,30},{7,31},{8,0},{9,1... | collective-permute-start | bytes 196616 | tf_op jit(solution)/shard_map/ppermute | solution.py:426
  243.6 5.2 %collective-permute-start.34 = (bf16[32,1024]{1,0:T(8,128)(2,1)S(1)}, bf16[32,1024]{1,0:T(8,128)(2,1)S(1)}, u32[]{:S(2)}, u32[]{:S(2)}) collective-permute-start(bf16[32,1024]{1,0:T(8,128)(2,1)S(1)} %get-tuple-element.87), channel_id=1, source_target_pairs={{0,16},{1,17},{2,18},{3,19},{4,20},{5,21},{6,22},{7,23},{8,24},{9,... | collective-permute-start | bytes 196616 | tf_op jit(solution)/shard_map/ppermute | solution.py:426
  (45 other events, 487.4 us)
Sparse Core Ops, SparseCore 0:
  11.0 77.1 all-gather.2
  89.8 26.2 all-gather.4
  142.2 43.7 reduce-scatter.4
  204.1 49.6 reduce-scatter.2

commit v3 on v2

--- a/solution.py
+++ b/solution.py
@@ -94,24 +94,31 @@
             piece = pieces_ref[:, part * own_rows : (part + 1) * own_rows, :]
             weight_ref[:, part * width : (part + 1) * width] = piece.reshape(-1, width)
 
-    pick_block(step, token_refs, block_ref)
+    rows = block_ref.shape[0] // 2
+    pick_block(step, token_refs[0::2], block_ref.at[pl.ds(0, rows)])
+    pick_block(step, token_refs[1::2], block_ref.at[pl.ds(rows, rows)])
     normed, _ = norm_rows(block_ref[...].astype(WIDE))
     hidden = (normed * gain_ref[...] + offset_ref[...]).astype(LOW)
     normed_ref[...] = normed.astype(LOW)
     hidden_ref[...] = hidden
     packed = (plain_dot(hidden, weight_ref[...]) + bias_ref[...]).astype(LOW)
     packed_ref[...] = packed
-    key, value = packed[:, width : 2 * width], packed[:, 2 * width :]
-    allowed = allowed_ref[0] > 0
-    total = None
-    for mask in head_masks():
-        weights = softmax_rows(packed[:, :width] * mask, key, allowed).astype(LOW)
-        term = plain_dot(weights, value * mask)
-        total = term if total is None else total + term
-    out_ref[...] = total.astype(LOW)
+    odd = (place_ref[0] >> 1) & 1
+    for block in range(2):
+        part = packed[block * rows : (block + 1) * rows]
+        query, key, value = (part[:, k * width : (k + 1) * width] for k in range(3))
+        allowed = allowed_ref[odd ^ block, 0] > 0
+        total = None
+        for mask in head_masks():
+            weights = softmax_rows(query * mask, key, allowed).astype(LOW)
+            term = plain_dot(weights, value * mask)
+            total = term if total is None else total + term
+        out_ref[odd ^ block, 0] = total.astype(LOW)
 
 
 def attention_back_kernel(
+    place_ref,
+    earlier_ref,
     packed_ref,
     grad_ref,
     allowed_ref,
@@ -124,16 +131,17 @@
     bias_sums_ref,
 ):
     masks = head_masks()
-    rows = allowed_ref.shape[1]
+    rows = allowed_ref.shape[2]
     width = 2 * HEAD_DIM
     scale = 1.0 / math.sqrt(HEAD_DIM)
-    for block in range(allowed_ref.shape[0]):
+    odd = (place_ref[0] >> 1) & 1
+    for block in range(2):
         part = pl.ds(block * rows, rows)
         query = packed_ref[part, :width]
         key = packed_ref[part, width : 2 * width]
         value = packed_ref[part, 2 * width :]
-        grad = grad_ref[part, :]
-        allowed = allowed_ref[block] > 0
+        grad = grad_ref[odd ^ block, 0]
+        allowed = allowed_ref[odd ^ block, 0] > 0
         sums = [None, None, None]
         for mask in masks:
             query_head = query * mask
@@ -171,17 +179,26 @@
         norm_sums_ref[...] += norm_sums
         bias_sums_ref[...] += bias_sums
 
-    @pl.when(step < pl.num_programs(0) // 2)
-    def _():
-        near_ref[...] = hidden
-
-    @pl.when(step >= pl.num_programs(0) // 2)
-    def _():
-        far_ref[...] = hidden
-
-
-def block_place(i, place_ref):
-    return place_ref[0] ^ (((i & 3) << 1) | (i >> 2))
+    store_pair(step, odd, hidden, near_ref, far_ref)
+
+
+def store_pair(step, odd, pair, near_ref, far_ref):
+    rows = pair.shape[0] // 2
+    first = pl.ds(pl.multiple_of(odd * rows, rows), rows)
+    second = pl.ds(pl.multiple_of((1 - odd) * rows, rows), rows)
+    half = pl.num_programs(0) // 2
+    for ref, wanted in ((near_ref, step < half), (far_ref, step >= half)):
+
+        @pl.when(wanted)
+        def _(ref=ref):
+            ref[first, :] = pair[:rows]
+            ref[second, :] = pair[rows:]
+
+
+def pair_spec(rows, columns):
+    return pl.BlockSpec(
+        (2, 1, rows, columns), lambda i, p: ((p[0] >> 2) ^ (i & 1), (p[0] & 1) ^ (i >> 1), 0, 0)
+    )
 
 
 def fixed(shape):
@@ -196,30 +213,30 @@
         attention_kernel,
         grid_spec=pltpu.PrefetchScalarGridSpec(
             num_scalar_prefetch=1,
-            grid=(count,),
+            grid=(count // 2,),
             in_specs=[fixed((rows, model_width))] * count
             + [
                 fixed((1, model_width)),
                 fixed((1, model_width)),
                 fixed((1, 3 * width)),
                 fixed(pieces.shape),
-                pl.BlockSpec((1, rows, rows), lambda i, p: (block_place(i, p), 0, 0)),
+                pair_spec(rows, rows),
             ],
             out_specs=[
-                pl.BlockSpec((rows, model_width), lambda i, p: (i, 0)),
-                pl.BlockSpec((rows, model_width), lambda i, p: (i, 0)),
-                pl.BlockSpec((rows, 3 * width), lambda i, p: (i, 0)),
+                pl.BlockSpec((2 * rows, model_width), lambda i, p: (i, 0)),
+                pl.BlockSpec((2 * rows, model_width), lambda i, p: (i, 0)),
+                pl.BlockSpec((2 * rows, 3 * width), lambda i, p: (i, 0)),
                 fixed((model_width, 3 * width)),
-                pl.BlockSpec((rows, width), lambda i, p: (block_place(i, p), 0)),
+                pair_spec(rows, width),
             ],
-            scratch_shapes=[pltpu.VMEM((rows, model_width), LOW)],
+            scratch_shapes=[pltpu.VMEM((2 * rows, model_width), LOW)],
         ),
         out_shape=[
             jax.ShapeDtypeStruct((count * rows, model_width), LOW),
             jax.ShapeDtypeStruct((count * rows, model_width), LOW),
             jax.ShapeDtypeStruct((count * rows, 3 * width), LOW),
             jax.ShapeDtypeStruct((model_width, 3 * width), LOW),
-            jax.ShapeDtypeStruct((count * rows, width), LOW),
+            jax.ShapeDtypeStruct((count // 2, 2, rows, width), LOW),
         ],
         compiler_params=pltpu.CompilerParams(vmem_limit_bytes=VMEM_BYTES),
         cost_estimate=pl.CostEstimate(
@@ -227,35 +244,36 @@
             bytes_accessed=count * rows * model_width,
             transcendentals=0,
         ),
-    )(places, *blocks, gain, offset, bias, pieces, allowed)
+    )(places, *blocks, gain, offset, bias, pieces, allowed.reshape(count // 2, 2, rows, rows))
 
 
 def attention_back(packed, grad, allowed, weight, normed, places, earlier):
     blocks, rows, _ = allowed.shape
+    grad = grad.reshape(blocks // 2, 2, rows, -1)
+    allowed = allowed.reshape(blocks // 2, 2, rows, rows)
     width = 2 * HEAD_DIM
     model_width = weight.shape[0]
     half = blocks // 2
     return pl.pallas_call(
-        lambda place_ref, a_ref, *refs: attention_back_kernel(*refs),
+        attention_back_kernel,
         grid_spec=pltpu.PrefetchScalarGridSpec(
             num_scalar_prefetch=1,
-            grid=(blocks,),
+            grid=(blocks // 2,),
             in_specs=[
                 pl.BlockSpec(memory_space=pl.ANY),
-                pl.BlockSpec((rows, 3 * width), lambda i, p: (i, 0)),
-                pl.BlockSpec((rows, width), lambda i, p: (block_place(i, p), 0)),
-                pl.BlockSpec((1, rows, rows), lambda i, p: (block_place(i, p), 0, 0)),
+                pl.BlockSpec((2 * rows, 3 * width), lambda i, p: (i, 0)),
+                pair_spec(rows, width),
+                pair_spec(rows, rows),
                 pl.BlockSpec((model_width, 3 * width), lambda i, p: (0, 0)),
-                pl.BlockSpec((rows, model_width), lambda i, p: (i, 0)),
+                pl.BlockSpec((2 * rows, model_width), lambda i, p: (i, 0)),
             ],
             out_specs=[
-                pl.BlockSpec((rows, 3 * width), lambda i, p: (i, 0)),
+                pl.BlockSpec((2 * rows, 3 * width), lambda i, p: (i, 0)),
                 pl.BlockSpec(
-                    (rows, model_width), lambda i, p: ((p[0] >> 1) ^ jnp.minimum(i, half - 1), 0)
+                    (2 * rows, model_width), lambda i, p: ((p[0] >> 2) ^ jnp.minimum(i, 1), 0)
                 ),
                 pl.BlockSpec(
-                    (rows, model_width),
-                    lambda i, p: ((p[0] >> 1) ^ (jnp.maximum(i, half) - half), 0),
+                    (2 * rows, model_width), lambda i, p: ((p[0] >> 2) ^ (jnp.maximum(i, 2) - 2), 0)
                 ),
                 pl.BlockSpec((2, model_width), lambda i, p: (0, 0)),
                 pl.BlockSpec((1, 3 * width), lambda i, p: (0, 0)),
@@ -318,18 +336,7 @@
         sums_ref[...] += sums
 
     hidden = right_dot(grad_pre, up_ref[...]).astype(LOW)
-    odd = (place_ref[0] >> 1) & 1
-    first = pl.ds(pl.multiple_of(odd * rows, rows), rows)
-    second = pl.ds(pl.multiple_of((1 - odd) * rows, rows), rows)
-    for ref, wanted in (
-        (near_ref, step < pl.num_programs(0) // 2),
-        (far_ref, step >= pl.num_programs(0) // 2),
-    ):
-
-        @pl.when(wanted)
-        def _(ref=ref):
-            ref[first, :] = hidden[:rows]
-            ref[second, :] = hidden[rows:]
+    store_pair(step, (place_ref[0] >> 1) & 1, hidden, near_ref, far_ref)
 
 
 def feed_forward(inputs, grads, up_parts, down, bias, places):

time: 264 us -> 262 us (level)
  Pallas kernels: 41.1 us -> 37.4 us
    unnamed x96 -> x95, local copies, waits for them, and re-layouts: 6.91 us -> 6.91 us
  transfers between devices with their start and end apart: 48 -> 48, of which waited for: 18 -> 18; matrix products, arithmetic and copies ran while one was open for 22% -> 22% of each run, Pallas kernels for 11% -> 10%
where the time goes in v3:
time: 262 us; the launch traced here: 260 us
  waiting for transfers between devices  76.3 us (29%)
  starting transfers between devices  63.5 us (24%)
  Pallas kernels  37.4 us (14%)
  local copies, waits for them, and re-layouts  27.8 us (11%)
  other arithmetic  23.5 us (9%)
  between operations  18.7 us (7%)
  matrix products  13.2 us (5%)
    ppermute x27, waiting for transfers between devices, swap(): return lax.ppermute(array, 'dp', [(i, i ^ flip) for i in range(self.count)])  39.3 us
    ppermute x27, starting transfers between devices, swap(): return lax.ppermute(array, 'dp', [(i, i ^ flip) for i in range(self.count)])  17.2 us
    all_to_all x4, starting transfers between devices, exchange(): lax.all_to_all(parts, 'dp', 0, 0, axis_index_groups=self.group_lists(), t...  15.7 us
    ppermute x9, starting transfers between devices, shift(): lax.ppermute(array, 'dp', [(i, (i + hop) % self.count) for i in range(sel...  13.6 us
    dot_general x7, matrix products, dot(): lax.dot_general(first, second, (dims, ((), ())), preferred_element_type=j...  13.2 us
    ppermute x9, waiting for transfers between devices, shift(): lax.ppermute(array, 'dp', [(i, (i + hop) % self.count) for i in range(sel...  12.5 us
    pallas_call x1, Pallas kernels, feed_forward(): pl.pallas_call(feed_kernel, grid_spec=pltpu.PrefetchScalarGridSpec(num_sc...  11.7 us
    all_to_all x4, waiting for transfers between devices, exchange(): lax.all_to_all(parts, 'dp', 0, 0, axis_index_groups=self.group_lists(), t...  10.6 us
  transfers between devices with their start and end apart: 48, of which 18 were waited for; matrix products, arithmetic and copies ran while one was open for 22% of the time, Pallas kernels for 10%

profile of v3, /device:TPU:0, one launch (start us, length us, event | category | flops | bytes accessed | tf_op | source)
XLA Modules:
  0.0 260.4 jit_solution(3836836794883439314)
XLA Ops:
  9.9 5.2 %all-to-all-start = ((bf16[8,32,512]{2,1,0:T(8,128)(2,1)}), bf16[8,32,512]{2,1,0:T(8,128)(2,1)S(1)}, u32[]{:S(2)}, u32[]{:S(2)}) async-start(bf16[8,32,512]{2,1,0:T(8,128)(2,1)} %reshape.437), calls=%async_computation | async-start | bytes 524288 | tf_op jit(solution)/shard_map/all_to_all | solution.py:475
  15.4 6.6 %all-to-all-done.refs_16_ = bf16[8,32,512]{2,1,0:T(8,128)(2,1)S(1)} async-done(((bf16[8,32,512]{2,1,0:T(8,128)(2,1)}), bf16[8,32,512]{2,1,0:T(8,128)(2,1)S(1)}, u32[]{:S(2)}, u32[]{:S(2)}) %all-to-all-start) | async-done | bytes 262176 | tf_op jit(solution)/shard_map/all_to_all | solution.py:475
  24.3 4.0 %all-to-all-start.1 = ((bf16[32,104,128]{2,1,0:T(8,128)(2,1)}), bf16[32,104,128]{2,1,0:T(8,128)(2,1)S(1)}, u32[]{:S(2)}, u32[]{:S(2)}) async-start(bf16[32,104,128]{2,1,0:T(8,128)(2,1)} %bitcast.10), calls=%async_computation.1 | async-start | bytes 1703936 | tf_op jit(solution)/shard_map/all_to_all | solution.py:561
  28.3 2.7 %collective-permute-start.2 = (bf16[128,1024]{1,0:T(8,128)(2,1)S(1)}, bf16[128,1024]{1,0:T(8,128)(2,1)S(1)}, u32[]{:S(2)}, u32[]{:S(2)}) collective-permute-start(bf16[128,1024]{1,0:T(8,128)(2,1)S(1)} %copy-done), channel_id=1, source_target_pairs={{0,6},{1,7},{2,4},{3,5},{4,2},{5,3},{6,0},{7,1},{8,14},{9,15},{10,... | collective-permute-start | bytes 786440 | tf_op jit(solution)/shard_map/ppermute | solution.py:429
  32.0 2.7 %collective-permute-start.19 = (bf16[128,1024]{1,0:T(8,128)(2,1)S(1)}, bf16[128,1024]{1,0:T(8,128)(2,1)S(1)}, u32[]{:S(2)}, u32[]{:S(2)}) collective-permute-start(bf16[128,1024]{1,0:T(8,128)(2,1)S(1)} %get-tuple-element.64.refs_8_), channel_id=1, source_target_pairs={{0,6},{1,7},{2,4},{3,5},{4,2},{5,3},{6,0},{7,1},{8,14},{9,15},{10,... | collective-permute-start | bytes 786440 | tf_op jit(solution)/shard_map/ppermute | solution.py:429
  35.4 12.5 %collective-permute-done.2.refs_3_ = bf16[128,1024]{1,0:T(8,128)(2,1)S(1)} collective-permute-done((bf16[128,1024]{1,0:T(8,128)(2,1)S(1)}, bf16[128,1024]{1,0:T(8,128)(2,1)S(1)}, u32[]{:S(2)}, u32[]{:S(2)}) %collective-permute-start.2) | collective-permute-done | bytes 262176 | tf_op jit(solution)/shard_map/ppermute | solution.py:429
  47.9 4.8 %collective-permute-done.1.refs_2_ = bf16[128,1024]{1,0:T(8,128)(2,1)S(1)} collective-permute-done((bf16[128,1024]{1,0:T(8,128)(2,1)S(1)}, bf16[128,1024]{1,0:T(8,128)(2,1)S(1)}, u32[]{:S(2)}, u32[]{:S(2)}) %collective-permute-start.1) | collective-permute-done | bytes 262176 | tf_op jit(solution)/shard_map/ppermute | solution.py:429
  55.6 1.6 collective-permute-start.18
  57.2 3.6 %collective-permute-start.9 = (bf16[8,32,512]{2,1,0:T(8,128)(2,1)S(1)}, bf16[8,32,512]{2,1,0:T(8,128)(2,1)S(1)}, u32[]{:S(2)}, u32[]{:S(2)}) collective-permute-start(bf16[8,32,512]{2,1,0:T(8,128)(2,1)S(1)} %all-to-all-done.refs_16_), channel_id=1, source_target_pairs={{0,24},{1,25},{2,26},{3,27},{4,28},{5,29},{6,30},{7,31},{8,0},{9,1... | collective-permute-start | bytes 786440 | tf_op jit(solution)/shard_map/ppermute | solution.py:433
  60.9 1.6 collective-permute-start.7
  64.4 9.9 %shard_map.263 = (bf16[1024,1024]{1,0:T(8,128)(2,1)}, bf16[1024,1024]{1,0:T(8,128)(2,1)}, bf16[1024,384]{1,0:T(8,128)(2,1)}, bf16[1024,384]{1,0:T(8,128)(2,1)}, bf16[4,2,128,128]{3,2,1,0:T(8,128)(2,1)}) custom-call(s32[2]{0:T(128)} %pad_add_fusion.place_ref, bf16[128,1024]{1,0:T(8,128)(2,1)} %refs_0_.1, bf16[128,1024]{1,0:T(8,128)(2,1)} %copy-done.22, ...), custom_call_target="tpu_custom_call" | custom-call | flops 134217728 | bytes 1048576 | tf_op jit(solution)/shard_map/pallas_call | solution.py:212
  74.3 1.8 copy.77
  76.1 3.4 %all-to-all-start.2 = ((bf16[8,128,128]{1,2,0:T(8,128)(2,1)}), bf16[8,128,128]{1,2,0:T(8,128)(2,1)S(1)}, u32[]{:S(2)}, u32[]{:S(2)}) async-start(bf16[8,128,128]{1,2,0:T(8,128)(2,1)} %copy.77), calls=%async_computation.2 | async-start | bytes 524288 | tf_op jit(solution)/shard_map/all_to_all | solution.py:475
  80.3 9.5 %collective-permute-done.8.refs_18_ = bf16[8,32,512]{2,1,0:T(8,128)(2,1)S(1)} collective-permute-done((bf16[8,32,512]{2,1,0:T(8,128)(2,1)S(1)}, bf16[8,32,512]{2,1,0:T(8,128)(2,1)S(1)}, u32[]{:S(2)}, u32[]{:S(2)}) %collective-permute-start.8) | collective-permute-done | bytes 262176 | tf_op jit(solution)/shard_map/ppermute | solution.py:433
  95.3 2.2 fusion.40
  98.0 1.4 collective-permute-start.12
  99.4 1.7 collective-permute-start.11
  102.0 6.2 %collective-permute-done.12.refs_3_ = bf16[128,1024]{1,0:T(8,128)(2,1)} collective-permute-done((bf16[128,1024]{1,0:T(8,128)(2,1)S(1)}, bf16[128,1024]{1,0:T(8,128)(2,1)}, u32[]{:S(2)}, u32[]{:S(2)}) %collective-permute-start.12) | collective-permute-done | bytes 262176 | tf_op jit(solution)/shard_map/ppermute | solution.py:429
  108.2 4.8 %collective-permute-done.11.refs_2_ = bf16[128,1024]{1,0:T(8,128)(2,1)} collective-permute-done((bf16[128,1024]{1,0:T(8,128)(2,1)S(1)}, bf16[128,1024]{1,0:T(8,128)(2,1)}, u32[]{:S(2)}, u32[]{:S(2)}) %collective-permute-start.11) | collective-permute-done | bytes 262176 | tf_op jit(solution)/shard_map/ppermute | solution.py:429
  114.1 1.9 all-gather.5.cloned.1.call-done.refs_20_.down_ref
  116.8 11.7 %shard_map.264 = (bf16[1024,1024]{1,0:T(8,128)(2,1)}, bf16[1024,1024]{1,0:T(8,128)(2,1)}, bf16[1024,512]{1,0:T(8,128)(2,1)}, bf16[1024,512]{1,0:T(8,128)(2,1)}, ...) custom-call(s32[2]{0:T(128)} %pad_add_fusion.place_ref, bf16[128,1024]{1,0:T(8,128)(2,1)} %copy-done.10, ...), custom_call_target="tpu_custom_call" | custom-call | flops 536870912 | bytes 1048576 | tf_op jit(solution)/shard_map/pallas_call | solution.py:349
  128.6 3.1 %convolution_convert_fusion.3 = bf16[512,512]{1,0:T(8,128)(2,1)} fusion(bf16[1024,512]{1,0:T(8,128)(2,1)} %get-tuple-element.39.act_ref, bf16[1024,1024]{1,0:T(8,128)(2,1)} %get-tuple-element.47), kind=kOutput, calls=%fused_computation.10 | convolution fusion | flops 537133056 | bytes 2621440 | tf_op jit(solution)/shard_map/dot_general | solution.py:47
  131.7 1.4 add_convert_fusion.2
  133.1 3.8 %all-to-all-start.3 = ((bf16[4,128,1024]{2,1,0:T(8,128)(2,1)}), bf16[4,128,1024]{2,1,0:T(8,128)(2,1)S(1)}, u32[]{:S(2)}, u32[]{:S(2)}) async-start(bf16[4,128,1024]{2,1,0:T(8,128)(2,1)} %bitcast.21), calls=%async_computation.3 | async-start | bytes 2097152 | tf_op jit(solution)/shard_map/all_to_all | solution.py:459
  137.0 2.1 convolution_convert_fusion.4
  140.5 1.5 pad_maximum_fusion
  142.0 9.2 %all-to-all-done.3 = bf16[4,128,1024]{2,1,0:T(8,128)(2,1)S(1)} async-done(((bf16[4,128,1024]{2,1,0:T(8,128)(2,1)}), bf16[4,128,1024]{2,1,0:T(8,128)(2,1)S(1)}, u32[]{:S(2)}, u32[]{:S(2)}) %all-to-all-start.3) | async-done | bytes 1048608 | tf_op jit(solution)/shard_map/all_to_all | solution.py:459
  157.5 3.4 %all-to-all-start.4 = ((bf16[8,128,128]{2,1,0:T(8,128)(2,1)}), bf16[8,128,128]{2,1,0:T(8,128)(2,1)S(1)}, u32[]{:S(2)}, u32[]{:S(2)}) async-start(bf16[8,128,128]{2,1,0:T(8,128)(2,1)} %bitcast.141), calls=%async_computation.4 | async-start | bytes 524288 | tf_op jit(solution)/shard_map/all_to_all | solution.py:475
  161.0 2.9 %add_convert_fusion.1.earlier_ref = bf16[4,128,1024]{2,1,0:T(8,128)(2,1)} fusion(bf16[4,128,1024]{2,1,0:T(8,128)(2,1)} %collective-permute-done.25, bf16[1,128,1024]{2,1,0:T(8,128)(2,1)} %bitcast.146, bf16[1,128,1024]{2,1,0:T(8,128)(2,1)} %bitcast.148, bf16[1,128,1024]{2,1,0:T(8,128)(2,1)} %bitcast.150, bf16[1,128,1024]{2,1,0:T(8,128)(2,1)} %bitcast.144), kind=kLoop, calls=%fused_computation.5 | loop fusion | flops 3670016 | bytes 3145728 | tf_op jit(solution)/shard_map/convert_element_type | solution.py:443
  163.9 4.0 %all-to-all-done.4 = bf16[8,128,128]{2,1,0:T(8,128)(2,1)S(1)} async-done(((bf16[8,128,128]{2,1,0:T(8,128)(2,1)}), bf16[8,128,128]{2,1,0:T(8,128)(2,1)S(1)}, u32[]{:S(2)}, u32[]{:S(2)}) %all-to-all-start.4) | async-done | bytes 262176 | tf_op jit(solution)/shard_map/all_to_all | solution.py:475
  168.5 10.3 %shard_map.265 = (bf16[1024,384]{1,0:T(8,128)(2,1)}, bf16[512,1024]{1,0:T(8,128)(2,1)}, bf16[512,1024]{1,0:T(8,128)(2,1)}, f32[2,1024]{1,0:T(2,128)}, f32[1,384]{1,0:T(1,128)}) custom-call(s32[2]{0:T(128)} %pad_add_fusion.place_ref, bf16[4,128,1024]{2,1,0:T(8,128)(2,1)} %add_convert_fusion.1.earlier_ref, bf16[1024,384]{1,0:T(8,128)(2,1)} %get-tuple-element.34.packed_ref, ...), custom_call_target="tpu_custom_call" | custom-call | flops 335544320 | bytes 2097152 | tf_op jit(solution)/shard_map/pallas_call | solution.py:257
  181.7 2.7 %add_convert_fusion.earlier_ref = bf16[512,1024]{1,0:T(8,128)(2,1)} fusion(bf16[512,1024]{1,0:T(8,128)(2,1)S(1)} %collective-permute-done.26, bf16[512,1024]{1,0:T(8,128)(2,1)} %get-tuple-element.37), kind=kLoop, calls=%fused_computation.4 | loop fusion | flops 2097152 | bytes 3145728 | tf_op jit(solution)/shard_map/convert_element_type | solution.py:443
  184.4 3.5 %all-to-all-start.5 = ((bf16[4,128,1024]{2,1,0:T(8,128)(2,1)}), bf16[4,128,1024]{2,1,0:T(8,128)(2,1)S(1)}, u32[]{:S(2)}, u32[]{:S(2)}) async-start(bf16[4,128,1024]{2,1,0:T(8,128)(2,1)} %bitcast.33), calls=%async_computation.6 | async-start | bytes 2097152 | tf_op jit(solution)/shard_map/all_to_all | solution.py:459
  188.2 2.9 %convolution_convert_fusion.2 = bf16[1024,384]{1,0:T(8,128)(2,1)S(1)} fusion(bf16[1024,1024]{1,0:T(8,128)(2,1)} %get-tuple-element.43, bf16[1024,384]{1,0:T(8,128)(2,1)S(1)} %copy-done.44), kind=kOutput, calls=%fused_computation.9 | convolution fusion | flops 805699584 | bytes 3670016 | tf_op jit(solution)/shard_map/dot_general | solution.py:47
  192.8 1.5 collective-permute-start.27
  194.3 2.4 collective-permute-start.29
  196.8 5.5 %shard_map.266 = bf16[1024,1024]{1,0:T(8,128)(2,1)} custom-call(s32[2]{0:T(128)} %pad_add_fusion.place_ref, bf16[512,1024]{1,0:T(8,128)(2,1)} %add_convert_fusion.earlier_ref, bf16[1024,512]{1,0:T(8,128)(2,1)} %get-tuple-element.39.act_ref, bf16[512,1024]{1,0:T(8,128)(2,1)} %all-gather.5.cloned.1.call-done.refs_20_.down_ref), custom_call_target="tpu_custom_call" | custom-call | tf_op jit(solution)/shard_map/pallas_call | solution.py:400
  202.3 1.8 fusion.36
  207.3 5.5 %all-to-all-start.6 = ((f32[32,1,384]{2,1,0:T(1,128)}), f32[32,1,384]{2,1,0:T(1,128)S(1)}, u32[]{:S(2)}, u32[]{:S(2)}) async-start(f32[32,1,384]{2,1,0:T(1,128)} %copy.89), calls=%async_computation.7 | async-start | bytes 98304 | tf_op jit(solution)/shard_map/all_to_all | solution.py:687
  212.8 1.8 broadcast_add_fusion
  215.5 2.7 %collective-permute-start.30 = (bf16[128,1024]{1,0:T(8,128)(2,1)}, bf16[128,1024]{1,0:T(8,128)(2,1)S(1)}, u32[]{:S(2)}, u32[]{:S(2)}) collective-permute-start(bf16[128,1024]{1,0:T(8,128)(2,1)} %get-tuple-element.75), channel_id=1, source_target_pairs={{0,6},{1,7},{2,4},{3,5},{4,2},{5,3},{6,0},{7,1},{8,14},{9,15},{10,... | collective-permute-start | bytes 786440 | tf_op jit(solution)/shard_map/ppermute | solution.py:429
  224.1 3.7 %all-to-all-start.7 = ((bf16[8,32,896]{2,1,0:T(8,128)(2,1)}), bf16[8,32,896]{2,1,0:T(8,128)(2,1)S(1)}, u32[]{:S(2)}, u32[]{:S(2)}) async-start(bf16[8,32,896]{2,1,0:T(8,128)(2,1)} %pad_maximum_fusion.2), calls=%async_computation.9 | async-start | bytes 917504 | tf_op jit(solution)/shard_map/all_to_all | solution.py:475
  227.7 7.6 %collective-permute-done.32 = bf16[128,1024]{1,0:T(8,128)(2,1)} collective-permute-done((bf16[128,1024]{1,0:T(8,128)(2,1)}, bf16[128,1024]{1,0:T(8,128)(2,1)}, u32[]{:S(2)}, u32[]{:S(2)}) %collective-permute-start.32) | collective-permute-done | bytes 262176 | tf_op jit(solution)/shard_map/ppermute | solution.py:429
  235.4 1.5 collective-permute-done.31
  238.0 1.5 collective-permute-start.33
  239.5 2.4 collective-permute-start.35
  244.9 2.2 collective-permute-done.34
  252.1 1.7 add_convert_fusion.3
  (262 shorter events, 49.3 us)
Async XLA Ops:
  7.3 87.9 %all-gather.3.cloned.1.call-start = ((), (), s32[]{:S(2)}) async-start(), calls=%async_computation.10 | async-start | bytes 2162688 | tf_op jit(solution)/shard_map/all_gather | solution.py:562
  9.9 12.1 %all-to-all-start = ((bf16[8,32,512]{2,1,0:T(8,128)(2,1)}), bf16[8,32,512]{2,1,0:T(8,128)(2,1)S(1)}, u32[]{:S(2)}, u32[]{:S(2)}) async-start(bf16[8,32,512]{2,1,0:T(8,128)(2,1)} %reshape.437), calls=%async_computation | async-start | bytes 524288 | tf_op jit(solution)/shard_map/all_to_all | solution.py:475
  24.3 29.5 %all-to-all-start.1 = ((bf16[32,104,128]{2,1,0:T(8,128)(2,1)}), bf16[32,104,128]{2,1,0:T(8,128)(2,1)S(1)}, u32[]{:S(2)}, u32[]{:S(2)}) async-start(bf16[32,104,128]{2,1,0:T(8,128)(2,1)} %bitcast.10), calls=%async_computation.1 | async-start | bytes 1703936 | tf_op jit(solution)/shard_map/all_to_all | solution.py:561
  28.3 19.6 %collective-permute-start.2 = (bf16[128,1024]{1,0:T(8,128)(2,1)S(1)}, bf16[128,1024]{1,0:T(8,128)(2,1)S(1)}, u32[]{:S(2)}, u32[]{:S(2)}) collective-permute-start(bf16[128,1024]{1,0:T(8,128)(2,1)S(1)} %copy-done), channel_id=1, source_target_pairs={{0,6},{1,7},{2,4},{3,5},{4,2},{5,3},{6,0},{7,1},{8,14},{9,15},{10,... | collective-permute-start | bytes 786440 | tf_op jit(solution)/shard_map/ppermute | solution.py:429
  31.1 21.6 %collective-permute-start.1 = (bf16[128,1024]{1,0:T(8,128)(2,1)S(1)}, bf16[128,1024]{1,0:T(8,128)(2,1)S(1)}, u32[]{:S(2)}, u32[]{:S(2)}) collective-permute-start(bf16[128,1024]{1,0:T(8,128)(2,1)S(1)} %copy-done), channel_id=1, source_target_pairs={{0,4},{1,5},{2,6},{3,7},{4,0},{5,1},{6,2},{7,3},{8,12},{9,13},{10,... | collective-permute-start | bytes 786440 | tf_op jit(solution)/shard_map/ppermute | solution.py:429
  31.6 22.3 %collective-permute-start = (bf16[128,1024]{1,0:T(8,128)(2,1)S(1)}, bf16[128,1024]{1,0:T(8,128)(2,1)S(1)}, u32[]{:S(2)}, u32[]{:S(2)}) collective-permute-start(bf16[128,1024]{1,0:T(8,128)(2,1)S(1)} %copy-done), channel_id=1, source_target_pairs={{0,2},{1,3},{2,0},{3,1},{4,6},{5,7},{6,4},{7,5},{8,10},{9,11},{10,... | collective-permute-start | bytes 786440 | tf_op jit(solution)/shard_map/ppermute | solution.py:429
  31.9 23.7 %collective-permute-start.3 = (bf16[128,1024]{1,0:T(8,128)(2,1)S(1)}, bf16[128,1024]{1,0:T(8,128)(2,1)}, u32[]{:S(2)}, u32[]{:S(2)}) collective-permute-start(bf16[128,1024]{1,0:T(8,128)(2,1)S(1)} %copy-done), channel_id=1, source_target_pairs={{0,1},{1,0},{2,3},{3,2},{4,5},{5,4},{6,7},{7,6},{8,9},{9,8},{10,11... | collective-permute-start | bytes 786440 | tf_op jit(solution)/shard_map/ppermute | solution.py:429
  32.0 58.4 %collective-permute-start.19 = (bf16[128,1024]{1,0:T(8,128)(2,1)S(1)}, bf16[128,1024]{1,0:T(8,128)(2,1)S(1)}, u32[]{:S(2)}, u32[]{:S(2)}) collective-permute-start(bf16[128,1024]{1,0:T(8,128)(2,1)S(1)} %get-tuple-element.64.refs_8_), channel_id=1, source_target_pairs={{0,6},{1,7},{2,4},{3,5},{4,2},{5,3},{6,0},{7,1},{8,14},{9,15},{10,... | collective-permute-start | bytes 786440 | tf_op jit(solution)/shard_map/ppermute | solution.py:429
  47.9 9.3 %collective-permute-start.6 = (bf16[128,1024]{1,0:T(8,128)(2,1)S(1)}, bf16[128,1024]{1,0:T(8,128)(2,1)}, u32[]{:S(2)}, u32[]{:S(2)}) collective-permute-start(bf16[128,1024]{1,0:T(8,128)(2,1)S(1)} %collective-permute-done.2.refs_3_), channel_id=1, source_target_pairs={{0,1},{1,0},{2,3},{3,2},{4,5},{5,4},{6,7},{7,6},{8,9},{9,8},{10,11... | collective-permute-start | bytes 786440 | tf_op jit(solution)/shard_map/ppermute | solution.py:429
  52.7 8.2 %collective-permute-start.5 = (bf16[128,1024]{1,0:T(8,128)(2,1)S(1)}, bf16[128,1024]{1,0:T(8,128)(2,1)}, u32[]{:S(2)}, u32[]{:S(2)}) collective-permute-start(bf16[128,1024]{1,0:T(8,128)(2,1)S(1)} %collective-permute-done.1.refs_2_), channel_id=1, source_target_pairs={{0,1},{1,0},{2,3},{3,2},{4,5},{5,4},{6,7},{7,6},{8,9},{9,8},{10,11... | collective-permute-start | bytes 786440 | tf_op jit(solution)/shard_map/ppermute | solution.py:429
  53.9 7.0 %collective-permute-start.4 = (bf16[128,1024]{1,0:T(8,128)(2,1)S(1)}, bf16[128,1024]{1,0:T(8,128)(2,1)}, u32[]{:S(2)}, u32[]{:S(2)}) collective-permute-start(bf16[128,1024]{1,0:T(8,128)(2,1)S(1)} %collective-permute-done.refs_1_), channel_id=1, source_target_pairs={{0,1},{1,0},{2,3},{3,2},{4,5},{5,4},{6,7},{7,6},{8,9},{9,8},{10,11... | collective-permute-start | bytes 786440 | tf_op jit(solution)/shard_map/ppermute | solution.py:429
  55.6 35.2 %collective-permute-start.18 = (bf16[128,1024]{1,0:T(8,128)(2,1)S(1)}, bf16[128,1024]{1,0:T(8,128)(2,1)S(1)}, u32[]{:S(2)}, u32[]{:S(2)}) collective-permute-start(bf16[128,1024]{1,0:T(8,128)(2,1)S(1)} %get-tuple-element.64.refs_8_), channel_id=1, source_target_pairs={{0,4},{1,5},{2,6},{3,7},{4,0},{5,1},{6,2},{7,3},{8,12},{9,13},{10,... | collective-permute-start | bytes 786440 | tf_op jit(solution)/shard_map/ppermute | solution.py:429
  57.2 36.6 %collective-permute-start.9 = (bf16[8,32,512]{2,1,0:T(8,128)(2,1)S(1)}, bf16[8,32,512]{2,1,0:T(8,128)(2,1)S(1)}, u32[]{:S(2)}, u32[]{:S(2)}) collective-permute-start(bf16[8,32,512]{2,1,0:T(8,128)(2,1)S(1)} %all-to-all-done.refs_16_), channel_id=1, source_target_pairs={{0,24},{1,25},{2,26},{3,27},{4,28},{5,29},{6,30},{7,31},{8,0},{9,1... | collective-permute-start | bytes 786440 | tf_op jit(solution)/shard_map/ppermute | solution.py:433
  60.8 29.0 %collective-permute-start.8 = (bf16[8,32,512]{2,1,0:T(8,128)(2,1)S(1)}, bf16[8,32,512]{2,1,0:T(8,128)(2,1)S(1)}, u32[]{:S(2)}, u32[]{:S(2)}) collective-permute-start(bf16[8,32,512]{2,1,0:T(8,128)(2,1)S(1)} %all-to-all-done.refs_16_), channel_id=1, source_target_pairs={{0,16},{1,17},{2,18},{3,19},{4,20},{5,21},{6,22},{7,23},{8,24},{9,... | collective-permute-start | bytes 786440 | tf_op jit(solution)/shard_map/ppermute | solution.py:433
  60.9 30.1 %collective-permute-start.7 = (bf16[8,32,512]{2,1,0:T(8,128)(2,1)S(1)}, bf16[8,32,512]{2,1,0:T(8,128)(2,1)}, u32[]{:S(2)}, u32[]{:S(2)}) collective-permute-start(bf16[8,32,512]{2,1,0:T(8,128)(2,1)S(1)} %all-to-all-done.refs_16_), channel_id=1, source_target_pairs={{0,8},{1,9},{2,10},{3,11},{4,12},{5,13},{6,14},{7,15},{8,16},{9,17... | collective-permute-start | bytes 786440 | tf_op jit(solution)/shard_map/ppermute | solution.py:433
  76.1 19.1 %all-to-all-start.2 = ((bf16[8,128,128]{1,2,0:T(8,128)(2,1)}), bf16[8,128,128]{1,2,0:T(8,128)(2,1)S(1)}, u32[]{:S(2)}, u32[]{:S(2)}) async-start(bf16[8,128,128]{1,2,0:T(8,128)(2,1)} %copy.77), calls=%async_computation.2 | async-start | bytes 524288 | tf_op jit(solution)/shard_map/all_to_all | solution.py:475
  79.6 36.5 %all-gather.5.cloned.1.call-start = ((), (), s32[]{:S(2)}) async-start(), calls=%async_computation.11 | async-start | bytes 1310720 | tf_op jit(solution)/shard_map/all_gather | solution.py:563
  89.8 9.5 %collective-permute-start.20 = (bf16[128,1024]{1,0:T(8,128)(2,1)S(1)}, bf16[128,1024]{1,0:T(8,128)(2,1)S(1)}, u32[]{:S(2)}, u32[]{:S(2)}) collective-permute-start(bf16[128,1024]{1,0:T(8,128)(2,1)S(1)} %get-tuple-element.64.refs_8_), channel_id=1, source_target_pairs={{0,1},{1,0},{2,3},{3,2},{4,5},{5,4},{6,7},{7,6},{8,9},{9,8},{10,11... | collective-permute-start | bytes 786440 | tf_op jit(solution)/shard_map/ppermute | solution.py:429
  90.4 10.7 %collective-permute-start.17 = (bf16[128,1024]{1,0:T(8,128)(2,1)S(1)}, bf16[128,1024]{1,0:T(8,128)(2,1)S(1)}, u32[]{:S(2)}, u32[]{:S(2)}) collective-permute-start(bf16[128,1024]{1,0:T(8,128)(2,1)S(1)} %get-tuple-element.64.refs_8_), channel_id=1, source_target_pairs={{0,2},{1,3},{2,0},{3,1},{4,6},{5,7},{6,4},{7,5},{8,10},{9,11},{10,... | collective-permute-start | bytes 786440 | tf_op jit(solution)/shard_map/ppermute | solution.py:429
  90.8 10.7 %collective-permute-start.23 = (bf16[128,1024]{1,0:T(8,128)(2,1)S(1)}, bf16[128,1024]{1,0:T(8,128)(2,1)S(1)}, u32[]{:S(2)}, u32[]{:S(2)}) collective-permute-start(bf16[128,1024]{1,0:T(8,128)(2,1)S(1)} %collective-permute-done.19.refs_11_), channel_id=1, source_target_pairs={{0,1},{1,0},{2,3},{3,2},{4,5},{5,4},{6,7},{7,6},{8,9},{9,8},{10,11... | collective-permute-start | bytes 786440 | tf_op jit(solution)/shard_map/ppermute | solution.py:429
  91.0 10.6 %collective-permute-start.22 = (bf16[128,1024]{1,0:T(8,128)(2,1)S(1)}, bf16[128,1024]{1,0:T(8,128)(2,1)S(1)}, u32[]{:S(2)}, u32[]{:S(2)}) collective-permute-start(bf16[128,1024]{1,0:T(8,128)(2,1)S(1)} %collective-permute-done.18.refs_10_), channel_id=1, source_target_pairs={{0,1},{1,0},{2,3},{3,2},{4,5},{5,4},{6,7},{7,6},{8,9},{9,8},{10,11... | collective-permute-start | bytes 786440 | tf_op jit(solution)/shard_map/ppermute | solution.py:429
  98.0 10.3 %collective-permute-start.12 = (bf16[128,1024]{1,0:T(8,128)(2,1)S(1)}, bf16[128,1024]{1,0:T(8,128)(2,1)}, u32[]{:S(2)}, u32[]{:S(2)}) collective-permute-start(bf16[128,1024]{1,0:T(8,128)(2,1)S(1)} %add_convert_fusion.4.refs_0_), channel_id=1, source_target_pairs={{0,6},{1,7},{2,4},{3,5},{4,2},{5,3},{6,0},{7,1},{8,14},{9,15},{10,... | collective-permute-start | bytes 786440 | tf_op jit(solution)/shard_map/ppermute | solution.py:429
  99.4 13.6 %collective-permute-start.11 = (bf16[128,1024]{1,0:T(8,128)(2,1)S(1)}, bf16[128,1024]{1,0:T(8,128)(2,1)}, u32[]{:S(2)}, u32[]{:S(2)}) collective-permute-start(bf16[128,1024]{1,0:T(8,128)(2,1)S(1)} %add_convert_fusion.4.refs_0_), channel_id=1, source_target_pairs={{0,4},{1,5},{2,6},{3,7},{4,0},{5,1},{6,2},{7,3},{8,12},{9,13},{10,... | collective-permute-start | bytes 786440 | tf_op jit(solution)/shard_map/ppermute | solution.py:429
  101.1 11.9 %collective-permute-start.10 = (bf16[128,1024]{1,0:T(8,128)(2,1)S(1)}, bf16[128,1024]{1,0:T(8,128)(2,1)}, u32[]{:S(2)}, u32[]{:S(2)}) collective-permute-start(bf16[128,1024]{1,0:T(8,128)(2,1)S(1)} %add_convert_fusion.4.refs_0_), channel_id=1, source_target_pairs={{0,2},{1,3},{2,0},{3,1},{4,6},{5,7},{6,4},{7,5},{8,10},{9,11},{10,... | collective-permute-start | bytes 786440 | tf_op jit(solution)/shard_map/ppermute | solution.py:429
  101.5 12.6 %collective-permute-start.21 = (bf16[128,1024]{1,0:T(8,128)(2,1)S(1)}, bf16[128,1024]{1,0:T(8,128)(2,1)S(1)}, u32[]{:S(2)}, u32[]{:S(2)}) collective-permute-start(bf16[128,1024]{1,0:T(8,128)(2,1)S(1)} %collective-permute-done.17.refs_9_), channel_id=1, source_target_pairs={{0,1},{1,0},{2,3},{3,2},{4,5},{5,4},{6,7},{7,6},{8,9},{9,8},{10,11... | collective-permute-start | bytes 786440 | tf_op jit(solution)/shard_map/ppermute | solution.py:429
  101.5 14.5 %collective-permute-start.13 = (bf16[128,1024]{1,0:T(8,128)(2,1)S(1)}, bf16[128,1024]{1,0:T(8,128)(2,1)S(1)}, u32[]{:S(2)}, u32[]{:S(2)}) collective-permute-start(bf16[128,1024]{1,0:T(8,128)(2,1)S(1)} %add_convert_fusion.4.refs_0_), channel_id=1, source_target_pairs={{0,1},{1,0},{2,3},{3,2},{4,5},{5,4},{6,7},{7,6},{8,9},{9,8},{10,11... | collective-permute-start | bytes 786440 | tf_op jit(solution)/shard_map/ppermute | solution.py:429
  108.2 7.9 %collective-permute-start.16 = (bf16[128,1024]{1,0:T(8,128)(2,1)}, bf16[128,1024]{1,0:T(8,128)(2,1)}, u32[]{:S(2)}, u32[]{:S(2)}) collective-permute-start(bf16[128,1024]{1,0:T(8,128)(2,1)} %collective-permute-done.12.refs_3_), channel_id=1, source_target_pairs={{0,1},{1,0},{2,3},{3,2},{4,5},{5,4},{6,7},{7,6},{8,9},{9,8},{10,11... | collective-permute-start | bytes 786440 | tf_op jit(solution)/shard_map/ppermute | solution.py:429
  113.0 3.0 %collective-permute-start.15 = (bf16[128,1024]{1,0:T(8,128)(2,1)}, bf16[128,1024]{1,0:T(8,128)(2,1)}, u32[]{:S(2)}, u32[]{:S(2)}) collective-permute-start(bf16[128,1024]{1,0:T(8,128)(2,1)} %collective-permute-done.11.refs_2_), channel_id=1, source_target_pairs={{0,1},{1,0},{2,3},{3,2},{4,5},{5,4},{6,7},{7,6},{8,9},{9,8},{10,11... | collective-permute-start | bytes 786440 | tf_op jit(solution)/shard_map/ppermute | solution.py:429
  113.0 3.0 %collective-permute-start.14 = (bf16[128,1024]{1,0:T(8,128)(2,1)}, bf16[128,1024]{1,0:T(8,128)(2,1)}, u32[]{:S(2)}, u32[]{:S(2)}) collective-permute-start(bf16[128,1024]{1,0:T(8,128)(2,1)} %collective-permute-done.10.refs_1_), channel_id=1, source_target_pairs={{0,1},{1,0},{2,3},{3,2},{4,5},{5,4},{6,7},{7,6},{8,9},{9,8},{10,11... | collective-permute-start | bytes 786440 | tf_op jit(solution)/shard_map/ppermute | solution.py:429
  128.5 3.3 %collective-permute-start.24 = (bf16[512,1024]{1,0:T(8,128)(2,1)}, bf16[512,1024]{1,0:T(8,128)(2,1)S(1)}, u32[]{:S(2)}, u32[]{:S(2)}) collective-permute-start(bf16[512,1024]{1,0:T(8,128)(2,1)} %get-tuple-element.33), channel_id=1, source_target_pairs={{0,1},{1,0},{2,3},{3,2},{4,5},{5,4},{6,7},{7,6},{8,9},{9,8},{10,11... | collective-permute-start | bytes 3145736 | tf_op jit(solution)/shard_map/ppermute | solution.py:429
  133.1 18.1 %all-to-all-start.3 = ((bf16[4,128,1024]{2,1,0:T(8,128)(2,1)}), bf16[4,128,1024]{2,1,0:T(8,128)(2,1)S(1)}, u32[]{:S(2)}, u32[]{:S(2)}) async-start(bf16[4,128,1024]{2,1,0:T(8,128)(2,1)} %bitcast.21), calls=%async_computation.3 | async-start | bytes 2097152 | tf_op jit(solution)/shard_map/all_to_all | solution.py:459
  136.9 65.4 %reduce-scatter.5.cloned.1.call-start = ((), (), s32[]{:S(2)}) async-start(), calls=%async_computation.13 | async-start | bytes 2621440 | tf_op jit(solution)/shard_map/reduce_scatter | solution.py:638
  155.1 5.9 %collective-permute-start.25 = (bf16[4,128,1024]{2,1,0:T(8,128)(2,1)}, bf16[4,128,1024]{2,1,0:T(8,128)(2,1)}, u32[]{:S(2)}, u32[]{:S(2)}) collective-permute-start(bf16[4,128,1024]{2,1,0:T(8,128)(2,1)} %pad_maximum_fusion.1), channel_id=1, source_target_pairs={{0,1},{1,0},{2,3},{3,2},{4,5},{5,4},{6,7},{7,6},{8,9},{9,8},{10,11... | collective-permute-start | bytes 3145736 | tf_op jit(solution)/shard_map/ppermute | solution.py:429
  157.5 10.3 %all-to-all-start.4 = ((bf16[8,128,128]{2,1,0:T(8,128)(2,1)}), bf16[8,128,128]{2,1,0:T(8,128)(2,1)S(1)}, u32[]{:S(2)}, u32[]{:S(2)}) async-start(bf16[8,128,128]{2,1,0:T(8,128)(2,1)} %bitcast.141), calls=%async_computation.4 | async-start | bytes 524288 | tf_op jit(solution)/shard_map/all_to_all | solution.py:475
  178.8 2.9 %collective-permute-start.26 = (bf16[512,1024]{1,0:T(8,128)(2,1)}, bf16[512,1024]{1,0:T(8,128)(2,1)S(1)}, u32[]{:S(2)}, u32[]{:S(2)}) collective-permute-start(bf16[512,1024]{1,0:T(8,128)(2,1)} %get-tuple-element.38), channel_id=1, source_target_pairs={{0,1},{1,0},{2,3},{3,2},{4,5},{5,4},{6,7},{7,6},{8,9},{9,8},{10,11... | collective-permute-start | bytes 3145736 | tf_op jit(solution)/shard_map/ppermute | solution.py:429
  184.4 20.8 %all-to-all-start.5 = ((bf16[4,128,1024]{2,1,0:T(8,128)(2,1)}), bf16[4,128,1024]{2,1,0:T(8,128)(2,1)S(1)}, u32[]{:S(2)}, u32[]{:S(2)}) async-start(bf16[4,128,1024]{2,1,0:T(8,128)(2,1)} %bitcast.33), calls=%async_computation.6 | async-start | bytes 2097152 | tf_op jit(solution)/shard_map/all_to_all | solution.py:459
  187.9 64.2 %reduce-scatter.3.cloned.1.call-start = ((), (), s32[]{:S(2)}) async-start(), calls=%async_computation.12 | async-start | bytes 2359296 | tf_op jit(solution)/shard_map/reduce_scatter | solution.py:654
  192.8 28.6 %collective-permute-start.27 = (bf16[8,32,384]{2,1,0:T(8,128)(2,1)}, bf16[8,32,384]{2,1,0:T(8,128)(2,1)}, u32[]{:S(2)}, u32[]{:S(2)}) collective-permute-start(bf16[8,32,384]{2,1,0:T(8,128)(2,1)} %get-tuple-element.80), channel_id=1, source_target_pairs={{0,8},{1,9},{2,10},{3,11},{4,12},{5,13},{6,14},{7,15},{8,16},{9,17... | collective-permute-start | bytes 589832 | tf_op jit(solution)/shard_map/ppermute | solution.py:433
  194.3 27.6 %collective-permute-start.29 = (bf16[8,32,384]{2,1,0:T(8,128)(2,1)}, bf16[8,32,384]{2,1,0:T(8,128)(2,1)}, u32[]{:S(2)}, u32[]{:S(2)}) collective-permute-start(bf16[8,32,384]{2,1,0:T(8,128)(2,1)} %get-tuple-element.81), channel_id=1, source_target_pairs={{0,24},{1,25},{2,26},{3,27},{4,28},{5,29},{6,30},{7,31},{8,0},{9,1... | collective-permute-start | bytes 589832 | tf_op jit(solution)/shard_map/ppermute | solution.py:433
  196.6 25.3 %collective-permute-start.28 = (bf16[8,32,384]{2,1,0:T(8,128)(2,1)}, bf16[8,32,384]{2,1,0:T(8,128)(2,1)}, u32[]{:S(2)}, u32[]{:S(2)}) collective-permute-start(bf16[8,32,384]{2,1,0:T(8,128)(2,1)} %get-tuple-element.82), channel_id=1, source_target_pairs={{0,16},{1,17},{2,18},{3,19},{4,20},{5,21},{6,22},{7,23},{8,24},{9,... | collective-permute-start | bytes 589832 | tf_op jit(solution)/shard_map/ppermute | solution.py:433
  207.3 12.8 %all-to-all-start.6 = ((f32[32,1,384]{2,1,0:T(1,128)}), f32[32,1,384]{2,1,0:T(1,128)S(1)}, u32[]{:S(2)}, u32[]{:S(2)}) async-start(f32[32,1,384]{2,1,0:T(1,128)} %copy.89), calls=%async_computation.7 | async-start | bytes 98304 | tf_op jit(solution)/shard_map/all_to_all | solution.py:687
  215.5 12.2 %collective-permute-start.30 = (bf16[128,1024]{1,0:T(8,128)(2,1)}, bf16[128,1024]{1,0:T(8,128)(2,1)S(1)}, u32[]{:S(2)}, u32[]{:S(2)}) collective-permute-start(bf16[128,1024]{1,0:T(8,128)(2,1)} %get-tuple-element.75), channel_id=1, source_target_pairs={{0,6},{1,7},{2,4},{3,5},{4,2},{5,3},{6,0},{7,1},{8,14},{9,15},{10,... | collective-permute-start | bytes 786440 | tf_op jit(solution)/shard_map/ppermute | solution.py:429
  218.2 17.2 %collective-permute-start.32 = (bf16[128,1024]{1,0:T(8,128)(2,1)}, bf16[128,1024]{1,0:T(8,128)(2,1)}, u32[]{:S(2)}, u32[]{:S(2)}) collective-permute-start(bf16[128,1024]{1,0:T(8,128)(2,1)} %get-tuple-element.76), channel_id=1, source_target_pairs={{0,4},{1,5},{2,6},{3,7},{4,0},{5,1},{6,2},{7,3},{8,12},{9,13},{10,... | collective-permute-start | bytes 786440 | tf_op jit(solution)/shard_map/ppermute | solution.py:429
  221.4 15.5 %collective-permute-start.31 = (bf16[128,1024]{1,0:T(8,128)(2,1)}, bf16[128,1024]{1,0:T(8,128)(2,1)S(1)}, u32[]{:S(2)}, u32[]{:S(2)}) collective-permute-start(bf16[128,1024]{1,0:T(8,128)(2,1)} %get-tuple-element.77), channel_id=1, source_target_pairs={{0,2},{1,3},{2,0},{3,1},{4,6},{5,7},{6,4},{7,5},{8,10},{9,11},{10,... | collective-permute-start | bytes 786440 | tf_op jit(solution)/shard_map/ppermute | solution.py:429
  224.1 23.8 %all-to-all-start.7 = ((bf16[8,32,896]{2,1,0:T(8,128)(2,1)}), bf16[8,32,896]{2,1,0:T(8,128)(2,1)S(1)}, u32[]{:S(2)}, u32[]{:S(2)}) async-start(bf16[8,32,896]{2,1,0:T(8,128)(2,1)} %pad_maximum_fusion.2), calls=%async_computation.9 | async-start | bytes 917504 | tf_op jit(solution)/shard_map/all_to_all | solution.py:475
  238.0 6.2 %collective-permute-start.33 = (bf16[32,1024]{1,0:T(8,128)(2,1)S(1)}, bf16[32,1024]{1,0:T(8,128)(2,1)S(1)}, u32[]{:S(2)}, u32[]{:S(2)}) collective-permute-start(bf16[32,1024]{1,0:T(8,128)(2,1)S(1)} %get-tuple-element.85), channel_id=1, source_target_pairs={{0,8},{1,9},{2,10},{3,11},{4,12},{5,13},{6,14},{7,15},{8,16},{9,17... | collective-permute-start | bytes 196616 | tf_op jit(solution)/shard_map/ppermute | solution.py:433
  239.5 5.4 %collective-permute-start.35 = (bf16[32,1024]{1,0:T(8,128)(2,1)S(1)}, bf16[32,1024]{1,0:T(8,128)(2,1)S(1)}, u32[]{:S(2)}, u32[]{:S(2)}) collective-permute-start(bf16[32,1024]{1,0:T(8,128)(2,1)S(1)} %get-tuple-element.86), channel_id=1, source_target_pairs={{0,24},{1,25},{2,26},{3,27},{4,28},{5,29},{6,30},{7,31},{8,0},{9,1... | collective-permute-start | bytes 196616 | tf_op jit(solution)/shard_map/ppermute | solution.py:433
  241.9 5.2 %collective-permute-start.34 = (bf16[32,1024]{1,0:T(8,128)(2,1)S(1)}, bf16[32,1024]{1,0:T(8,128)(2,1)S(1)}, u32[]{:S(2)}, u32[]{:S(2)}) collective-permute-start(bf16[32,1024]{1,0:T(8,128)(2,1)S(1)} %get-tuple-element.87), channel_id=1, source_target_pairs={{0,16},{1,17},{2,18},{3,19},{4,20},{5,21},{6,22},{7,23},{8,24},{9,... | collective-permute-start | bytes 196616 | tf_op jit(solution)/shard_map/ppermute | solution.py:433
  (45 other events, 485.6 us)
Sparse Core Ops, SparseCore 0:
  11.0 77.1 all-gather.2
  89.8 26.2 all-gather.4
  142.1 43.7 reduce-scatter.4
  202.4 49.6 reduce-scatter.2

commit v4 on v3

--- a/solution.py
+++ b/solution.py
@@ -645,12 +645,12 @@
     grad_packed, near, far, norm_sums, packed_sums = attention_back(
         packed, grad_mixed, allowed, qkv_full, normed_low, places, out_half
     )
-    proj_rows = left_dot(hidden_one, grad_packed).astype(LOW)
+    grad_hidden_half = links.core_sum(near, far)
+    feed_parts = branch_terms(activated_low, down_full, places, grad_hidden_half)
+    proj_rows = (left_dot(hidden_one, grad_packed) + order_zero(feed_parts)).astype(LOW)
     proj_rows = proj_rows.reshape(planes, GROUP, own_rows, heads_width)
     proj_sum = links.plane_sum(proj_rows)
-    grad_hidden_half = links.core_sum(near, far)
     grad_hidden_one = links.chip_exchange(grad_hidden_half)
-    feed_parts = branch_terms(activated_low, down_full, places, grad_hidden_half)
     feed = lax.psum_scatter(
         feed_parts, "dp", axis_index_groups=links.core_lists(), scatter_dimension=0, tiled=True
     )
@@ -683,7 +683,7 @@
     ]
     vectors = jnp.concatenate([v.reshape(planes, GROUP, -1) for v in vectors], axis=2)
     grad_out_w = links.plane_sum(out_sum.reshape(planes, own_rows, width))
-    vectors = vectors.reshape(count, -1) + order_zero(grad_hidden_one)
+    vectors = vectors.reshape(count, -1) + order_zero(out_chips)
     sums = jnp.sum(lax.all_to_all(vectors, "dp", 0, 0, tiled=True), axis=0)
     proj_rows = (proj_sum + order_zero(sums)).astype(LOW)
     row_blocks = links.exchange(jnp.concatenate([proj_rows, up_rows], axis=2))

time: 262 us -> 261 us (level)
  waiting for transfers between devices: 76.3 us -> 72.8 us
    ppermute x27, waiting for transfers between devices: 39.3 us -> 35 us  [swap(): return lax.ppermute(array, 'dp', [(i, i ^ flip) for i in range(self.count)])]
    slice x6 -> x8, local copies, waits for them, and re-layouts: 3.86 us -> 5.62 us  [order_zero(): return array[(0,) * array.ndim].astype(WIDE) * 0.0]
    unnamed x95 -> x91, local copies, waits for them, and re-layouts: 6.91 us -> 6.03 us
  transfers between devices with their start and end apart: 48 -> 48, of which waited for: 18 -> 16; matrix products, arithmetic and copies ran while one was open for 22% -> 23% of each run, Pallas kernels for 10% -> 10%
where the time goes in v4:
time: 261 us; the launch traced here: 260 us
  waiting for transfers between devices  72.8 us (28%)
  starting transfers between devices  63.1 us (24%)
  Pallas kernels  37.4 us (14%)
  local copies, waits for them, and re-layouts  29 us (11%)
  other arithmetic  24.7 us (9%)
  between operations  20 us (8%)
  matrix products  12.7 us (5%)
    ppermute x27, waiting for transfers between devices, swap(): return lax.ppermute(array, 'dp', [(i, i ^ flip) for i in range(self.count)])  35 us
    ppermute x27, starting transfers between devices, swap(): return lax.ppermute(array, 'dp', [(i, i ^ flip) for i in range(self.count)])  17.3 us
    all_to_all x4, starting transfers between devices, exchange(): lax.all_to_all(parts, 'dp', 0, 0, axis_index_groups=self.group_lists(), t...  15.5 us
    ppermute x9, starting transfers between devices, shift(): lax.ppermute(array, 'dp', [(i, (i + hop) % self.count) for i in range(sel...  13.7 us
    ppermute x9, waiting for transfers between devices, shift(): lax.ppermute(array, 'dp', [(i, (i + hop) % self.count) for i in range(sel...  13.2 us
    dot_general x7, matrix products, dot(): lax.dot_general(first, second, (dims, ((), ())), preferred_element_type=j...  12.7 us
    pallas_call x1, Pallas kernels, feed_forward(): pl.pallas_call(feed_kernel, grid_spec=pltpu.PrefetchScalarGridSpec(num_sc...  11.6 us
    all_to_all x4, waiting for transfers between devices, exchange(): lax.all_to_all(parts, 'dp', 0, 0, axis_index_groups=self.group_lists(), t...  10.6 us
  transfers between devices with their start and end apart: 48, of which 16 were waited for; matrix products, arithmetic and copies ran while one was open for 23% of the time, Pallas kernels for 10%

profile of v4, /device:TPU:0, one launch (start us, length us, event | category | flops | bytes accessed | tf_op | source)
XLA Modules:
  0.0 259.5 jit_solution(6735591481025410365)
XLA Ops:
  9.9 5.2 %all-to-all-start = ((bf16[8,32,512]{2,1,0:T(8,128)(2,1)}), bf16[8,32,512]{2,1,0:T(8,128)(2,1)S(1)}, u32[]{:S(2)}, u32[]{:S(2)}) async-start(bf16[8,32,512]{2,1,0:T(8,128)(2,1)} %reshape.444), calls=%async_computation | async-start | bytes 524288 | tf_op jit(solution)/shard_map/all_to_all | solution.py:475
  15.4 6.6 %all-to-all-done.refs_16_ = bf16[8,32,512]{2,1,0:T(8,128)(2,1)S(1)} async-done(((bf16[8,32,512]{2,1,0:T(8,128)(2,1)}), bf16[8,32,512]{2,1,0:T(8,128)(2,1)S(1)}, u32[]{:S(2)}, u32[]{:S(2)}) %all-to-all-start) | async-done | bytes 262176 | tf_op jit(solution)/shard_map/all_to_all | solution.py:475
  24.3 4.0 %all-to-all-start.1 = ((bf16[32,104,128]{2,1,0:T(8,128)(2,1)}), bf16[32,104,128]{2,1,0:T(8,128)(2,1)S(1)}, u32[]{:S(2)}, u32[]{:S(2)}) async-start(bf16[32,104,128]{2,1,0:T(8,128)(2,1)} %bitcast.10), calls=%async_computation.1 | async-start | bytes 1703936 | tf_op jit(solution)/shard_map/all_to_all | solution.py:561
  28.3 2.7 %collective-permute-start.2 = (bf16[128,1024]{1,0:T(8,128)(2,1)S(1)}, bf16[128,1024]{1,0:T(8,128)(2,1)S(1)}, u32[]{:S(2)}, u32[]{:S(2)}) collective-permute-start(bf16[128,1024]{1,0:T(8,128)(2,1)S(1)} %copy-done), channel_id=1, source_target_pairs={{0,6},{1,7},{2,4},{3,5},{4,2},{5,3},{6,0},{7,1},{8,14},{9,15},{10,... | collective-permute-start | bytes 786440 | tf_op jit(solution)/shard_map/ppermute | solution.py:429
  32.0 2.7 %collective-permute-start.19 = (bf16[128,1024]{1,0:T(8,128)(2,1)S(1)}, bf16[128,1024]{1,0:T(8,128)(2,1)S(1)}, u32[]{:S(2)}, u32[]{:S(2)}) collective-permute-start(bf16[128,1024]{1,0:T(8,128)(2,1)S(1)} %get-tuple-element.64.refs_8_), channel_id=1, source_target_pairs={{0,6},{1,7},{2,4},{3,5},{4,2},{5,3},{6,0},{7,1},{8,14},{9,15},{10,... | collective-permute-start | bytes 786440 | tf_op jit(solution)/shard_map/ppermute | solution.py:429
  35.4 12.5 %collective-permute-done.2.refs_3_ = bf16[128,1024]{1,0:T(8,128)(2,1)S(1)} collective-permute-done((bf16[128,1024]{1,0:T(8,128)(2,1)S(1)}, bf16[128,1024]{1,0:T(8,128)(2,1)S(1)}, u32[]{:S(2)}, u32[]{:S(2)}) %collective-permute-start.2) | collective-permute-done | bytes 262176 | tf_op jit(solution)/shard_map/ppermute | solution.py:429
  47.9 4.8 %collective-permute-done.1.refs_2_ = bf16[128,1024]{1,0:T(8,128)(2,1)S(1)} collective-permute-done((bf16[128,1024]{1,0:T(8,128)(2,1)S(1)}, bf16[128,1024]{1,0:T(8,128)(2,1)S(1)}, u32[]{:S(2)}, u32[]{:S(2)}) %collective-permute-start.1) | collective-permute-done | bytes 262176 | tf_op jit(solution)/shard_map/ppermute | solution.py:429
  55.6 1.6 collective-permute-start.18
  57.2 3.7 %collective-permute-start.9 = (bf16[8,32,512]{2,1,0:T(8,128)(2,1)S(1)}, bf16[8,32,512]{2,1,0:T(8,128)(2,1)S(1)}, u32[]{:S(2)}, u32[]{:S(2)}) collective-permute-start(bf16[8,32,512]{2,1,0:T(8,128)(2,1)S(1)} %all-to-all-done.refs_16_), channel_id=1, source_target_pairs={{0,24},{1,25},{2,26},{3,27},{4,28},{5,29},{6,30},{7,31},{8,0},{9,1... | collective-permute-start | bytes 786440 | tf_op jit(solution)/shard_map/ppermute | solution.py:433
  60.9 1.6 collective-permute-start.7
  64.4 9.9 %shard_map.263 = (bf16[1024,1024]{1,0:T(8,128)(2,1)}, bf16[1024,1024]{1,0:T(8,128)(2,1)}, bf16[1024,384]{1,0:T(8,128)(2,1)}, bf16[1024,384]{1,0:T(8,128)(2,1)}, bf16[4,2,128,128]{3,2,1,0:T(8,128)(2,1)}) custom-call(s32[2]{0:T(128)} %pad_add_fusion.place_ref, bf16[128,1024]{1,0:T(8,128)(2,1)} %refs_0_.1, bf16[128,1024]{1,0:T(8,128)(2,1)} %copy-done.20, ...), custom_call_target="tpu_custom_call" | custom-call | flops 134217728 | bytes 1048576 | tf_op jit(solution)/shard_map/pallas_call | solution.py:212
  74.4 1.8 copy.77
  76.2 3.4 %all-to-all-start.2 = ((bf16[8,128,128]{1,2,0:T(8,128)(2,1)}), bf16[8,128,128]{1,2,0:T(8,128)(2,1)S(1)}, u32[]{:S(2)}, u32[]{:S(2)}) async-start(bf16[8,128,128]{1,2,0:T(8,128)(2,1)} %copy.77), calls=%async_computation.2 | async-start | bytes 524288 | tf_op jit(solution)/shard_map/all_to_all | solution.py:475
  80.3 9.5 %collective-permute-done.8.refs_18_ = bf16[8,32,512]{2,1,0:T(8,128)(2,1)S(1)} collective-permute-done((bf16[8,32,512]{2,1,0:T(8,128)(2,1)S(1)}, bf16[8,32,512]{2,1,0:T(8,128)(2,1)S(1)}, u32[]{:S(2)}, u32[]{:S(2)}) %collective-permute-start.8) | collective-permute-done | bytes 262176 | tf_op jit(solution)/shard_map/ppermute | solution.py:433
  95.3 2.2 fusion.40
  97.9 1.4 collective-permute-start.12
  99.4 1.7 collective-permute-start.11
  102.0 6.2 %collective-permute-done.12.refs_3_ = bf16[128,1024]{1,0:T(8,128)(2,1)} collective-permute-done((bf16[128,1024]{1,0:T(8,128)(2,1)S(1)}, bf16[128,1024]{1,0:T(8,128)(2,1)}, u32[]{:S(2)}, u32[]{:S(2)}) %collective-permute-start.12) | collective-permute-done | bytes 262176 | tf_op jit(solution)/shard_map/ppermute | solution.py:429
  108.2 4.8 %collective-permute-done.11.refs_2_ = bf16[128,1024]{1,0:T(8,128)(2,1)} collective-permute-done((bf16[128,1024]{1,0:T(8,128)(2,1)S(1)}, bf16[128,1024]{1,0:T(8,128)(2,1)}, u32[]{:S(2)}, u32[]{:S(2)}) %collective-permute-start.11) | collective-permute-done | bytes 262176 | tf_op jit(solution)/shard_map/ppermute | solution.py:429
  114.1 2.0 all-gather.5.cloned.1.call-done.refs_20_.down_ref
  116.8 11.6 %shard_map.264 = (bf16[1024,1024]{1,0:T(8,128)(2,1)}, bf16[1024,1024]{1,0:T(8,128)(2,1)}, bf16[1024,512]{1,0:T(8,128)(2,1)}, bf16[1024,512]{1,0:T(8,128)(2,1)}, ...) custom-call(s32[2]{0:T(128)} %pad_add_fusion.place_ref, bf16[128,1024]{1,0:T(8,128)(2,1)} %copy-done.10, ...), custom_call_target="tpu_custom_call" | custom-call | flops 536870912 | bytes 1048576 | tf_op jit(solution)/shard_map/pallas_call | solution.py:349
  128.6 2.3 convolution_convert_fusion.2
  131.6 2.6 %add_convert_fusion.2 = bf16[512,1024]{1,0:T(8,128)(2,1)} fusion(bf16[512,1024]{1,0:T(8,128)(2,1)} %collective-permute-done.24, bf16[512,1024]{1,0:T(8,128)(2,1)S(1)} %copy-done.6), kind=kLoop, calls=%fused_computation.6 | loop fusion | flops 2097152 | bytes 3145728 | tf_op jit(solution)/shard_map/convert_element_type | solution.py:443
  134.2 3.6 %all-to-all-start.3 = ((bf16[4,128,1024]{2,1,0:T(8,128)(2,1)}), bf16[4,128,1024]{2,1,0:T(8,128)(2,1)S(1)}, u32[]{:S(2)}, u32[]{:S(2)}) async-start(bf16[4,128,1024]{2,1,0:T(8,128)(2,1)} %bitcast.21), calls=%async_computation.3 | async-start | bytes 2097152 | tf_op jit(solution)/shard_map/all_to_all | solution.py:459
  137.9 2.4 convolution_convert_fusion.3
  141.7 1.5 pad_maximum_fusion
  143.2 8.6 %all-to-all-done.3 = bf16[4,128,1024]{2,1,0:T(8,128)(2,1)S(1)} async-done(((bf16[4,128,1024]{2,1,0:T(8,128)(2,1)}), bf16[4,128,1024]{2,1,0:T(8,128)(2,1)S(1)}, u32[]{:S(2)}, u32[]{:S(2)}) %all-to-all-start.3) | async-done | bytes 1048608 | tf_op jit(solution)/shard_map/all_to_all | solution.py:459
  158.2 3.4 %all-to-all-start.4 = ((bf16[8,128,128]{2,1,0:T(8,128)(2,1)}), bf16[8,128,128]{2,1,0:T(8,128)(2,1)S(1)}, u32[]{:S(2)}, u32[]{:S(2)}) async-start(bf16[8,128,128]{2,1,0:T(8,128)(2,1)} %bitcast.143), calls=%async_computation.4 | async-start | bytes 524288 | tf_op jit(solution)/shard_map/all_to_all | solution.py:475
  161.6 2.9 %add_convert_fusion.1.earlier_ref = bf16[4,128,1024]{2,1,0:T(8,128)(2,1)} fusion(bf16[4,128,1024]{2,1,0:T(8,128)(2,1)} %collective-permute-done.25, bf16[1,128,1024]{2,1,0:T(8,128)(2,1)} %bitcast.148, bf16[1,128,1024]{2,1,0:T(8,128)(2,1)} %bitcast.150, bf16[1,128,1024]{2,1,0:T(8,128)(2,1)} %bitcast.152, bf16[1,128,1024]{2,1,0:T(8,128)(2,1)} %bitcast.146), kind=kLoop, calls=%fused_computation.5 | loop fusion | flops 3670016 | bytes 3145728 | tf_op jit(solution)/shard_map/convert_element_type | solution.py:443
  164.5 4.0 %all-to-all-done.4 = bf16[8,128,128]{2,1,0:T(8,128)(2,1)S(1)} async-done(((bf16[8,128,128]{2,1,0:T(8,128)(2,1)}), bf16[8,128,128]{2,1,0:T(8,128)(2,1)S(1)}, u32[]{:S(2)}, u32[]{:S(2)}) %all-to-all-start.4) | async-done | bytes 262176 | tf_op jit(solution)/shard_map/all_to_all | solution.py:475
  169.2 10.3 %shard_map.265 = (bf16[1024,384]{1,0:T(8,128)(2,1)}, bf16[512,1024]{1,0:T(8,128)(2,1)}, bf16[512,1024]{1,0:T(8,128)(2,1)}, f32[2,1024]{1,0:T(2,128)}, f32[1,384]{1,0:T(1,128)}) custom-call(s32[2]{0:T(128)} %pad_add_fusion.place_ref, bf16[4,128,1024]{2,1,0:T(8,128)(2,1)} %add_convert_fusion.1.earlier_ref, bf16[1024,384]{1,0:T(8,128)(2,1)} %get-tuple-element.34.packed_ref, ...), custom_call_target="tpu_custom_call" | custom-call | flops 335544320 | bytes 2097152 | tf_op jit(solution)/shard_map/pallas_call | solution.py:257
  182.4 2.6 %add_convert_fusion.earlier_ref = bf16[512,1024]{1,0:T(8,128)(2,1)} fusion(bf16[512,1024]{1,0:T(8,128)(2,1)S(1)} %collective-permute-done.26, bf16[512,1024]{1,0:T(8,128)(2,1)} %get-tuple-element.37), kind=kLoop, calls=%fused_computation.4 | loop fusion | flops 2097152 | bytes 3145728 | tf_op jit(solution)/shard_map/convert_element_type | solution.py:443
  185.0 3.5 %all-to-all-start.5 = ((bf16[4,128,1024]{2,1,0:T(8,128)(2,1)}), bf16[4,128,1024]{2,1,0:T(8,128)(2,1)S(1)}, u32[]{:S(2)}, u32[]{:S(2)}) async-start(bf16[4,128,1024]{2,1,0:T(8,128)(2,1)} %bitcast.33), calls=%async_computation.6 | async-start | bytes 2097152 | tf_op jit(solution)/shard_map/all_to_all | solution.py:459
  188.9 5.5 %shard_map.266 = bf16[1024,1024]{1,0:T(8,128)(2,1)} custom-call(s32[2]{0:T(128)} %pad_add_fusion.place_ref, bf16[512,1024]{1,0:T(8,128)(2,1)} %add_convert_fusion.earlier_ref, bf16[1024,512]{1,0:T(8,128)(2,1)} %get-tuple-element.39.act_ref, bf16[512,1024]{1,0:T(8,128)(2,1)} %all-gather.5.cloned.1.call-done.refs_20_.down_ref), custom_call_target="tpu_custom_call" | custom-call | tf_op jit(solution)/shard_map/pallas_call | solution.py:400
  196.3 2.9 %add_convert_fusion.3 = bf16[1024,384]{1,0:T(8,128)(2,1)S(1)} fusion(bf16[1024,1024]{1,0:T(8,128)(2,1)} %get-tuple-element.43, bf16[1024,384]{1,0:T(8,128)(2,1)S(1)} %copy-done.42, f32[]{:T(128)} %bitcast.39), kind=kOutput, calls=%fused_computation.8 | convolution fusion | flops 806092800 | bytes 3670020 | tf_op jit(solution)/shard_map/dot_general | solution.py:47
  200.2 1.5 collective-permute-start.27
  201.6 2.4 collective-permute-start.29
  204.1 1.9 fusion.36
  208.5 1.7 broadcast_add_fusion
  212.1 5.4 %all-to-all-start.6 = ((f32[32,1,384]{2,1,0:T(1,128)}), f32[32,1,384]{2,1,0:T(1,128)S(1)}, u32[]{:S(2)}, u32[]{:S(2)}) async-start(f32[32,1,384]{2,1,0:T(1,128)} %copy.89), calls=%async_computation.7 | async-start | bytes 98304 | tf_op jit(solution)/shard_map/all_to_all | solution.py:687
  218.4 2.7 %collective-permute-start.30 = (bf16[128,1024]{1,0:T(8,128)(2,1)}, bf16[128,1024]{1,0:T(8,128)(2,1)S(1)}, u32[]{:S(2)}, u32[]{:S(2)}) collective-permute-start(bf16[128,1024]{1,0:T(8,128)(2,1)} %get-tuple-element.75), channel_id=1, source_target_pairs={{0,6},{1,7},{2,4},{3,5},{4,2},{5,3},{6,0},{7,1},{8,14},{9,15},{10,... | collective-permute-start | bytes 786440 | tf_op jit(solution)/shard_map/ppermute | solution.py:429
  222.9 1.9 all-to-all-done.6
  228.8 3.5 %all-to-all-start.7 = ((bf16[8,32,896]{2,1,0:T(8,128)(2,1)}), bf16[8,32,896]{2,1,0:T(8,128)(2,1)S(1)}, u32[]{:S(2)}, u32[]{:S(2)}) async-start(bf16[8,32,896]{2,1,0:T(8,128)(2,1)} %pad_maximum_fusion.2), calls=%async_computation.9 | async-start | bytes 917504 | tf_op jit(solution)/shard_map/all_to_all | solution.py:475
  232.3 4.3 %collective-permute-done.32 = bf16[128,1024]{1,0:T(8,128)(2,1)} collective-permute-done((bf16[128,1024]{1,0:T(8,128)(2,1)}, bf16[128,1024]{1,0:T(8,128)(2,1)}, u32[]{:S(2)}, u32[]{:S(2)}) %collective-permute-start.32) | collective-permute-done | bytes 262176 | tf_op jit(solution)/shard_map/ppermute | solution.py:429
  237.7 1.5 collective-permute-start.33
  239.3 2.3 collective-permute-start.35
  244.5 3.1 %collective-permute-done.34 = bf16[32,1024]{1,0:T(8,128)(2,1)S(1)} collective-permute-done((bf16[32,1024]{1,0:T(8,128)(2,1)S(1)}, bf16[32,1024]{1,0:T(8,128)(2,1)S(1)}, u32[]{:S(2)}, u32[]{:S(2)}) %collective-permute-start.34) | collective-permute-done | bytes 65568 | tf_op jit(solution)/shard_map/ppermute | solution.py:433
  251.2 1.7 add_convert_fusion.4
  (260 shorter events, 49.4 us)
Async XLA Ops:
  7.3 87.9 %all-gather.3.cloned.1.call-start = ((), (), s32[]{:S(2)}) async-start(), calls=%async_computation.10 | async-start | bytes 2162688 | tf_op jit(solution)/shard_map/all_gather | solution.py:562
  9.9 12.1 %all-to-all-start = ((bf16[8,32,512]{2,1,0:T(8,128)(2,1)}), bf16[8,32,512]{2,1,0:T(8,128)(2,1)S(1)}, u32[]{:S(2)}, u32[]{:S(2)}) async-start(bf16[8,32,512]{2,1,0:T(8,128)(2,1)} %reshape.444), calls=%async_computation | async-start | bytes 524288 | tf_op jit(solution)/shard_map/all_to_all | solution.py:475
  24.3 29.5 %all-to-all-start.1 = ((bf16[32,104,128]{2,1,0:T(8,128)(2,1)}), bf16[32,104,128]{2,1,0:T(8,128)(2,1)S(1)}, u32[]{:S(2)}, u32[]{:S(2)}) async-start(bf16[32,104,128]{2,1,0:T(8,128)(2,1)} %bitcast.10), calls=%async_computation.1 | async-start | bytes 1703936 | tf_op jit(solution)/shard_map/all_to_all | solution.py:561
  28.3 19.6 %collective-permute-start.2 = (bf16[128,1024]{1,0:T(8,128)(2,1)S(1)}, bf16[128,1024]{1,0:T(8,128)(2,1)S(1)}, u32[]{:S(2)}, u32[]{:S(2)}) collective-permute-start(bf16[128,1024]{1,0:T(8,128)(2,1)S(1)} %copy-done), channel_id=1, source_target_pairs={{0,6},{1,7},{2,4},{3,5},{4,2},{5,3},{6,0},{7,1},{8,14},{9,15},{10,... | collective-permute-start | bytes 786440 | tf_op jit(solution)/shard_map/ppermute | solution.py:429
  31.1 21.6 %collective-permute-start.1 = (bf16[128,1024]{1,0:T(8,128)(2,1)S(1)}, bf16[128,1024]{1,0:T(8,128)(2,1)S(1)}, u32[]{:S(2)}, u32[]{:S(2)}) collective-permute-start(bf16[128,1024]{1,0:T(8,128)(2,1)S(1)} %copy-done), channel_id=1, source_target_pairs={{0,4},{1,5},{2,6},{3,7},{4,0},{5,1},{6,2},{7,3},{8,12},{9,13},{10,... | collective-permute-start | bytes 786440 | tf_op jit(solution)/shard_map/ppermute | solution.py:429
  31.6 22.3 %collective-permute-start = (bf16[128,1024]{1,0:T(8,128)(2,1)S(1)}, bf16[128,1024]{1,0:T(8,128)(2,1)S(1)}, u32[]{:S(2)}, u32[]{:S(2)}) collective-permute-start(bf16[128,1024]{1,0:T(8,128)(2,1)S(1)} %copy-done), channel_id=1, source_target_pairs={{0,2},{1,3},{2,0},{3,1},{4,6},{5,7},{6,4},{7,5},{8,10},{9,11},{10,... | collective-permute-start | bytes 786440 | tf_op jit(solution)/shard_map/ppermute | solution.py:429
  31.9 23.7 %collective-permute-start.3 = (bf16[128,1024]{1,0:T(8,128)(2,1)S(1)}, bf16[128,1024]{1,0:T(8,128)(2,1)}, u32[]{:S(2)}, u32[]{:S(2)}) collective-permute-start(bf16[128,1024]{1,0:T(8,128)(2,1)S(1)} %copy-done), channel_id=1, source_target_pairs={{0,1},{1,0},{2,3},{3,2},{4,5},{5,4},{6,7},{7,6},{8,9},{9,8},{10,11... | collective-permute-start | bytes 786440 | tf_op jit(solution)/shard_map/ppermute | solution.py:429
  32.0 58.4 %collective-permute-start.19 = (bf16[128,1024]{1,0:T(8,128)(2,1)S(1)}, bf16[128,1024]{1,0:T(8,128)(2,1)S(1)}, u32[]{:S(2)}, u32[]{:S(2)}) collective-permute-start(bf16[128,1024]{1,0:T(8,128)(2,1)S(1)} %get-tuple-element.64.refs_8_), channel_id=1, source_target_pairs={{0,6},{1,7},{2,4},{3,5},{4,2},{5,3},{6,0},{7,1},{8,14},{9,15},{10,... | collective-permute-start | bytes 786440 | tf_op jit(solution)/shard_map/ppermute | solution.py:429
  47.9 9.3 %collective-permute-start.6 = (bf16[128,1024]{1,0:T(8,128)(2,1)S(1)}, bf16[128,1024]{1,0:T(8,128)(2,1)}, u32[]{:S(2)}, u32[]{:S(2)}) collective-permute-start(bf16[128,1024]{1,0:T(8,128)(2,1)S(1)} %collective-permute-done.2.refs_3_), channel_id=1, source_target_pairs={{0,1},{1,0},{2,3},{3,2},{4,5},{5,4},{6,7},{7,6},{8,9},{9,8},{10,11... | collective-permute-start | bytes 786440 | tf_op jit(solution)/shard_map/ppermute | solution.py:429
  52.7 8.2 %collective-permute-start.5 = (bf16[128,1024]{1,0:T(8,128)(2,1)S(1)}, bf16[128,1024]{1,0:T(8,128)(2,1)}, u32[]{:S(2)}, u32[]{:S(2)}) collective-permute-start(bf16[128,1024]{1,0:T(8,128)(2,1)S(1)} %collective-permute-done.1.refs_2_), channel_id=1, source_target_pairs={{0,1},{1,0},{2,3},{3,2},{4,5},{5,4},{6,7},{7,6},{8,9},{9,8},{10,11... | collective-permute-start | bytes 786440 | tf_op jit(solution)/shard_map/ppermute | solution.py:429
  53.9 7.0 %collective-permute-start.4 = (bf16[128,1024]{1,0:T(8,128)(2,1)S(1)}, bf16[128,1024]{1,0:T(8,128)(2,1)}, u32[]{:S(2)}, u32[]{:S(2)}) collective-permute-start(bf16[128,1024]{1,0:T(8,128)(2,1)S(1)} %collective-permute-done.refs_1_), channel_id=1, source_target_pairs={{0,1},{1,0},{2,3},{3,2},{4,5},{5,4},{6,7},{7,6},{8,9},{9,8},{10,11... | collective-permute-start | bytes 786440 | tf_op jit(solution)/shard_map/ppermute | solution.py:429
  55.6 35.2 %collective-permute-start.18 = (bf16[128,1024]{1,0:T(8,128)(2,1)S(1)}, bf16[128,1024]{1,0:T(8,128)(2,1)S(1)}, u32[]{:S(2)}, u32[]{:S(2)}) collective-permute-start(bf16[128,1024]{1,0:T(8,128)(2,1)S(1)} %get-tuple-element.64.refs_8_), channel_id=1, source_target_pairs={{0,4},{1,5},{2,6},{3,7},{4,0},{5,1},{6,2},{7,3},{8,12},{9,13},{10,... | collective-permute-start | bytes 786440 | tf_op jit(solution)/shard_map/ppermute | solution.py:429
  57.2 36.6 %collective-permute-start.9 = (bf16[8,32,512]{2,1,0:T(8,128)(2,1)S(1)}, bf16[8,32,512]{2,1,0:T(8,128)(2,1)S(1)}, u32[]{:S(2)}, u32[]{:S(2)}) collective-permute-start(bf16[8,32,512]{2,1,0:T(8,128)(2,1)S(1)} %all-to-all-done.refs_16_), channel_id=1, source_target_pairs={{0,24},{1,25},{2,26},{3,27},{4,28},{5,29},{6,30},{7,31},{8,0},{9,1... | collective-permute-start | bytes 786440 | tf_op jit(solution)/shard_map/ppermute | solution.py:433
  60.9 29.0 %collective-permute-start.8 = (bf16[8,32,512]{2,1,0:T(8,128)(2,1)S(1)}, bf16[8,32,512]{2,1,0:T(8,128)(2,1)S(1)}, u32[]{:S(2)}, u32[]{:S(2)}) collective-permute-start(bf16[8,32,512]{2,1,0:T(8,128)(2,1)S(1)} %all-to-all-done.refs_16_), channel_id=1, source_target_pairs={{0,16},{1,17},{2,18},{3,19},{4,20},{5,21},{6,22},{7,23},{8,24},{9,... | collective-permute-start | bytes 786440 | tf_op jit(solution)/shard_map/ppermute | solution.py:433
  60.9 30.1 %collective-permute-start.7 = (bf16[8,32,512]{2,1,0:T(8,128)(2,1)S(1)}, bf16[8,32,512]{2,1,0:T(8,128)(2,1)}, u32[]{:S(2)}, u32[]{:S(2)}) collective-permute-start(bf16[8,32,512]{2,1,0:T(8,128)(2,1)S(1)} %all-to-all-done.refs_16_), channel_id=1, source_target_pairs={{0,8},{1,9},{2,10},{3,11},{4,12},{5,13},{6,14},{7,15},{8,16},{9,17... | collective-permute-start | bytes 786440 | tf_op jit(solution)/shard_map/ppermute | solution.py:433
  76.2 19.1 %all-to-all-start.2 = ((bf16[8,128,128]{1,2,0:T(8,128)(2,1)}), bf16[8,128,128]{1,2,0:T(8,128)(2,1)S(1)}, u32[]{:S(2)}, u32[]{:S(2)}) async-start(bf16[8,128,128]{1,2,0:T(8,128)(2,1)} %copy.77), calls=%async_computation.2 | async-start | bytes 524288 | tf_op jit(solution)/shard_map/all_to_all | solution.py:475
  79.6 36.5 %all-gather.5.cloned.1.call-start = ((), (), s32[]{:S(2)}) async-start(), calls=%async_computation.11 | async-start | bytes 1310720 | tf_op jit(solution)/shard_map/all_gather | solution.py:563
  89.8 9.5 %collective-permute-start.20 = (bf16[128,1024]{1,0:T(8,128)(2,1)S(1)}, bf16[128,1024]{1,0:T(8,128)(2,1)S(1)}, u32[]{:S(2)}, u32[]{:S(2)}) collective-permute-start(bf16[128,1024]{1,0:T(8,128)(2,1)S(1)} %get-tuple-element.64.refs_8_), channel_id=1, source_target_pairs={{0,1},{1,0},{2,3},{3,2},{4,5},{5,4},{6,7},{7,6},{8,9},{9,8},{10,11... | collective-permute-start | bytes 786440 | tf_op jit(solution)/shard_map/ppermute | solution.py:429
  90.4 10.7 %collective-permute-start.17 = (bf16[128,1024]{1,0:T(8,128)(2,1)S(1)}, bf16[128,1024]{1,0:T(8,128)(2,1)S(1)}, u32[]{:S(2)}, u32[]{:S(2)}) collective-permute-start(bf16[128,1024]{1,0:T(8,128)(2,1)S(1)} %get-tuple-element.64.refs_8_), channel_id=1, source_target_pairs={{0,2},{1,3},{2,0},{3,1},{4,6},{5,7},{6,4},{7,5},{8,10},{9,11},{10,... | collective-permute-start | bytes 786440 | tf_op jit(solution)/shard_map/ppermute | solution.py:429
  90.8 10.7 %collective-permute-start.23 = (bf16[128,1024]{1,0:T(8,128)(2,1)S(1)}, bf16[128,1024]{1,0:T(8,128)(2,1)S(1)}, u32[]{:S(2)}, u32[]{:S(2)}) collective-permute-start(bf16[128,1024]{1,0:T(8,128)(2,1)S(1)} %collective-permute-done.19.refs_11_), channel_id=1, source_target_pairs={{0,1},{1,0},{2,3},{3,2},{4,5},{5,4},{6,7},{7,6},{8,9},{9,8},{10,11... | collective-permute-start | bytes 786440 | tf_op jit(solution)/shard_map/ppermute | solution.py:429
  91.0 10.5 %collective-permute-start.22 = (bf16[128,1024]{1,0:T(8,128)(2,1)S(1)}, bf16[128,1024]{1,0:T(8,128)(2,1)S(1)}, u32[]{:S(2)}, u32[]{:S(2)}) collective-permute-start(bf16[128,1024]{1,0:T(8,128)(2,1)S(1)} %collective-permute-done.18.refs_10_), channel_id=1, source_target_pairs={{0,1},{1,0},{2,3},{3,2},{4,5},{5,4},{6,7},{7,6},{8,9},{9,8},{10,11... | collective-permute-start | bytes 786440 | tf_op jit(solution)/shard_map/ppermute | solution.py:429
  97.9 10.3 %collective-permute-start.12 = (bf16[128,1024]{1,0:T(8,128)(2,1)S(1)}, bf16[128,1024]{1,0:T(8,128)(2,1)}, u32[]{:S(2)}, u32[]{:S(2)}) collective-permute-start(bf16[128,1024]{1,0:T(8,128)(2,1)S(1)} %add_convert_fusion.5.refs_0_), channel_id=1, source_target_pairs={{0,6},{1,7},{2,4},{3,5},{4,2},{5,3},{6,0},{7,1},{8,14},{9,15},{10,... | collective-permute-start | bytes 786440 | tf_op jit(solution)/shard_map/ppermute | solution.py:429
  99.4 13.6 %collective-permute-start.11 = (bf16[128,1024]{1,0:T(8,128)(2,1)S(1)}, bf16[128,1024]{1,0:T(8,128)(2,1)}, u32[]{:S(2)}, u32[]{:S(2)}) collective-permute-start(bf16[128,1024]{1,0:T(8,128)(2,1)S(1)} %add_convert_fusion.5.refs_0_), channel_id=1, source_target_pairs={{0,4},{1,5},{2,6},{3,7},{4,0},{5,1},{6,2},{7,3},{8,12},{9,13},{10,... | collective-permute-start | bytes 786440 | tf_op jit(solution)/shard_map/ppermute | solution.py:429
  101.1 11.9 %collective-permute-start.10 = (bf16[128,1024]{1,0:T(8,128)(2,1)S(1)}, bf16[128,1024]{1,0:T(8,128)(2,1)}, u32[]{:S(2)}, u32[]{:S(2)}) collective-permute-start(bf16[128,1024]{1,0:T(8,128)(2,1)S(1)} %add_convert_fusion.5.refs_0_), channel_id=1, source_target_pairs={{0,2},{1,3},{2,0},{3,1},{4,6},{5,7},{6,4},{7,5},{8,10},{9,11},{10,... | collective-permute-start | bytes 786440 | tf_op jit(solution)/shard_map/ppermute | solution.py:429
  101.5 12.6 %collective-permute-start.21 = (bf16[128,1024]{1,0:T(8,128)(2,1)S(1)}, bf16[128,1024]{1,0:T(8,128)(2,1)S(1)}, u32[]{:S(2)}, u32[]{:S(2)}) collective-permute-start(bf16[128,1024]{1,0:T(8,128)(2,1)S(1)} %collective-permute-done.17.refs_9_), channel_id=1, source_target_pairs={{0,1},{1,0},{2,3},{3,2},{4,5},{5,4},{6,7},{7,6},{8,9},{9,8},{10,11... | collective-permute-start | bytes 786440 | tf_op jit(solution)/shard_map/ppermute | solution.py:429
  101.5 14.6 %collective-permute-start.13 = (bf16[128,1024]{1,0:T(8,128)(2,1)S(1)}, bf16[128,1024]{1,0:T(8,128)(2,1)S(1)}, u32[]{:S(2)}, u32[]{:S(2)}) collective-permute-start(bf16[128,1024]{1,0:T(8,128)(2,1)S(1)} %add_convert_fusion.5.refs_0_), channel_id=1, source_target_pairs={{0,1},{1,0},{2,3},{3,2},{4,5},{5,4},{6,7},{7,6},{8,9},{9,8},{10,11... | collective-permute-start | bytes 786440 | tf_op jit(solution)/shard_map/ppermute | solution.py:429
  108.2 7.9 %collective-permute-start.16 = (bf16[128,1024]{1,0:T(8,128)(2,1)}, bf16[128,1024]{1,0:T(8,128)(2,1)}, u32[]{:S(2)}, u32[]{:S(2)}) collective-permute-start(bf16[128,1024]{1,0:T(8,128)(2,1)} %collective-permute-done.12.refs_3_), channel_id=1, source_target_pairs={{0,1},{1,0},{2,3},{3,2},{4,5},{5,4},{6,7},{7,6},{8,9},{9,8},{10,11... | collective-permute-start | bytes 786440 | tf_op jit(solution)/shard_map/ppermute | solution.py:429
  113.0 3.1 %collective-permute-start.15 = (bf16[128,1024]{1,0:T(8,128)(2,1)}, bf16[128,1024]{1,0:T(8,128)(2,1)}, u32[]{:S(2)}, u32[]{:S(2)}) collective-permute-start(bf16[128,1024]{1,0:T(8,128)(2,1)} %collective-permute-done.11.refs_2_), channel_id=1, source_target_pairs={{0,1},{1,0},{2,3},{3,2},{4,5},{5,4},{6,7},{7,6},{8,9},{9,8},{10,11... | collective-permute-start | bytes 786440 | tf_op jit(solution)/shard_map/ppermute | solution.py:429
  113.0 3.1 %collective-permute-start.14 = (bf16[128,1024]{1,0:T(8,128)(2,1)}, bf16[128,1024]{1,0:T(8,128)(2,1)}, u32[]{:S(2)}, u32[]{:S(2)}) collective-permute-start(bf16[128,1024]{1,0:T(8,128)(2,1)} %collective-permute-done.10.refs_1_), channel_id=1, source_target_pairs={{0,1},{1,0},{2,3},{3,2},{4,5},{5,4},{6,7},{7,6},{8,9},{9,8},{10,11... | collective-permute-start | bytes 786440 | tf_op jit(solution)/shard_map/ppermute | solution.py:429
  128.5 3.1 %collective-permute-start.24 = (bf16[512,1024]{1,0:T(8,128)(2,1)}, bf16[512,1024]{1,0:T(8,128)(2,1)}, u32[]{:S(2)}, u32[]{:S(2)}) collective-permute-start(bf16[512,1024]{1,0:T(8,128)(2,1)} %get-tuple-element.33), channel_id=1, source_target_pairs={{0,1},{1,0},{2,3},{3,2},{4,5},{5,4},{6,7},{7,6},{8,9},{9,8},{10,11... | collective-permute-start | bytes 3145736 | tf_op jit(solution)/shard_map/ppermute | solution.py:429
  134.2 17.7 %all-to-all-start.3 = ((bf16[4,128,1024]{2,1,0:T(8,128)(2,1)}), bf16[4,128,1024]{2,1,0:T(8,128)(2,1)S(1)}, u32[]{:S(2)}, u32[]{:S(2)}) async-start(bf16[4,128,1024]{2,1,0:T(8,128)(2,1)} %bitcast.21), calls=%async_computation.3 | async-start | bytes 2097152 | tf_op jit(solution)/shard_map/all_to_all | solution.py:459
  137.8 66.3 %reduce-scatter.5.cloned.1.call-start = ((), (), s32[]{:S(2)}) async-start(), calls=%async_computation.13 | async-start | bytes 2621440 | tf_op jit(solution)/shard_map/reduce_scatter | solution.py:638
  155.7 5.9 %collective-permute-start.25 = (bf16[4,128,1024]{2,1,0:T(8,128)(2,1)}, bf16[4,128,1024]{2,1,0:T(8,128)(2,1)}, u32[]{:S(2)}, u32[]{:S(2)}) collective-permute-start(bf16[4,128,1024]{2,1,0:T(8,128)(2,1)} %pad_maximum_fusion.1), channel_id=1, source_target_pairs={{0,1},{1,0},{2,3},{3,2},{4,5},{5,4},{6,7},{7,6},{8,9},{9,8},{10,11... | collective-permute-start | bytes 3145736 | tf_op jit(solution)/shard_map/ppermute | solution.py:429
  158.2 10.3 %all-to-all-start.4 = ((bf16[8,128,128]{2,1,0:T(8,128)(2,1)}), bf16[8,128,128]{2,1,0:T(8,128)(2,1)S(1)}, u32[]{:S(2)}, u32[]{:S(2)}) async-start(bf16[8,128,128]{2,1,0:T(8,128)(2,1)} %bitcast.143), calls=%async_computation.4 | async-start | bytes 524288 | tf_op jit(solution)/shard_map/all_to_all | solution.py:475
  179.5 2.9 %collective-permute-start.26 = (bf16[512,1024]{1,0:T(8,128)(2,1)}, bf16[512,1024]{1,0:T(8,128)(2,1)S(1)}, u32[]{:S(2)}, u32[]{:S(2)}) collective-permute-start(bf16[512,1024]{1,0:T(8,128)(2,1)} %get-tuple-element.38), channel_id=1, source_target_pairs={{0,1},{1,0},{2,3},{3,2},{4,5},{5,4},{6,7},{7,6},{8,9},{9,8},{10,11... | collective-permute-start | bytes 3145736 | tf_op jit(solution)/shard_map/ppermute | solution.py:429
  185.0 22.1 %all-to-all-start.5 = ((bf16[4,128,1024]{2,1,0:T(8,128)(2,1)}), bf16[4,128,1024]{2,1,0:T(8,128)(2,1)S(1)}, u32[]{:S(2)}, u32[]{:S(2)}) async-start(bf16[4,128,1024]{2,1,0:T(8,128)(2,1)} %bitcast.33), calls=%async_computation.6 | async-start | bytes 2097152 | tf_op jit(solution)/shard_map/all_to_all | solution.py:459
  188.6 62.7 %reduce-scatter.3.cloned.1.call-start = ((), (), s32[]{:S(2)}) async-start(), calls=%async_computation.12 | async-start | bytes 2359296 | tf_op jit(solution)/shard_map/reduce_scatter | solution.py:654
  200.2 25.9 %collective-permute-start.27 = (bf16[8,32,384]{2,1,0:T(8,128)(2,1)}, bf16[8,32,384]{2,1,0:T(8,128)(2,1)}, u32[]{:S(2)}, u32[]{:S(2)}) collective-permute-start(bf16[8,32,384]{2,1,0:T(8,128)(2,1)} %get-tuple-element.80), channel_id=1, source_target_pairs={{0,8},{1,9},{2,10},{3,11},{4,12},{5,13},{6,14},{7,15},{8,16},{9,17... | collective-permute-start | bytes 589832 | tf_op jit(solution)/shard_map/ppermute | solution.py:433
  201.6 25.0 %collective-permute-start.29 = (bf16[8,32,384]{2,1,0:T(8,128)(2,1)}, bf16[8,32,384]{2,1,0:T(8,128)(2,1)}, u32[]{:S(2)}, u32[]{:S(2)}) collective-permute-start(bf16[8,32,384]{2,1,0:T(8,128)(2,1)} %get-tuple-element.81), channel_id=1, source_target_pairs={{0,24},{1,25},{2,26},{3,27},{4,28},{5,29},{6,30},{7,31},{8,0},{9,1... | collective-permute-start | bytes 589832 | tf_op jit(solution)/shard_map/ppermute | solution.py:433
  204.0 22.6 %collective-permute-start.28 = (bf16[8,32,384]{2,1,0:T(8,128)(2,1)}, bf16[8,32,384]{2,1,0:T(8,128)(2,1)}, u32[]{:S(2)}, u32[]{:S(2)}) collective-permute-start(bf16[8,32,384]{2,1,0:T(8,128)(2,1)} %get-tuple-element.82), channel_id=1, source_target_pairs={{0,16},{1,17},{2,18},{3,19},{4,20},{5,21},{6,22},{7,23},{8,24},{9,... | collective-permute-start | bytes 589832 | tf_op jit(solution)/shard_map/ppermute | solution.py:433
  212.1 12.7 %all-to-all-start.6 = ((f32[32,1,384]{2,1,0:T(1,128)}), f32[32,1,384]{2,1,0:T(1,128)S(1)}, u32[]{:S(2)}, u32[]{:S(2)}) async-start(f32[32,1,384]{2,1,0:T(1,128)} %copy.89), calls=%async_computation.7 | async-start | bytes 98304 | tf_op jit(solution)/shard_map/all_to_all | solution.py:687
  218.4 13.9 %collective-permute-start.30 = (bf16[128,1024]{1,0:T(8,128)(2,1)}, bf16[128,1024]{1,0:T(8,128)(2,1)S(1)}, u32[]{:S(2)}, u32[]{:S(2)}) collective-permute-start(bf16[128,1024]{1,0:T(8,128)(2,1)} %get-tuple-element.75), channel_id=1, source_target_pairs={{0,6},{1,7},{2,4},{3,5},{4,2},{5,3},{6,0},{7,1},{8,14},{9,15},{10,... | collective-permute-start | bytes 786440 | tf_op jit(solution)/shard_map/ppermute | solution.py:429
  221.0 15.5 %collective-permute-start.32 = (bf16[128,1024]{1,0:T(8,128)(2,1)}, bf16[128,1024]{1,0:T(8,128)(2,1)}, u32[]{:S(2)}, u32[]{:S(2)}) collective-permute-start(bf16[128,1024]{1,0:T(8,128)(2,1)} %get-tuple-element.76), channel_id=1, source_target_pairs={{0,4},{1,5},{2,6},{3,7},{4,0},{5,1},{6,2},{7,3},{8,12},{9,13},{10,... | collective-permute-start | bytes 786440 | tf_op jit(solution)/shard_map/ppermute | solution.py:429
  226.1 10.5 %collective-permute-start.31 = (bf16[128,1024]{1,0:T(8,128)(2,1)}, bf16[128,1024]{1,0:T(8,128)(2,1)S(1)}, u32[]{:S(2)}, u32[]{:S(2)}) collective-permute-start(bf16[128,1024]{1,0:T(8,128)(2,1)} %get-tuple-element.77), channel_id=1, source_target_pairs={{0,2},{1,3},{2,0},{3,1},{4,6},{5,7},{6,4},{7,5},{8,10},{9,11},{10,... | collective-permute-start | bytes 786440 | tf_op jit(solution)/shard_map/ppermute | solution.py:429
  228.8 19.6 %all-to-all-start.7 = ((bf16[8,32,896]{2,1,0:T(8,128)(2,1)}), bf16[8,32,896]{2,1,0:T(8,128)(2,1)S(1)}, u32[]{:S(2)}, u32[]{:S(2)}) async-start(bf16[8,32,896]{2,1,0:T(8,128)(2,1)} %pad_maximum_fusion.2), calls=%async_computation.9 | async-start | bytes 917504 | tf_op jit(solution)/shard_map/all_to_all | solution.py:475
  237.7 6.8 %collective-permute-start.33 = (bf16[32,1024]{1,0:T(8,128)(2,1)S(1)}, bf16[32,1024]{1,0:T(8,128)(2,1)S(1)}, u32[]{:S(2)}, u32[]{:S(2)}) collective-permute-start(bf16[32,1024]{1,0:T(8,128)(2,1)S(1)} %get-tuple-element.85), channel_id=1, source_target_pairs={{0,8},{1,9},{2,10},{3,11},{4,12},{5,13},{6,14},{7,15},{8,16},{9,17... | collective-permute-start | bytes 196616 | tf_op jit(solution)/shard_map/ppermute | solution.py:433
  239.3 5.2 %collective-permute-start.35 = (bf16[32,1024]{1,0:T(8,128)(2,1)S(1)}, bf16[32,1024]{1,0:T(8,128)(2,1)S(1)}, u32[]{:S(2)}, u32[]{:S(2)}) collective-permute-start(bf16[32,1024]{1,0:T(8,128)(2,1)S(1)} %get-tuple-element.86), channel_id=1, source_target_pairs={{0,24},{1,25},{2,26},{3,27},{4,28},{5,29},{6,30},{7,31},{8,0},{9,1... | collective-permute-start | bytes 196616 | tf_op jit(solution)/shard_map/ppermute | solution.py:433
  241.6 6.0 %collective-permute-start.34 = (bf16[32,1024]{1,0:T(8,128)(2,1)S(1)}, bf16[32,1024]{1,0:T(8,128)(2,1)S(1)}, u32[]{:S(2)}, u32[]{:S(2)}) collective-permute-start(bf16[32,1024]{1,0:T(8,128)(2,1)S(1)} %get-tuple-element.87), channel_id=1, source_target_pairs={{0,16},{1,17},{2,18},{3,19},{4,20},{5,21},{6,22},{7,23},{8,24},{9,... | collective-permute-start | bytes 196616 | tf_op jit(solution)/shard_map/ppermute | solution.py:433
  (43 other events, 474.1 us)
Sparse Core Ops, SparseCore 0:
  11.0 77.1 all-gather.2
  89.8 26.2 all-gather.4
  143.4 43.7 reduce-scatter.4
  195.8 50.1 reduce-scatter.2
